TPU v7x, 32 devices: a whole 2x2x4 slice. The times are simulated.
32 devices in a mesh: ctx: 8 (over y, x, core), exp: 4 (over z).
Axes of the slice: x: 2, y: 2, z: 4, core: 2. Of those that a mesh axis runs over, the one named last changes fastest.
Arguments:
- block_input: bfloat16 [512, 2, 768], P('ctx'), may hold values from -6 to 6
- output_cotangent: bfloat16 [512, 2, 768], P(('ctx', 'exp')), may hold values from -6 to 6
- attn_gain: float32 [768], replicated, may hold values from 0.5 to 1.5
- query_weight: bfloat16 [768, 768], P('ctx', 'exp'), may hold values from -0.21875 to 0.21875
- key_weight: bfloat16 [768, 768], P('ctx', 'exp'), may hold values from -0.21875 to 0.21875
- value_weight: bfloat16 [768, 768], P('ctx', 'exp'), may hold values from -0.21875 to 0.21875
- output_weight: bfloat16 [768, 768], P('exp', 'ctx'), may hold values from -6 to 6
- bias_table: float32 [32, 12], replicated, may hold values from -6 to 6
- buckets: int32 [512], replicated, may hold values from 0 to 31
- ffn_gain: float32 [768], replicated, may hold values from 0.5 to 1.5
- router_weight: float32 [768, 4], replicated, may hold values from -0.15625 to 0.15625
- routes: int32 [512, 2, 2], P(('ctx', 'exp')), may hold values from 0 to 3, all different within a row; in each aligned block of 32 rows (0 to 31, 32 to 63, ..., all dimensions but the last counted through in order) at most 24 rows name the same one
- route_prior: float32 [512, 2, 2], P(('ctx', 'exp')), may hold values from 0.5 to 2
- gate_weight: bfloat16 [4, 768, 3072], P('exp', 'ctx'), may hold values from -0.21875 to 0.21875
- up_weight: bfloat16 [4, 768, 3072], P('exp', 'ctx'), may hold values from -0.21875 to 0.21875
- down_weight: bfloat16 [4, 3072, 768], P('exp', 'ctx'), may hold values from -0.109375 to 0.109375
Outputs:
- block_output: bfloat16 [512, 2, 768], P(('ctx', 'exp'))
- input_grad: float32 [512, 2, 768], P(('ctx', 'exp'))
- attn_gain_grad: float32 [768], replicated
- query_grad: float32 [768, 768], P('ctx', 'exp')
- key_grad: float32 [768, 768], P('ctx', 'exp')
- value_grad: float32 [768, 768], P('ctx', 'exp')
- output_grad: float32 [768, 768], P('exp', 'ctx')
- table_grad: float32 [32, 12], replicated
- ffn_gain_grad: float32 [768], replicated
- router_grad: float32 [768, 4], replicated
- gate_grad: float32 [4, 768, 3072], P('exp', 'ctx')
- up_grad: float32 [4, 768, 3072], P('exp', 'ctx')
- down_grad: float32 [4, 3072, 768], P('exp', 'ctx')
Inputs may be any that keep to these rules, and one draw needn't show every extreme that they name: `routes`: each token names two different experts. Taking positions in order with both sequences of a position together, every aligned block of 32 rows names no expert more than 24 times, a bound that some block reaches.
All inputs are finite; a program needn't handle non-finite values.
Results may differ from a plain program's by a relative error of at most 0.03.
Values may be sent and summed in bfloat16 or wider, within the bound.
No kernel may reach another device: no remote copies, remote signals or barrier semaphores. Data moves between devices by JAX's collectives and lax.ppermute only.
A program may use at most 320 MiB of HBM per device.

v0:
```python
import jax
import jax.numpy as jnp
from jax import lax
from jax.sharding import PartitionSpec as P

HD = 64


EPS = 1e-06
FLOOR = -1e30
HIGH = lax.Precision.HIGHEST


def passed_along(value, axis, by):
    devices = lax.axis_size(axis)
    pairs = [(i, i + by) for i in range(devices) if 0 <= i + by < devices]
    return lax.ppermute(value, axis, pairs)


def shifted(value, axis, by):
    devices = lax.axis_size(axis)
    return lax.ppermute(value, axis, [(i, (i + by) % devices) for i in range(devices)])


def rms_scale(values):
    return lax.rsqrt(jnp.mean(values * values, axis=-1, keepdims=True) + EPS)


def keep_same(current):
    return current


def lead_product(left, right):
    return lax.dot_general(
        left, right, (((0,), (0,)), ((), ())), preferred_element_type=jnp.float32
    )


def on_device(
    block_input,
    output_cotangent,
    attn_gain,
    query_weight,
    key_weight,
    value_weight,
    output_weight,
    bias_table,
    buckets,
    ffn_gain,
    router_weight,
    routes,
    route_prior,
    gate_weight,
    up_weight,
    down_weight,
):
    tok_dev, seq_count, model_width = block_input.shape
    quarter = routes.shape[0]
    ctx_size = lax.axis_size("ctx")
    ctx_pos = lax.axis_index("ctx")
    exp_pos = lax.axis_index("exp")
    head_local = query_weight.shape[1]
    head_count = head_local // HD
    kv_width = seq_count * head_local
    seq_len = tok_dev * ctx_size
    score_scale = HD ** (-0.5)
    block_start = ctx_pos * tok_dev
    bucket_total, head_total = bias_table.shape
    row_total = quarter * seq_count
    input_full = block_input.astype(jnp.float32).reshape(tok_dev * seq_count, model_width)
    norm_one = rms_scale(input_full)
    normed_one = (input_full * norm_one * attn_gain).astype(jnp.bfloat16)
    query_w, key_w, value_w, output_w, gate_w, up_w, down_w = (
        lax.all_gather(query_weight, "ctx", axis=0, tiled=True),
        lax.all_gather(key_weight, "ctx", axis=0, tiled=True),
        lax.all_gather(value_weight, "ctx", axis=0, tiled=True),
        lax.all_gather(output_weight, "ctx", axis=1, tiled=True),
        lax.all_gather(gate_weight, "ctx", axis=1, tiled=True),
        lax.all_gather(up_weight, "ctx", axis=1, tiled=True),
        lax.all_gather(down_weight, "ctx", axis=1, tiled=True),
    )

    def project(weight):
        return jnp.dot(normed_one, weight, preferred_element_type=jnp.float32).astype(jnp.bfloat16)

    queries = project(query_w)
    keys_local = project(key_w).reshape(tok_dev, kv_width)
    values_local = project(value_w).reshape(tok_dev, kv_width)
    query_heads = queries.reshape(tok_dev, seq_count, head_count, HD)
    query_pos = block_start + jnp.arange(tok_dev, dtype=jnp.int32)
    table_heads = lax.dynamic_slice_in_dim(bias_table, exp_pos * head_count, head_count, 1).T
    bucket_hot = (jnp.arange(bucket_total, dtype=jnp.int32)[:, None] == buckets[None, :]).astype(
        jnp.float32
    )
    distance_bias = jnp.dot(table_heads, bucket_hot, precision=HIGH)

    def scores_for(key_piece, offset):
        key_count = key_piece.shape[0]
        key_heads = key_piece.reshape(key_count, seq_count, head_count, HD)
        raw_scores = (
            jnp.einsum(
                "qshd,kshd->shqk", query_heads, key_heads, preferred_element_type=jnp.float32
            )
            * score_scale
        )
        distance = query_pos[:, None] - (offset + jnp.arange(key_count, dtype=jnp.int32))[None, :]
        places = jnp.clip(distance, 0, seq_len - 1)
        raw_scores = raw_scores + distance_bias[:, places][None]
        return (jnp.where((distance >= 0)[None, None], raw_scores, FLOOR), places)

    initial = (
        jnp.full((seq_count, head_count, tok_dev), FLOOR, jnp.float32),
        jnp.zeros((seq_count, head_count, tok_dev), jnp.float32),
        jnp.zeros((seq_count, head_count, tok_dev, HD), jnp.float32),
    )
    pieces = (
        lax.all_gather(keys_local, "ctx", axis=0, tiled=True),
        lax.all_gather(values_local, "ctx", axis=0, tiled=True),
    )
    offset = jnp.int32(0)

    def update(current):
        row_max, row_sum, weighted = current
        scores, places = scores_for(pieces[0], offset)
        new_max = jnp.maximum(row_max, jnp.max(scores, axis=-1))
        weights = jnp.exp(scores - new_max[..., None])
        key_count = pieces[1].shape[0]
        value_heads = pieces[1].reshape(key_count, seq_count, head_count, HD)
        weighted = jnp.einsum(
            "shqk,kshd->shqd",
            weights.astype(jnp.bfloat16),
            value_heads,
            preferred_element_type=jnp.float32,
        )
        return (new_max, jnp.sum(weights, axis=-1), weighted)

    stats = lax.cond(offset <= block_start, update, keep_same, (initial[0], initial[1], initial[2]))
    row_max, row_sum, weighted = (stats[0], stats[1], stats[2])
    attended = weighted / row_sum[..., None]
    log_sum = row_max + jnp.log(row_sum)
    attended_low = (
        jnp.transpose(attended, (2, 0, 1, 3))
        .reshape(tok_dev * seq_count, head_local)
        .astype(jnp.bfloat16)
    )
    partial_out = jnp.dot(attended_low, output_w, preferred_element_type=jnp.float32)
    attn_rows = lax.psum_scatter(
        partial_out.astype(jnp.bfloat16), "exp", scatter_dimension=0, tiled=True
    ).astype(jnp.float32)
    own_input = lax.dynamic_slice_in_dim(input_full, exp_pos * row_total, row_total, 0)
    resid_flat = own_input + attn_rows
    capacity = (3 * row_total + 3) // 4
    norm_two = rms_scale(resid_flat)
    centred_two = resid_flat * norm_two
    flat_two = (centred_two * ffn_gain).astype(jnp.bfloat16)
    flat_two_wide = flat_two.astype(jnp.float32)
    expert_count = router_weight.shape[1]
    logits = jnp.dot(flat_two_wide, router_weight, precision=HIGH)
    route_flat = routes.reshape(row_total, 2)
    onehot = (route_flat[:, :, None] == jnp.arange(expert_count, dtype=jnp.int32)).astype(
        jnp.float32
    )
    chosen = jnp.sum(onehot * logits[:, None, :], axis=-1)
    softened = jax.nn.softmax(chosen, axis=-1)
    prior_flat = route_prior.reshape(row_total, 2)
    gates = prior_flat * softened
    slot_expert = route_flat.reshape(row_total * 2)
    slot_int = (slot_expert[:, None] == jnp.arange(expert_count, dtype=jnp.int32)).astype(jnp.int32)
    places_slot = jnp.sum((jnp.cumsum(slot_int, axis=0) - 1) * slot_int, axis=1)
    targets = slot_expert * capacity + places_slot
    dispatch = (
        jnp.arange(expert_count * capacity, dtype=jnp.int32)[:, None] == targets[None, :]
    ).astype(jnp.bfloat16)
    doubled = jnp.repeat(flat_two, 2, axis=0)
    outgoing = jnp.dot(dispatch, doubled, preferred_element_type=jnp.float32).astype(jnp.bfloat16)
    arrived = lax.all_to_all(
        outgoing.reshape(expert_count, capacity, model_width),
        "exp",
        split_axis=0,
        concat_axis=0,
        tiled=True,
    )
    arrived = arrived.reshape(expert_count * capacity, model_width)
    gate_pre = jnp.dot(arrived, gate_w[0], preferred_element_type=jnp.float32)
    up_pre = jnp.dot(arrived, up_w[0], preferred_element_type=jnp.float32)
    activated, gelu_back = jax.vjp(jax.nn.gelu, gate_pre)
    hidden_low = (activated * up_pre).astype(jnp.bfloat16)
    expert_out = jnp.dot(hidden_low, down_w[0], preferred_element_type=jnp.float32).astype(
        jnp.bfloat16
    )
    returned = lax.all_to_all(
        expert_out.reshape(expert_count, capacity, model_width),
        "exp",
        split_axis=0,
        concat_axis=0,
        tiled=True,
    )
    returned = returned.reshape(expert_count * capacity, model_width)
    slot_out = jnp.dot(dispatch.T, returned, preferred_element_type=jnp.float32).reshape(
        row_total, 2, model_width
    )
    mixed = jnp.einsum("rk,rkd->rd", gates, slot_out)
    block_output = (
        (resid_flat + mixed).astype(jnp.bfloat16).reshape(quarter, seq_count, model_width)
    )
    upstream = output_cotangent.astype(jnp.float32).reshape(row_total, model_width)
    slot_grad = (
        (gates[:, :, None] * upstream[:, None, :])
        .astype(jnp.bfloat16)
        .reshape(row_total * 2, model_width)
    )
    gate_value_grad = jnp.sum(slot_out * upstream[:, None, :], axis=-1)
    soft_grad = gate_value_grad * prior_flat
    chosen_grad = softened * (soft_grad - jnp.sum(softened * soft_grad, axis=-1, keepdims=True))
    logit_grad = jnp.sum(chosen_grad[:, :, None] * onehot, axis=1)
    router_part = lax.dot_general(
        logit_grad, flat_two_wide, (((0,), (0,)), ((), ())), precision=HIGH
    )
    normed_grad = jnp.dot(logit_grad, router_weight.T, precision=HIGH)
    grad_out = jnp.dot(dispatch, slot_grad, preferred_element_type=jnp.float32).astype(jnp.bfloat16)
    grad_arrived = lax.all_to_all(
        grad_out.reshape(expert_count, capacity, model_width),
        "exp",
        split_axis=0,
        concat_axis=0,
        tiled=True,
    ).reshape(expert_count * capacity, model_width)
    hidden_grad = jnp.dot(grad_arrived, down_w[0].T, preferred_element_type=jnp.float32)
    down_part = lead_product(hidden_low, grad_arrived)
    gate_pre_grad = gelu_back(hidden_grad * up_pre)[0].astype(jnp.bfloat16)
    up_pre_grad = (hidden_grad * activated).astype(jnp.bfloat16)
    arrived_grad = (
        jnp.dot(gate_pre_grad, gate_w[0].T, preferred_element_type=jnp.float32)
        + jnp.dot(up_pre_grad, up_w[0].T, preferred_element_type=jnp.float32)
    ).astype(jnp.bfloat16)
    gate_part = lead_product(arrived, gate_pre_grad)
    up_part = lead_product(arrived, up_pre_grad)
    sent_back = lax.all_to_all(
        arrived_grad.reshape(expert_count, capacity, model_width),
        "exp",
        split_axis=0,
        concat_axis=0,
        tiled=True,
    ).reshape(expert_count * capacity, model_width)
    slot_input_grad = jnp.dot(dispatch.T, sent_back, preferred_element_type=jnp.float32)
    normed_grad = normed_grad + jnp.sum(slot_input_grad.reshape(row_total, 2, model_width), axis=1)
    ffn_gain_part = jnp.sum(normed_grad * centred_two, axis=0)
    inner_two = normed_grad * ffn_gain
    resid_grad = upstream + norm_two * (
        inner_two - centred_two * jnp.mean(inner_two * centred_two, axis=-1, keepdims=True)
    )
    attn_grad_low = resid_grad.astype(jnp.bfloat16)
    attn_grad_all = lax.all_gather(attn_grad_low, "exp", axis=0, tiled=True)
    output_part = lead_product(attn_grad_all, attended_low)
    attended_grad = jnp.dot(attn_grad_all, output_w.T, preferred_element_type=jnp.float32).astype(
        jnp.bfloat16
    )
    grad_heads = jnp.transpose(
        attended_grad.reshape(tok_dev, seq_count, head_count, HD), (1, 2, 0, 3)
    )
    delta = jnp.sum(grad_heads.astype(jnp.float32) * attended, axis=-1)

    def back_piece(step, running):
        key_held, value_held, key_acc, value_acc, query_acc, distance_acc = running
        owner = (ctx_pos - step) % ctx_size
        offset = owner * tok_dev
        key_piece, value_piece = (key_held, value_held)

        def compute(partial_state):
            key_sum, value_sum, query_sum, distance_sum = partial_state
            scores, places = scores_for(key_piece, offset)
            probs = jnp.exp(scores - log_sum[..., None])
            key_heads = key_piece.reshape(tok_dev, seq_count, head_count, HD)
            value_heads = value_piece.reshape(tok_dev, seq_count, head_count, HD)
            value_term = jnp.einsum(
                "shqk,shqd->kshd",
                probs.astype(jnp.bfloat16),
                grad_heads,
                preferred_element_type=jnp.float32,
            )
            prob_grad = jnp.einsum(
                "shqd,kshd->shqk", grad_heads, value_heads, preferred_element_type=jnp.float32
            )
            score_grad = (probs * (prob_grad - delta[..., None])).astype(jnp.bfloat16)
            query_sum = (
                query_sum
                + jnp.einsum(
                    "shqk,kshd->shqd", score_grad, key_heads, preferred_element_type=jnp.float32
                )
                * score_scale
            )
            key_term = (
                jnp.einsum(
                    "shqk,qshd->kshd", score_grad, query_heads, preferred_element_type=jnp.float32
                )
                * score_scale
            )
            summed = jnp.sum(score_grad.astype(jnp.float32), axis=0)
            distance_sum = distance_sum.at[:, places.reshape(-1)].add(
                summed.reshape(head_count, -1)
            )
            return (
                key_sum + key_term.reshape(tok_dev, kv_width),
                value_sum + value_term.reshape(tok_dev, kv_width),
                query_sum,
                distance_sum,
            )

        partial_state = lax.cond(
            owner <= ctx_pos, compute, keep_same, (key_acc, value_acc, query_acc, distance_acc)
        )
        next_keys, next_values = passed_along((key_held, value_held), "ctx", 1)
        key_acc, value_acc = (
            shifted(partial_state[0].astype(jnp.bfloat16), "ctx", 1).astype(jnp.float32),
            shifted(partial_state[1].astype(jnp.bfloat16), "ctx", 1).astype(jnp.float32),
        )
        return (next_keys, next_values, key_acc, value_acc, partial_state[2], partial_state[3])

    grad_zeros = jnp.zeros((tok_dev, kv_width), jnp.float32)
    finished = lax.fori_loop(
        0,
        ctx_size,
        back_piece,
        (
            keys_local,
            values_local,
            grad_zeros,
            grad_zeros,
            jnp.zeros((seq_count, head_count, tok_dev, HD), jnp.float32),
            jnp.zeros((head_count, seq_len), jnp.float32),
        ),
    )
    key_grad_low = finished[2].reshape(tok_dev * seq_count, head_local).astype(jnp.bfloat16)
    value_grad_low = finished[3].reshape(tok_dev * seq_count, head_local).astype(jnp.bfloat16)
    query_grad_low = (
        jnp.transpose(finished[4], (2, 0, 1, 3))
        .reshape(tok_dev * seq_count, head_local)
        .astype(jnp.bfloat16)
    )
    table_sum = lax.dot_general(finished[5], bucket_hot, (((1,), (1,)), ((), ())), precision=HIGH)

    def back_project(grad_low, weight):
        return jnp.dot(grad_low, weight.T, preferred_element_type=jnp.float32)

    normed_one_part = (
        back_project(query_grad_low, query_w)
        + back_project(key_grad_low, key_w)
        + back_project(value_grad_low, value_w)
    )
    query_part = lead_product(normed_one, query_grad_low)
    key_part = lead_product(normed_one, key_grad_low)
    value_part = lead_product(normed_one, value_grad_low)
    summed_heads = lax.psum(normed_one_part.astype(jnp.bfloat16), "exp").astype(jnp.float32)
    own_grad = lax.dynamic_slice_in_dim(summed_heads, exp_pos * row_total, row_total, 0)
    own_scale = lax.dynamic_slice_in_dim(norm_one, exp_pos * row_total, row_total, 0)
    centred_one = own_input * own_scale
    inner_one = own_grad * attn_gain
    attn_gain_part = jnp.sum(own_grad * centred_one, axis=0)
    input_grad = (
        resid_grad
        + own_scale
        * (inner_one - centred_one * jnp.mean(inner_one * centred_one, axis=-1, keepdims=True))
    ).reshape(quarter, seq_count, model_width)
    table_full = lax.dynamic_update_slice_in_dim(
        jnp.zeros((head_total, bucket_total), jnp.float32), table_sum, exp_pos * head_count, 0
    )
    attn_gain_grad, ffn_gain_grad, router_sum, table_sum_all = lax.psum(
        (attn_gain_part, ffn_gain_part, router_part, table_full), ("ctx", "exp")
    )
    query_grad, key_grad, value_grad, output_sum, gate_sum, up_sum, down_sum = (
        lax.psum_scatter(query_part, "ctx", scatter_dimension=0, tiled=True),
        lax.psum_scatter(key_part, "ctx", scatter_dimension=0, tiled=True),
        lax.psum_scatter(value_part, "ctx", scatter_dimension=0, tiled=True),
        lax.psum_scatter(output_part, "ctx", scatter_dimension=0, tiled=True),
        lax.psum_scatter(gate_part, "ctx", scatter_dimension=0, tiled=True),
        lax.psum_scatter(up_part, "ctx", scatter_dimension=0, tiled=True),
        lax.psum_scatter(down_part, "ctx", scatter_dimension=0, tiled=True),
    )
    return (
        block_output,
        input_grad,
        attn_gain_grad,
        query_grad,
        key_grad,
        value_grad,
        output_sum.T,
        table_sum_all.T,
        ffn_gain_grad,
        router_sum.T,
        gate_sum[None],
        up_sum[None],
        down_sum[None],
    )


def solution(mesh):
    return jax.shard_map(
        on_device,
        mesh=mesh,
        in_specs=(
            P("ctx", None, None),
            P(("ctx", "exp"), None, None),
            P(),
            P("ctx", "exp"),
            P("ctx", "exp"),
            P("ctx", "exp"),
            P("exp", "ctx"),
            P(),
            P(),
            P(),
            P(),
            P(("ctx", "exp"), None, None),
            P(("ctx", "exp"), None, None),
            P("exp", "ctx", None),
            P("exp", "ctx", None),
            P("exp", "ctx", None),
        ),
        out_specs=(
            P(("ctx", "exp"), None, None),
            P(("ctx", "exp"), None, None),
            P(),
            P("ctx", "exp"),
            P("ctx", "exp"),
            P("ctx", "exp"),
            P("exp", "ctx"),
            P(),
            P(),
            P(),
            P("exp", "ctx", None),
            P("exp", "ctx", None),
            P("exp", "ctx", None),
        ),
        check_vma=False,
    )
```

profile of v0, /device:TPU:0, one launch (start us, length us, event | category | flops | bytes accessed | tf_op | source)
XLA Modules:
  0.0 1172.2 jit_solution(16158726513732254154)
XLA Ops:
  10.6 11.3 all_gather.30
  23.2 9.3 all_gather.31
  32.5 8.8 all_gather.32
  42.7 9.3 all_gather.33
  53.3 8.9 all_gather.34
  63.6 124.3 %conditional.2 = (f32[2,3,64]{2,1,0:T(4,128)}, f32[2,3,64]{2,1,0:T(4,128)}, f32[2,3,64]{2,1,0:T(4,128)S(1)}, f32[2,3,64,64]{3,1,0,2:T(4,128)S(1)}) conditional(s32[]{:T(128)} %convert_element_type.185, () %tuple.52, (s32[]{:T(128)}, bf16[512,384]{1,0:T(8,128)(2,1)S(1)}, bf16[64,2,3,64]{3,2,1,0:T(4,128)(2,1)S(1)}, f32[3,512]{1,0:T(4,128)}, ...), branch_computations={%region_1.0_spmd, %region_2.5_spmd} | conditional | flops 52166336 | bytes 7906340 | solution.py:137
  64.7 108.5 %gather_fusion = f32[32768,3]{1,0:T(8,128)} fusion(f32[3,512]{0,1:T(8,128)S(1)} %copy.143, s32[32768]{0:T(1024)S(1)} %broadcast_clamp_fusion), kind=kCustom, calls=%fused_computation | custom fusion | bytes 917504 | tf_op jit(solution)/shard_map/cond/branch_1_fun/gather | solution.py:108
  173.1 10.0 copy.128
  189.9 9.3 all_gather.35
  208.6 11.4 reduce-scatter.9.cloned.1.call-done
  222.5 3.5 all-to-all-start
  226.8 5.0 all-to-all-done
  231.8 10.0 all-gather.4.cloned.1.call-done
  241.7 3.2 fusion.33
  245.0 37.4 %all-gather.6.cloned.1.call-done = bf16[1,768,3072]{2,1,0:T(8,128)(2,1)} async-done(((bf16[1,96,3072]{2,1,0:T(8,128)(2,1)}), bf16[1,768,3072]{2,1,0:T(8,128)(2,1)}) %all-gather.6.cloned.1.call-update) | async-done | bytes 4718608 | tf_op jit(solution)/shard_map/all_gather | solution.py:79
  282.4 4.6 multiply_convert_fusion.1
  287.1 36.1 %all-gather.8.cloned.1.call-done = bf16[1,3072,768]{2,1,0:T(8,128)(2,1)} async-done(((bf16[1,384,768]{2,1,0:T(8,128)(2,1)}), bf16[1,3072,768]{2,1,0:T(8,128)(2,1)}) %all-gather.8.cloned.1.call-update) | async-done | bytes 4718608 | tf_op jit(solution)/shard_map/all_gather | solution.py:80
  323.1 3.9 fusion.46
  327.0 4.7 all-to-all-start.1
  332.8 5.5 all-to-all-done.1
  342.7 3.3 all-to-all-start.2
  346.8 5.2 all-to-all-done.2
  352.0 4.6 fusion.41
  356.6 4.3 fusion.27
  361.0 4.7 fusion.49
  365.6 3.3 all-to-all-start.3
  369.3 5.6 all-to-all-done.3
  376.8 13.8 %all_gather.39 = bf16[128,768]{1,0:T(8,128)(2,1)S(1)} all-gather(bf16[32,768]{1,0:T(8,128)(2,1)S(1)} %get-tuple-element.687), channel_id=1, replica_groups=mesh['ctx'=8,'exp'=4] {'exp'}, dimensions={0}, use_global_device_ids=true | all-gather | bytes 245760 | tf_op jit(solution)/shard_map/all_gather | solution.py:253
  391.7 370.1 %while.26 = (s32[]{:T(128)}, bf16[64,384]{1,0:T(8,128)(2,1)S(1)}, bf16[64,384]{1,0:T(8,128)(2,1)S(1)}, f32[64,384]{1,0:T(8,128)S(1)}, f32[64,384]{1,0:T(8,128)S(...) while((s32[]{:T(128)}, bf16[64,384]{1,0:T(8,128)(2,1)S(1)}, ...), condition=%wide.region_23.24_spmd.clone, body=%wide.region_18.0_spmd.clone.sunk | while | flops 16298130 | bytes 5476542 | solution.py:320
  391.8 41.0 %conditional.5 = ((f32[64,384]{1,0:T(8,128)S(1)}, f32[64,384]{1,0:T(8,128)S(1)}, f32[2,3,64,64]{3,2,1,0:T(8,128)S(1)}, f32[3,512]{0,1:T(8,128)S(1)})) conditional(s32[]{:T(128)} %convert_element_type.278, (f32[64,384]{1,0:T(8,128)S(1)}, f32[64,384]{1,0:T(8,128)S(1)}, f32[2,3,64,64]{3,2,1,0:T(8,128)S(1)}, f32[3,512]{0,1:T(8,128)S(1)}) %tuple.103, ...), branch_computations={%region_19.19_spmd, %region_20.22_spmd} | conditional | flops 16150657 | bytes 3509592 | solution.py:309
  392.0 10.8 gather_fusion.1
  408.3 24.5 %scatter_fusion = f32[3,512]{0,1:T(8,128)S(1)} fusion(f32[3,512]{0,1:T(8,128)S(1)} %get-tuple-element.415, s32[4096]{0:T(1024)S(1)} %bitcast.147, f32[4096,3]{1,0:T(8,128)S(1)} %bitcast.140), kind=kCustom, calls=%fused_computation.2 | custom fusion | flops 12288 | bytes 163840 | tf_op jit(solution)/shard_map/while/body/eval_jaxpr/cond/branch_1_fun/scatter-add | solution.py:299
  436.4 3.3 collective-permute-start.1
  440.7 39.3 %collective-permute-start.2 = (bf16[64,384]{1,0:T(8,128)(2,1)S(1)}, bf16[64,384]{1,0:T(8,128)(2,1)S(1)}, u32[]{:S(2)}, u32[]{:S(2)}) collective-permute-start(bf16[64,384]{1,0:T(8,128)(2,1)S(1)} %convert_element_type.279), channel_id=1, source_target_pairs={{0,4},{4,8},{8,12},{12,16},{16,20},{20,24},{24,28},{28,0},{1,5},{5... | collective-permute-start | bytes 147464 | tf_op jit(solution)/shard_map/while/body/eval_jaxpr/ppermute | solution.py:22
  480.0 2.4 collective-permute-start.3
  484.3 3.6 collective-permute-start.1
  489.3 41.3 %collective-permute-start.3 = (bf16[64,384]{1,0:T(8,128)(2,1)S(1)}, bf16[64,384]{1,0:T(8,128)(2,1)S(1)}, u32[]{:S(2)}, u32[]{:S(2)}) collective-permute-start(bf16[64,384]{1,0:T(8,128)(2,1)S(1)} %convert_element_type.281), channel_id=1, source_target_pairs={{0,4},{4,8},{8,12},{12,16},{16,20},{20,24},{24,28},{28,0},{1,5},{5... | collective-permute-start | bytes 147464 | tf_op jit(solution)/shard_map/while/body/eval_jaxpr/ppermute | solution.py:22
  532.5 3.5 collective-permute-start.1
  537.4 2.4 collective-permute-start.3
  539.8 38.6 %collective-permute-start = (bf16[64,384]{1,0:T(8,128)(2,1)S(1)}, bf16[64,384]{1,0:T(8,128)(2,1)S(1)}, u32[]{:S(2)}, u32[]{:S(2)}) collective-permute-start(bf16[64,384]{1,0:T(8,128)(2,1)S(1)} %copy.221), channel_id=1, source_target_pairs={{0,4},{4,8},{8,12},{12,16},{16,20},{20,24},{24,28},{1,5},{5,9},{9,... | collective-permute-start | bytes 147464 | tf_op jit(solution)/shard_map/while/body/eval_jaxpr/ppermute | solution.py:17
  578.3 5.1 collective-permute-start.1
  584.8 2.4 collective-permute-start.3
  589.1 41.7 %collective-permute-start.1 = (bf16[64,384]{1,0:T(8,128)(2,1)S(1)}, bf16[64,384]{1,0:T(8,128)(2,1)S(1)}, u32[]{:S(2)}, u32[]{:S(2)}) collective-permute-start(bf16[64,384]{1,0:T(8,128)(2,1)S(1)} %copy.222), channel_id=1, source_target_pairs={{0,4},{4,8},{8,12},{12,16},{16,20},{20,24},{24,28},{1,5},{5,9},{9,... | collective-permute-start | bytes 147464 | tf_op jit(solution)/shard_map/while/body/eval_jaxpr/ppermute | solution.py:17
  632.2 2.4 collective-permute-start.3
  636.5 2.8 collective-permute-start.1
  639.4 28.8 %collective-permute-done.2 = bf16[64,384]{1,0:T(8,128)(2,1)S(1)} collective-permute-done((bf16[64,384]{1,0:T(8,128)(2,1)S(1)}, bf16[64,384]{1,0:T(8,128)(2,1)S(1)}, u32[]{:S(2)}, u32[]{:S(2)}) %collective-permute-start.2) | collective-permute-done | bytes 49184 | tf_op jit(solution)/shard_map/while/body/eval_jaxpr/ppermute | solution.py:22
  668.9 7.5 collective-permute-start.2
  676.4 2.4 collective-permute-start.3
  680.8 3.0 collective-permute-start.1
  683.8 30.9 %collective-permute-done.2 = bf16[64,384]{1,0:T(8,128)(2,1)S(1)} collective-permute-done((bf16[64,384]{1,0:T(8,128)(2,1)S(1)}, bf16[64,384]{1,0:T(8,128)(2,1)S(1)}, u32[]{:S(2)}, u32[]{:S(2)}) %collective-permute-start.2) | collective-permute-done | bytes 49184 | tf_op jit(solution)/shard_map/while/body/eval_jaxpr/ppermute | solution.py:22
  715.5 7.4 collective-permute-start.3
  722.9 2.2 collective-permute-start
  725.2 5.1 collective-permute-start.1
  730.3 30.9 %collective-permute-done.2 = bf16[64,384]{1,0:T(8,128)(2,1)S(1)} collective-permute-done((bf16[64,384]{1,0:T(8,128)(2,1)S(1)}, bf16[64,384]{1,0:T(8,128)(2,1)S(1)}, u32[]{:S(2)}, u32[]{:S(2)}) %collective-permute-start.2) | collective-permute-done | bytes 49184 | tf_op jit(solution)/shard_map/while/body/eval_jaxpr/ppermute | solution.py:22
  770.5 5.1 fusion.87
  776.6 5.0 fusion.88
  782.8 5.1 fusion.89
  789.9 13.9 %all-reduce.3.cloned.1.call-done = bf16[128,768]{1,0:T(8,128)(2,1)} async-done(((bf16[128,768]{1,0:T(8,128)(2,1)}), bf16[128,768]{1,0:T(8,128)(2,1)}) %all-reduce.3.cloned.1.call-update) | async-done | bytes 196624 | tf_op jit(solution)/shard_map/psum | solution.py:353
  806.4 40.9 %all-reduce = (f32[768]{0:T(1024)}, f32[32,12]{0,1:T(8,128)}, f32[768]{0:T(1024)}, f32[768,4]{0,1:T(4,128)}) all-reduce(f32[768]{0:T(1024)S(1)} %get-tuple-element.651, f32[32,12]{0,1:T(8,128)S(1)} %bitcast.158, f32[768]{0:T(1024)S(1)} %copy-done.38, f32[768,4]{0,1:T(4,128)S(1)} %fusion.86), channel_id=1, replica_groups=mesh['ctx'=8,'exp'=4] {'ctx','exp'}, use_global_device_ids=true, to_apply=%region_27.28 | all-reduce | flops 4992 | bytes 39936 | tf_op jit(solution)/shard_map/psum | solution.py:367
  848.9 36.3 %reduce-scatter.13.cloned.1.call-done = f32[96,192]{1,0:T(8,128)} async-done(((f32[768,192]{1,0:T(8,128)}), f32[96,192]{1,0:T(8,128)}) %reduce-scatter.13.cloned.1.call-update) | async-done | bytes 73744 | tf_op jit(solution)/shard_map/reduce_scatter | solution.py:372
  885.2 38.6 %reduce-scatter.15.cloned.1.call-done = f32[96,192]{1,0:T(8,128)} async-done(((f32[768,192]{1,0:T(8,128)}), f32[96,192]{1,0:T(8,128)}) %reduce-scatter.15.cloned.1.call-update) | async-done | bytes 73744 | tf_op jit(solution)/shard_map/reduce_scatter | solution.py:373
  923.8 80.3 %reduce-scatter.19.cloned.1.call-done = f32[96,3072]{1,0:T(8,128)} async-done(((f32[768,3072]{1,0:T(8,128)}), f32[96,3072]{1,0:T(8,128)}) %reduce-scatter.19.cloned.1.call-update) | async-done | bytes 1179664 | tf_op jit(solution)/shard_map/reduce_scatter | solution.py:375
  1004.1 80.3 %reduce-scatter.21.cloned.1.call-done = f32[96,3072]{1,0:T(8,128)} async-done(((f32[768,3072]{1,0:T(8,128)}), f32[96,3072]{1,0:T(8,128)}) %reduce-scatter.21.cloned.1.call-update) | async-done | bytes 1179664 | tf_op jit(solution)/shard_map/reduce_scatter | solution.py:376
  1084.3 80.5 %reduce-scatter.23.cloned.1.call-done = f32[384,768]{1,0:T(8,128)} async-done(((f32[3072,768]{1,0:T(8,128)}), f32[384,768]{1,0:T(8,128)}) %reduce-scatter.23.cloned.1.call-update) | async-done | bytes 1179664 | tf_op jit(solution)/shard_map/reduce_scatter | solution.py:377
  (389 shorter events, 80.7 us)
Async XLA Ops:
  8.0 218.0 %copy-start = (f32[768,4]{0,1:T(4,128)S(1)}, f32[768,4]{0,1:T(4,128)}, u32[]{:S(2)}) copy-start(f32[768,4]{0,1:T(4,128)} %param.32) | copy-start | bytes 36868
  8.0 211.9 %reduce-scatter.9.cloned.1.call-start = ((), (), s32[]{:S(2)}) async-start(), calls=%async_computation.12 | async-start | bytes 245760 | tf_op jit(solution)/shard_map/reduce_scatter | solution.py:147
  9.1 210.9 %copy-start.9 = (f32[128,768]{1,0:T(8,128)}, f32[128,768]{1,0:T(8,128)S(1)}, u32[]{:S(2)}) copy-start(f32[128,768]{1,0:T(8,128)S(1)} %reshape.555) | copy-start | bytes 1179652
  10.6 21.9 %copy-start.30 = (bf16[96,192]{1,0:T(8,128)(2,1)S(1)}, bf16[96,192]{1,0:T(8,128)(2,1)}, u32[]{:S(2)}) copy-start(bf16[96,192]{1,0:T(8,128)(2,1)} %param.25) | copy-start | bytes 110596
  23.0 19.7 %copy-start.31 = (bf16[96,192]{1,0:T(8,128)(2,1)S(1)}, bf16[96,192]{1,0:T(8,128)(2,1)}, u32[]{:S(2)}) copy-start(bf16[96,192]{1,0:T(8,128)(2,1)} %param.27) | copy-start | bytes 110596
  42.4 19.7 %copy-start.50 = (s32[512]{0:T(512)S(1)}, s32[512]{0:T(512)}, u32[]{:S(2)}) copy-start(s32[512]{0:T(512)} %param.30) | copy-start | bytes 6148
  63.6 126.1 %copy-start.32 = (bf16[192,96]{1,0:T(8,128)(2,1)S(1)}, bf16[192,96]{1,0:T(8,128)(2,1)}, u32[]{:S(2)}) copy-start(bf16[192,96]{1,0:T(8,128)(2,1)} %param.28) | copy-start | bytes 110596
  200.2 41.6 %all-gather.4.cloned.1.call-start = ((), (), s32[]{:S(2)}) async-start(), calls=%async_computation.13 | async-start | bytes 5308416 | tf_op jit(solution)/shard_map/all_gather | solution.py:78
  200.8 81.6 %all-gather.6.cloned.1.call-start = ((), (), s32[]{:S(2)}) async-start(), calls=%async_computation.14 | async-start | bytes 5308416 | tf_op jit(solution)/shard_map/all_gather | solution.py:79
  201.4 20.0 %copy-start.34 = (f32[768]{0:T(1024)S(1)}, f32[768]{0:T(1024)}, u32[]{:S(2)}) copy-start(f32[768]{0:T(1024)} %param.31) | copy-start | bytes 9220
  201.4 121.7 %all-gather.8.cloned.1.call-start = ((), (), s32[]{:S(2)}) async-start(), calls=%async_computation.15 | async-start | bytes 5308416 | tf_op jit(solution)/shard_map/all_gather | solution.py:80
  205.9 16.6 %copy-start.48 = (s32[64]{0:T(128)}, s32[64]{0:T(128)S(1)}, u32[]{:S(2)}) copy-start(s32[64]{0:T(128)S(1)} %multiply_add_fusion.1) | copy-start | bytes 772
  221.5 23.5 %copy-start.18 = (bf16[32,768]{1,0:T(8,128)(2,1)}, bf16[32,768]{1,0:T(8,128)(2,1)S(1)}, u32[]{:S(2)}) copy-start(bf16[32,768]{1,0:T(8,128)(2,1)S(1)} %multiply_convert_fusion.6) | copy-start | bytes 147460
  222.5 9.3 all-to-all-start
  287.1 39.9 %copy-start.2 = (bf16[96,3072]{1,0:T(8,128)(2,1)}, bf16[96,3072]{1,0:T(8,128)(2,1)S(1)}, u32[]{:S(2)}) copy-start(bf16[96,3072]{1,0:T(8,128)(2,1)S(1)} %get-tuple-element.704) | copy-start | bytes 1769476
  327.0 19.0 %copy-start.42 = (f32[32,2]{0,1:T(2,128)S(1)}, f32[32,2]{0,1:T(2,128)}, u32[]{:S(2)}) copy-start(f32[32,2]{0,1:T(2,128)} %reshape.559) | copy-start | bytes 772
  327.0 19.8 %copy-start.43 = (s32[32,2]{0,1:T(2,128)S(1)}, s32[32,2]{0,1:T(2,128)}, u32[]{:S(2)}) copy-start(s32[32,2]{0,1:T(2,128)} %eq.83) | copy-start | bytes 772
  327.0 11.3 all-to-all-start.1
  342.7 9.3 all-to-all-start.2
  346.8 28.3 %copy-start.36 = (f32[32,4]{0,1:T(4,128)}, f32[32,4]{0,1:T(4,128)S(1)}, u32[]{:S(2)}) copy-start(f32[32,4]{0,1:T(4,128)S(1)} %select_reduce_fusion.1) | copy-start | bytes 1540
  365.6 9.3 all-to-all-start.3
  369.0 434.8 %all-reduce.3.cloned.1.call-start = ((), (), s32[]{:S(2)}) async-start(), calls=%async_computation.16 | async-start | bytes 393216 | tf_op jit(solution)/shard_map/psum | solution.py:353
  432.8 6.9 collective-permute-start.2
  432.9 6.9 collective-permute-start.3
  434.5 5.3 collective-permute-start
  436.4 4.1 collective-permute-start.1
  440.7 47.3 %collective-permute-start.2 = (bf16[64,384]{1,0:T(8,128)(2,1)S(1)}, bf16[64,384]{1,0:T(8,128)(2,1)S(1)}, u32[]{:S(2)}, u32[]{:S(2)}) collective-permute-start(bf16[64,384]{1,0:T(8,128)(2,1)S(1)} %convert_element_type.279), channel_id=1, source_target_pairs={{0,4},{4,8},{8,12},{12,16},{16,20},{20,24},{24,28},{28,0},{1,5},{5... | collective-permute-start | bytes 147464 | tf_op jit(solution)/shard_map/while/body/eval_jaxpr/ppermute | solution.py:22
  480.0 8.0 collective-permute-start.3
  482.4 5.6 collective-permute-start
  484.3 4.5 collective-permute-start.1
  488.9 47.1 %collective-permute-start.2 = (bf16[64,384]{1,0:T(8,128)(2,1)S(1)}, bf16[64,384]{1,0:T(8,128)(2,1)S(1)}, u32[]{:S(2)}, u32[]{:S(2)}) collective-permute-start(bf16[64,384]{1,0:T(8,128)(2,1)S(1)} %convert_element_type.279), channel_id=1, source_target_pairs={{0,4},{4,8},{8,12},{12,16},{16,20},{20,24},{24,28},{28,0},{1,5},{5... | collective-permute-start | bytes 147464 | tf_op jit(solution)/shard_map/while/body/eval_jaxpr/ppermute | solution.py:22
  489.3 46.7 %collective-permute-start.3 = (bf16[64,384]{1,0:T(8,128)(2,1)S(1)}, bf16[64,384]{1,0:T(8,128)(2,1)S(1)}, u32[]{:S(2)}, u32[]{:S(2)}) collective-permute-start(bf16[64,384]{1,0:T(8,128)(2,1)S(1)} %convert_element_type.281), channel_id=1, source_target_pairs={{0,4},{4,8},{8,12},{12,16},{16,20},{20,24},{24,28},{28,0},{1,5},{5... | collective-permute-start | bytes 147464 | tf_op jit(solution)/shard_map/while/body/eval_jaxpr/ppermute | solution.py:22
  530.6 5.5 collective-permute-start
  532.5 4.3 collective-permute-start.1
  537.0 46.5 %collective-permute-start.2 = (bf16[64,384]{1,0:T(8,128)(2,1)S(1)}, bf16[64,384]{1,0:T(8,128)(2,1)S(1)}, u32[]{:S(2)}, u32[]{:S(2)}) collective-permute-start(bf16[64,384]{1,0:T(8,128)(2,1)S(1)} %convert_element_type.279), channel_id=1, source_target_pairs={{0,4},{4,8},{8,12},{12,16},{16,20},{20,24},{24,28},{28,0},{1,5},{5... | collective-permute-start | bytes 147464 | tf_op jit(solution)/shard_map/while/body/eval_jaxpr/ppermute | solution.py:22
  537.4 46.1 %collective-permute-start.3 = (bf16[64,384]{1,0:T(8,128)(2,1)S(1)}, bf16[64,384]{1,0:T(8,128)(2,1)S(1)}, u32[]{:S(2)}, u32[]{:S(2)}) collective-permute-start(bf16[64,384]{1,0:T(8,128)(2,1)S(1)} %convert_element_type.281), channel_id=1, source_target_pairs={{0,4},{4,8},{8,12},{12,16},{16,20},{20,24},{24,28},{28,0},{1,5},{5... | collective-permute-start | bytes 147464 | tf_op jit(solution)/shard_map/while/body/eval_jaxpr/ppermute | solution.py:22
  539.8 43.7 %collective-permute-start = (bf16[64,384]{1,0:T(8,128)(2,1)S(1)}, bf16[64,384]{1,0:T(8,128)(2,1)S(1)}, u32[]{:S(2)}, u32[]{:S(2)}) collective-permute-start(bf16[64,384]{1,0:T(8,128)(2,1)S(1)} %copy.221), channel_id=1, source_target_pairs={{0,4},{4,8},{8,12},{12,16},{16,20},{20,24},{24,28},{1,5},{5,9},{9,... | collective-permute-start | bytes 147464 | tf_op jit(solution)/shard_map/while/body/eval_jaxpr/ppermute | solution.py:17
  578.3 6.0 collective-permute-start.1
  584.4 46.5 %collective-permute-start.2 = (bf16[64,384]{1,0:T(8,128)(2,1)S(1)}, bf16[64,384]{1,0:T(8,128)(2,1)S(1)}, u32[]{:S(2)}, u32[]{:S(2)}) collective-permute-start(bf16[64,384]{1,0:T(8,128)(2,1)S(1)} %convert_element_type.279), channel_id=1, source_target_pairs={{0,4},{4,8},{8,12},{12,16},{16,20},{20,24},{24,28},{28,0},{1,5},{5... | collective-permute-start | bytes 147464 | tf_op jit(solution)/shard_map/while/body/eval_jaxpr/ppermute | solution.py:22
  584.8 46.1 %collective-permute-start.3 = (bf16[64,384]{1,0:T(8,128)(2,1)S(1)}, bf16[64,384]{1,0:T(8,128)(2,1)S(1)}, u32[]{:S(2)}, u32[]{:S(2)}) collective-permute-start(bf16[64,384]{1,0:T(8,128)(2,1)S(1)} %convert_element_type.281), channel_id=1, source_target_pairs={{0,4},{4,8},{8,12},{12,16},{16,20},{20,24},{24,28},{28,0},{1,5},{5... | collective-permute-start | bytes 147464 | tf_op jit(solution)/shard_map/while/body/eval_jaxpr/ppermute | solution.py:22
  587.2 43.7 %collective-permute-start = (bf16[64,384]{1,0:T(8,128)(2,1)S(1)}, bf16[64,384]{1,0:T(8,128)(2,1)S(1)}, u32[]{:S(2)}, u32[]{:S(2)}) collective-permute-start(bf16[64,384]{1,0:T(8,128)(2,1)S(1)} %copy.221), channel_id=1, source_target_pairs={{0,4},{4,8},{8,12},{12,16},{16,20},{20,24},{24,28},{1,5},{5,9},{9,... | collective-permute-start | bytes 147464 | tf_op jit(solution)/shard_map/while/body/eval_jaxpr/ppermute | solution.py:17
  589.1 42.6 %collective-permute-start.1 = (bf16[64,384]{1,0:T(8,128)(2,1)S(1)}, bf16[64,384]{1,0:T(8,128)(2,1)S(1)}, u32[]{:S(2)}, u32[]{:S(2)}) collective-permute-start(bf16[64,384]{1,0:T(8,128)(2,1)S(1)} %copy.222), channel_id=1, source_target_pairs={{0,4},{4,8},{8,12},{12,16},{16,20},{20,24},{24,28},{1,5},{5,9},{9,... | collective-permute-start | bytes 147464 | tf_op jit(solution)/shard_map/while/body/eval_jaxpr/ppermute | solution.py:17
  631.8 36.3 %collective-permute-start.2 = (bf16[64,384]{1,0:T(8,128)(2,1)S(1)}, bf16[64,384]{1,0:T(8,128)(2,1)S(1)}, u32[]{:S(2)}, u32[]{:S(2)}) collective-permute-start(bf16[64,384]{1,0:T(8,128)(2,1)S(1)} %convert_element_type.279), channel_id=1, source_target_pairs={{0,4},{4,8},{8,12},{12,16},{16,20},{20,24},{24,28},{28,0},{1,5},{5... | collective-permute-start | bytes 147464 | tf_op jit(solution)/shard_map/while/body/eval_jaxpr/ppermute | solution.py:22
  632.2 36.5 %collective-permute-start.3 = (bf16[64,384]{1,0:T(8,128)(2,1)S(1)}, bf16[64,384]{1,0:T(8,128)(2,1)S(1)}, u32[]{:S(2)}, u32[]{:S(2)}) collective-permute-start(bf16[64,384]{1,0:T(8,128)(2,1)S(1)} %convert_element_type.281), channel_id=1, source_target_pairs={{0,4},{4,8},{8,12},{12,16},{16,20},{20,24},{24,28},{28,0},{1,5},{5... | collective-permute-start | bytes 147464 | tf_op jit(solution)/shard_map/while/body/eval_jaxpr/ppermute | solution.py:22
  634.6 34.1 %collective-permute-start = (bf16[64,384]{1,0:T(8,128)(2,1)S(1)}, bf16[64,384]{1,0:T(8,128)(2,1)S(1)}, u32[]{:S(2)}, u32[]{:S(2)}) collective-permute-start(bf16[64,384]{1,0:T(8,128)(2,1)S(1)} %copy.221), channel_id=1, source_target_pairs={{0,4},{4,8},{8,12},{12,16},{16,20},{20,24},{24,28},{1,5},{5,9},{9,... | collective-permute-start | bytes 147464 | tf_op jit(solution)/shard_map/while/body/eval_jaxpr/ppermute | solution.py:17
  636.5 32.2 %collective-permute-start.1 = (bf16[64,384]{1,0:T(8,128)(2,1)S(1)}, bf16[64,384]{1,0:T(8,128)(2,1)S(1)}, u32[]{:S(2)}, u32[]{:S(2)}) collective-permute-start(bf16[64,384]{1,0:T(8,128)(2,1)S(1)} %copy.222), channel_id=1, source_target_pairs={{0,4},{4,8},{8,12},{12,16},{16,20},{20,24},{24,28},{1,5},{5,9},{9,... | collective-permute-start | bytes 147464 | tf_op jit(solution)/shard_map/while/body/eval_jaxpr/ppermute | solution.py:17
  668.9 45.8 %collective-permute-start.2 = (bf16[64,384]{1,0:T(8,128)(2,1)S(1)}, bf16[64,384]{1,0:T(8,128)(2,1)S(1)}, u32[]{:S(2)}, u32[]{:S(2)}) collective-permute-start(bf16[64,384]{1,0:T(8,128)(2,1)S(1)} %convert_element_type.279), channel_id=1, source_target_pairs={{0,4},{4,8},{8,12},{12,16},{16,20},{20,24},{24,28},{28,0},{1,5},{5... | collective-permute-start | bytes 147464 | tf_op jit(solution)/shard_map/while/body/eval_jaxpr/ppermute | solution.py:22
  676.4 38.8 %collective-permute-start.3 = (bf16[64,384]{1,0:T(8,128)(2,1)S(1)}, bf16[64,384]{1,0:T(8,128)(2,1)S(1)}, u32[]{:S(2)}, u32[]{:S(2)}) collective-permute-start(bf16[64,384]{1,0:T(8,128)(2,1)S(1)} %convert_element_type.281), channel_id=1, source_target_pairs={{0,4},{4,8},{8,12},{12,16},{16,20},{20,24},{24,28},{28,0},{1,5},{5... | collective-permute-start | bytes 147464 | tf_op jit(solution)/shard_map/while/body/eval_jaxpr/ppermute | solution.py:22
  678.8 36.4 %collective-permute-start = (bf16[64,384]{1,0:T(8,128)(2,1)S(1)}, bf16[64,384]{1,0:T(8,128)(2,1)S(1)}, u32[]{:S(2)}, u32[]{:S(2)}) collective-permute-start(bf16[64,384]{1,0:T(8,128)(2,1)S(1)} %copy.221), channel_id=1, source_target_pairs={{0,4},{4,8},{8,12},{12,16},{16,20},{20,24},{24,28},{1,5},{5,9},{9,... | collective-permute-start | bytes 147464 | tf_op jit(solution)/shard_map/while/body/eval_jaxpr/ppermute | solution.py:17
  680.8 34.5 %collective-permute-start.1 = (bf16[64,384]{1,0:T(8,128)(2,1)S(1)}, bf16[64,384]{1,0:T(8,128)(2,1)S(1)}, u32[]{:S(2)}, u32[]{:S(2)}) collective-permute-start(bf16[64,384]{1,0:T(8,128)(2,1)S(1)} %copy.222), channel_id=1, source_target_pairs={{0,4},{4,8},{8,12},{12,16},{16,20},{20,24},{24,28},{1,5},{5,9},{9,... | collective-permute-start | bytes 147464 | tf_op jit(solution)/shard_map/while/body/eval_jaxpr/ppermute | solution.py:17
  715.4 45.8 %collective-permute-start.2 = (bf16[64,384]{1,0:T(8,128)(2,1)S(1)}, bf16[64,384]{1,0:T(8,128)(2,1)S(1)}, u32[]{:S(2)}, u32[]{:S(2)}) collective-permute-start(bf16[64,384]{1,0:T(8,128)(2,1)S(1)} %convert_element_type.279), channel_id=1, source_target_pairs={{0,4},{4,8},{8,12},{12,16},{16,20},{20,24},{24,28},{28,0},{1,5},{5... | collective-permute-start | bytes 147464 | tf_op jit(solution)/shard_map/while/body/eval_jaxpr/ppermute | solution.py:22
  715.5 46.2 %collective-permute-start.3 = (bf16[64,384]{1,0:T(8,128)(2,1)S(1)}, bf16[64,384]{1,0:T(8,128)(2,1)S(1)}, u32[]{:S(2)}, u32[]{:S(2)}) collective-permute-start(bf16[64,384]{1,0:T(8,128)(2,1)S(1)} %convert_element_type.281), channel_id=1, source_target_pairs={{0,4},{4,8},{8,12},{12,16},{16,20},{20,24},{24,28},{28,0},{1,5},{5... | collective-permute-start | bytes 147464 | tf_op jit(solution)/shard_map/while/body/eval_jaxpr/ppermute | solution.py:22
  722.9 38.8 %collective-permute-start = (bf16[64,384]{1,0:T(8,128)(2,1)S(1)}, bf16[64,384]{1,0:T(8,128)(2,1)S(1)}, u32[]{:S(2)}, u32[]{:S(2)}) collective-permute-start(bf16[64,384]{1,0:T(8,128)(2,1)S(1)} %copy.221), channel_id=1, source_target_pairs={{0,4},{4,8},{8,12},{12,16},{16,20},{20,24},{24,28},{1,5},{5,9},{9,... | collective-permute-start | bytes 147464 | tf_op jit(solution)/shard_map/while/body/eval_jaxpr/ppermute | solution.py:17
  725.2 36.6 %collective-permute-start.1 = (bf16[64,384]{1,0:T(8,128)(2,1)S(1)}, bf16[64,384]{1,0:T(8,128)(2,1)S(1)}, u32[]{:S(2)}, u32[]{:S(2)}) collective-permute-start(bf16[64,384]{1,0:T(8,128)(2,1)S(1)} %copy.222), channel_id=1, source_target_pairs={{0,4},{4,8},{8,12},{12,16},{16,20},{20,24},{24,28},{1,5},{5,9},{9,... | collective-permute-start | bytes 147464 | tf_op jit(solution)/shard_map/while/body/eval_jaxpr/ppermute | solution.py:17
  765.0 82.3 %reduce-scatter.17.cloned.1.call-start = ((), (), s32[]{:S(2)}) async-start(), calls=%async_computation.20 | async-start | bytes 884736 | tf_op jit(solution)/shard_map/reduce_scatter | solution.py:374
  766.2 82.7 %reduce-scatter.11.cloned.1.call-start = ((), (), s32[]{:S(2)}) async-start(), calls=%async_computation.17 | async-start | bytes 884736 | tf_op jit(solution)/shard_map/reduce_scatter | solution.py:371
  767.9 117.3 %reduce-scatter.13.cloned.1.call-start = ((), (), s32[]{:S(2)}) async-start(), calls=%async_computation.18 | async-start | bytes 884736 | tf_op jit(solution)/shard_map/reduce_scatter | solution.py:372
  769.2 154.6 %reduce-scatter.15.cloned.1.call-start = ((), (), s32[]{:S(2)}) async-start(), calls=%async_computation.19 | async-start | bytes 884736 | tf_op jit(solution)/shard_map/reduce_scatter | solution.py:373
  770.4 233.6 %reduce-scatter.19.cloned.1.call-start = ((), (), s32[]{:S(2)}) async-start(), calls=%async_computation.21 | async-start | bytes 10616832 | tf_op jit(solution)/shard_map/reduce_scatter | solution.py:375
  775.6 308.7 %reduce-scatter.21.cloned.1.call-start = ((), (), s32[]{:S(2)}) async-start(), calls=%async_computation.22 | async-start | bytes 10616832 | tf_op jit(solution)/shard_map/reduce_scatter | solution.py:376
  781.7 383.1 %reduce-scatter.23.cloned.1.call-start = ((), (), s32[]{:S(2)}) async-start(), calls=%async_computation.23 | async-start | bytes 10616832 | tf_op jit(solution)/shard_map/reduce_scatter | solution.py:377
  787.9 16.9 %copy-start.26 = (f32[32,768]{1,0:T(8,128)S(1)}, f32[32,768]{1,0:T(8,128)}, u32[]{:S(2)}) copy-start(f32[32,768]{1,0:T(8,128)} %get-tuple-element.688) | copy-start | bytes 294916
  788.0 18.5 %copy-start.38 = (f32[768]{0:T(1024)S(1)}, f32[768]{0:T(1024)}, u32[]{:S(2)}) copy-start(f32[768]{0:T(1024)} %get-tuple-element.653) | copy-start | bytes 9220
  788.0 376.8 %copy-start.1 = (f32[768,4]{0,1:T(4,128)S(1)}, f32[768,4]{0,1:T(4,128)}, u32[]{:S(2)}) copy-start(f32[768,4]{0,1:T(4,128)} %param.32) | copy-start | bytes 36868
  (36 other events, 165.5 us)
Sparse Core Ops, SparseCore 0:
  200.3 19.6 reduce-scatter.8
  765.1 38.6 all-reduce.2
Sparse Core Ops, SparseCore 1:
  202.7 39.0 all-gather.3
  243.7 38.7 all-gather.5
  284.4 38.7 all-gather.7
  768.9 38.8 reduce-scatter.16
  811.5 34.9 reduce-scatter.10
  850.2 34.9 reduce-scatter.12
  888.8 34.9 reduce-scatter.14
  927.7 76.3 reduce-scatter.18
  1008.0 76.3 reduce-scatter.20
  1088.4 76.3 reduce-scatter.22
where the time goes:
time: 1170 us
  waiting for transfers between devices  544 us (46%)
  starting transfers between devices  247 us (21%)
  local copies, waits for them, and re-layouts  153 us (13%)
  blocking collectives  112 us (10%)
  matrix products  61.6 us (5%)
  other arithmetic  37.5 us (3%)
  between operations  16.5 us (1%)
    gather x4, local copies, waits for them, and re-layouts, scores_for(): raw_scores = raw_scores + distance_bias[:, places][None]  130 us
    ppermute x16, starting transfers between devices, passed_along(): return lax.ppermute(value, axis, pairs)  120 us
    ppermute x16, starting transfers between devices, shifted(): lax.ppermute(value, axis, [(i, (i + by) % devices) for i in range(devices)])  111 us
    ppermute x16, waiting for transfers between devices, shifted(): lax.ppermute(value, axis, [(i, (i + by) % devices) for i in range(devices)])  92.2 us
    reduce_scatter x1, waiting for transfers between devices, on_device(): lax.psum_scatter(down_part, 'ctx', scatter_dimension=0, tiled=True)  80.5 us
    reduce_scatter x1, waiting for transfers between devices, on_device(): lax.psum_scatter(gate_part, 'ctx', scatter_dimension=0, tiled=True)  80.3 us
    reduce_scatter x1, waiting for transfers between devices, on_device(): lax.psum_scatter(up_part, 'ctx', scatter_dimension=0, tiled=True)  80.3 us
    psum x1, blocking collectives, on_device(): lax.psum((attn_gain_part, ffn_gain_part, router_part, table_full), ('ctx'...  40.9 us
  transfers between devices with their start and end apart: 48, of which 25 were waited for; matrix products, arithmetic and copies ran while one was open for 4% of the time, Pallas kernels for 0%

commit v1 on v0

v1 whole, which is shorter than its diff:
```python
import functools

import jax
import jax.numpy as jnp
from jax import lax
from jax.experimental import pallas as pl
from jax.experimental.pallas import tpu as pltpu
from jax.sharding import PartitionSpec as P

HD = 64
EPS = 1e-06
FLOOR = -1e30
HIGH = lax.Precision.HIGHEST
F32 = jnp.float32
BF16 = jnp.bfloat16
LANES = 128
GELU_C = 0.7978845608028654
GELU_A = 0.044715


def swap(value, axis, bits):
    devices = lax.axis_size(axis)
    return lax.ppermute(value, axis, [(i, i ^ bits) for i in range(devices)])


def gather_ctx(value):
    devices = lax.axis_size("ctx")
    near = jnp.concatenate(
        [value[None]] + [swap(value, "ctx", 2 * j)[None] for j in range(1, devices // 2)], axis=0
    )
    return near, swap(near, "ctx", 1)


def reduce_ctx(near, far):
    got = swap(far, "ctx", 1)
    both = (near.astype(F32) + got.astype(F32)).astype(near.dtype)
    return [both[0]] + [swap(both[j], "ctx", 2 * j) for j in range(1, near.shape[0])]


def spread_exp(value):
    return [value] + [swap(value, "exp", d) for d in range(1, lax.axis_size("exp"))]


def nn(left, right, precision=None):
    return lax.dot_general(
        left, right, (((1,), (0,)), ((), ())), precision=precision, preferred_element_type=F32
    )


def nt(left, right, precision=None):
    return lax.dot_general(
        left, right, (((1,), (1,)), ((), ())), precision=precision, preferred_element_type=F32
    )


def tn(left, right, precision=None):
    return lax.dot_general(
        left, right, (((0,), (0,)), ((), ())), precision=precision, preferred_element_type=F32
    )


def call(body, name, outs, ids, *args, scratch=()):
    single = not isinstance(outs, list)
    specs = [pl.BlockSpec(memory_space=pltpu.SMEM)]
    specs += [pl.BlockSpec(memory_space=pltpu.VMEM)] * len(args)
    shapes = [jax.ShapeDtypeStruct(*o) for o in ([outs] if single else outs)]
    out_specs = [pl.BlockSpec(memory_space=pltpu.VMEM)] * len(shapes)
    return pl.pallas_call(
        body,
        out_shape=shapes[0] if single else shapes,
        in_specs=specs,
        out_specs=out_specs[0] if single else out_specs,
        scratch_shapes=list(scratch),
        compiler_params=pltpu.CompilerParams(vmem_limit_bytes=58 * 1024 * 1024),
        name=name,
    )(ids, *args)


def rms_scale(values):
    return lax.rsqrt(jnp.mean(values * values, axis=-1, keepdims=True) + EPS)


def iota(shape, axis):
    return lax.broadcasted_iota(jnp.int32, shape, axis)


def block_before(rows, tok, quarter):
    early, late = iota((rows, rows), 0), iota((rows, rows), 1)
    same = (early % tok) // quarter == (late % tok) // quarter
    return jnp.where(same & (early < late), 1.0, 0.0).astype(BF16)


def slot_hot(route0, route1, expert, before, tok, quarter, cap, parts):
    rows = route0.shape[1]
    named = (route0 == expert) | (route1 == expert)
    flags = jnp.broadcast_to(jnp.where(named, 1.0, 0.0), (16, rows)).astype(BF16)
    rank = nn(flags, before)[0:1].astype(jnp.int32)
    block = (iota((1, rows), 1) % tok) // quarter
    place = jnp.where(named, block * cap + rank, -1)
    return iota((parts * cap, rows), 0) == place, named


def pack_body(quarter, ids, cot, info, out):
    width = out.shape[1]
    out[0:quarter, :] = cot[:, :width]
    out[quarter : 2 * quarter, :] = cot[:, width:]
    values = info[...]
    hi = values.astype(BF16)
    rest = values - hi.astype(F32)
    mid = rest.astype(BF16)
    low = (rest - mid.astype(F32)).astype(BF16)
    lanes = values.shape[1]
    eye = (iota((lanes, width), 0) == iota((lanes, width), 1)).astype(F32).astype(BF16)
    stacked = jnp.concatenate(
        [hi.astype(F32), mid.astype(F32), low.astype(F32), jnp.zeros((4, lanes), F32)], axis=0
    ).astype(BF16)
    out[2 * quarter :, :] = nn(stacked, eye).astype(BF16)


def early_body(tok, quarter, cap, ids, *refs):
    pieces, (cot_out, info_out, slots_out) = refs[:-3], refs[-3:]
    exp_pos = ids[1]
    rows = 2 * tok
    info = jnp.zeros((16, rows), F32)
    for d, piece in enumerate(pieces):
        owner = exp_pos ^ d
        for s in range(2):
            cot_out[pl.ds(pl.multiple_of(s * tok + owner * quarter, quarter), quarter), :] = piece[
                s * quarter : (s + 1) * quarter, :
            ]
        lane, row = iota((LANES, rows), 0), iota((LANES, rows), 1)
        target = (lane // quarter) * tok + owner * quarter + lane % quarter
        spot = jnp.where((target == row) & (lane < 2 * quarter), 1.0, 0.0).astype(BF16)
        info = info + nn(piece[2 * quarter :, :LANES], spot)
    low = info[0:4] + (info[4:8] + info[8:12])
    info_out[...] = jnp.concatenate([low, jnp.zeros((4, rows), F32)], axis=0)
    before = block_before(rows, tok, quarter)
    hot, _ = slot_hot(
        low[0:1].astype(jnp.int32),
        low[1:2].astype(jnp.int32),
        exp_pos,
        before,
        tok,
        quarter,
        cap,
        len(pieces),
    )
    slots_out[...] = nn(jnp.where(hot, 1.0, 0.0).astype(BF16), cot_out[...]).astype(BF16)


def project_body(aligned, head_local, ids, x, gain, near, far, q_out, kv_out, a_out, w_out, out_t):
    ctx_pos = ids[0]
    tok, width = x.shape[0], gain.shape[1]
    if aligned:
        count, rows, _ = near.shape
        for j in range(count):
            for par, ref in ((0, near), (1, far)):
                owner = ctx_pos ^ (2 * j + par)
                spot = pl.ds(pl.multiple_of(owner * rows, rows), rows)
                w_out[spot, :] = ref[j, :, : 3 * head_local]
                out_t[spot, :] = ref[j, :, 3 * head_local :]
    else:
        w_out[...] = near[:, : 3 * head_local]
        out_t[...] = near[:, 3 * head_local :]
    for s in range(2):
        piece = x[:, s * width : (s + 1) * width].astype(F32)
        a_out[s * tok : (s + 1) * tok, :] = (piece * rms_scale(piece) * gain[...]).astype(BF16)
    full = nn(a_out[...], w_out[...]).astype(BF16)
    q_out[...] = full[:, :head_local]
    kv_out[...] = full[:, head_local:]


def attend_body(
    heads, ids, q, near, far, table, rev, o_out, low_out, p_out, kv_out
):
    ctx_pos, exp_pos = ids[0], ids[1]
    count, rows, _ = near.shape
    tok = rows // 2
    hl = heads * HD
    seq_len = rev.shape[1]
    start = ctx_pos * tok
    for j in range(count):
        for par, ref in ((0, near), (1, far)):
            kv_out[ctx_pos ^ (2 * j + par)] = ref[j].reshape(2, tok, 2 * hl)
    buckets, head_total = table.shape
    pick = jnp.where(
        iota((8, head_total), 1) == exp_pos * heads + iota((8, head_total), 0), 1.0, 0.0
    )
    own_table = nt(pick, table[...], HIGH)
    hot = jnp.where(iota((buckets, seq_len), 0) == rev[...], 1.0, 0.0)
    bias = pltpu.roll(nn(own_table, hot, HIGH), start + 1, 1)
    open_keys = iota((tok, seq_len), 1) <= start + iota((tok, seq_len), 0)
    skewed = []
    for h in range(heads):
        wide = jnp.broadcast_to(bias[h : h + 1, :], (tok, seq_len))
        turned = pltpu.roll(wide, 0, 1, stride=1, stride_axis=0)
        skewed.append(jnp.where(open_keys, turned, FLOOR))
    for s in range(2):
        outs = []
        for h in range(heads):
            query = q[s * tok : (s + 1) * tok, h * HD : (h + 1) * HD]
            key = kv_out[:, s, :, h * HD : (h + 1) * HD].reshape(seq_len, HD)
            value = kv_out[:, s, :, hl + h * HD : hl + (h + 1) * HD].reshape(seq_len, HD)
            scores = nt(query, key) * (HD**-0.5) + skewed[h]
            top = jnp.max(scores, axis=-1, keepdims=True)
            weights = jnp.exp(scores - top)
            probs = weights * (1.0 / jnp.sum(weights, axis=-1, keepdims=True))
            p_out[s * heads + h] = probs
            outs.append(nn(probs.astype(BF16), value))
        out = jnp.concatenate(outs, axis=1)
        o_out[s * tok : (s + 1) * tok, :] = out
        low_out[s * tok : (s + 1) * tok, :] = out.astype(BF16)


def gate_values(logits, info):
    route0, route1 = info[0:1].astype(jnp.int32), info[1:2].astype(jnp.int32)
    choice0 = jnp.zeros_like(info[0:1])
    choice1 = jnp.zeros_like(info[0:1])
    for e in range(logits.shape[0]):
        choice0 = choice0 + jnp.where(route0 == e, logits[e : e + 1], 0.0)
        choice1 = choice1 + jnp.where(route1 == e, logits[e : e + 1], 0.0)
    top = jnp.maximum(choice0, choice1)
    up0, up1 = jnp.exp(choice0 - top), jnp.exp(choice1 - top)
    total = up0 + up1
    return up0 / total, up1 / total


def route_body(tok, quarter, cap, parts, ids, *refs):
    x = refs[0]
    lows, mats = refs[1 : 1 + parts], refs[1 + parts : 1 + 2 * parts]
    gain, router_t, info_ref, resid_out, gates_out, slots_out = refs[1 + 2 * parts :]
    exp_pos = ids[1]
    rows, width = 2 * tok, gain.shape[1]
    attn = nt(lows[0][...], mats[0][...])
    for d in range(1, parts):
        attn = attn + nt(lows[d][...], mats[d][...])
    for s in range(2):
        resid_out[s * tok : (s + 1) * tok, :] = (
            x[:, s * width : (s + 1) * width].astype(F32) + attn[s * tok : (s + 1) * tok]
        )
    resid = resid_out[...]
    normed = (resid * rms_scale(resid) * gain[...]).astype(BF16)
    logits = nt(router_t[...], normed.astype(F32), HIGH)
    info = info_ref[...]
    soft0, soft1 = gate_values(logits, info)
    gate0, gate1 = info[2:3] * soft0, info[3:4] * soft1
    gates_out[...] = jnp.concatenate([gate0, gate1, jnp.zeros((6, rows), F32)], axis=0)
    route0, route1 = info[0:1].astype(jnp.int32), info[1:2].astype(jnp.int32)
    before = block_before(rows, tok, quarter)
    hot, _ = slot_hot(route0, route1, exp_pos, before, tok, quarter, cap, parts)
    hot = jnp.where(hot, 1.0, 0.0).astype(BF16)
    first = route0 == exp_pos
    gate = jnp.where(first, gate0, gate1)
    slope = soft0 * soft1 * jnp.where(first, info[2:3], info[3:4])
    other = jnp.where(first, info[1:2], info[0:1])
    gate_hi, slope_hi = gate.astype(BF16).astype(F32), slope.astype(BF16).astype(F32)
    extras = jnp.concatenate(
        [gate_hi, gate - gate_hi, slope_hi, slope - slope_hi, other, jnp.zeros((LANES - 5, rows), F32)],
        axis=0,
    ).astype(BF16)
    slots_out[:, :width] = nn(hot, normed).astype(BF16)
    slots_out[:, width:] = nt(hot, extras).astype(BF16)


def expert_back_body(
    step, ids, x_near, x_far, c_near, c_far, w_in, down, router_t,
    dx_near, dx_far, hid_near, hid_far, dg_near, dg_far, du_near, du_far, router_out,
):
    exp_pos = ids[1]
    width, hidden = w_in.shape[0], down.shape[0]
    experts = router_t.shape[0]
    gate_w, up_w = w_in[:, :hidden], w_in[:, hidden:]
    down_w = down[...]
    own = jnp.zeros((1, width), F32)
    for e in range(experts):
        own = own + jnp.where(exp_pos == e, router_t[e : e + 1, :], 0.0)
    router_sum = jnp.zeros((8, width), F32)
    sides = (
        (x_near, c_near, dx_near, hid_near, dg_near, du_near),
        (x_far, c_far, dx_far, hid_far, dg_far, du_far),
    )
    for x, c, dx, hid, dg_out, du_out in sides:
        for lead in range(0, x.shape[0], step):
            part = slice(lead, lead + step)
            rows = x[part, :width]
            extras = x[part, width:].astype(F32)
            gate = extras[:, 0:1] + extras[:, 1:2]
            slope = extras[:, 2:3] + extras[:, 3:4]
            other = extras[:, 4:5].astype(jnp.int32)
            pre = nn(rows, gate_w)
            up = nn(rows, up_w)
            raw = nt(c[part, :], down_w)
            squared = pre * pre
            tanh = jnp.tanh(GELU_C * (pre + GELU_A * pre * squared))
            half = 0.5 * (1.0 + tanh)
            act = pre * half
            hidden_low = (act * up).astype(BF16)
            hid[part, :] = hidden_low
            slope_act = half + 0.5 * pre * (1.0 - tanh * tanh) * (
                GELU_C * (1.0 + 3.0 * GELU_A * squared)
            )
            gate_grad = jnp.sum(hidden_low.astype(F32) * raw, axis=-1, keepdims=True)
            grad = gate * raw
            dg = (grad * up * slope_act).astype(BF16)
            du = (grad * act).astype(BF16)
            dg_out[part, :] = dg
            du_out[part, :] = du
            tilt = gate_grad * slope
            kind = iota((step, 8), 1)
            spread = jnp.where(kind == exp_pos, tilt, 0.0) - jnp.where(kind == other, tilt, 0.0)
            back = nt(dg, gate_w) + nt(du, up_w) + tilt * own
            for e in range(experts):
                back = back - jnp.where(other == e, tilt, 0.0) * router_t[e : e + 1, :]
            dx[part, :] = back.astype(BF16)
            router_sum = router_sum + tn(spread, rows.astype(F32), HIGH)
    router_out[...] = router_sum


def expert_rest_body(
    step, ids, x_near, x_far, c_near, c_far, down, hid_near, hid_far, dg_near, dg_far, du_near, du_far,
    y_near, y_far, down_out, w_out,
):
    width, hidden = down.shape[1], down.shape[0]
    down_w = down[...]
    totals = [0.0, 0.0, 0.0]
    sides = (
        (x_near, c_near, hid_near, dg_near, du_near, y_near),
        (x_far, c_far, hid_far, dg_far, du_far, y_far),
    )
    for x, c, hid, dg, du, y in sides:
        for lead in range(0, x.shape[0], step):
            part = slice(lead, lead + step)
            rows = x[part, :width]
            extras = x[part, width:].astype(F32)
            gate = extras[:, 0:1] + extras[:, 1:2]
            y[part, :] = nn(hid[part, :], down_w).astype(BF16)
            dy = (gate * c[part, :].astype(F32)).astype(BF16)
            totals[0] = totals[0] + tn(hid[part, :], dy)
            totals[1] = totals[1] + tn(rows, dg[part, :])
            totals[2] = totals[2] + tn(rows, du[part, :])
    down_out[...] = totals[0]
    w_out[:, :hidden] = totals[1].astype(BF16)
    w_out[:, hidden:] = totals[2].astype(BF16)


def mix_body(tok, quarter, cap, parts, ids, resid, info_ref, gates_ref, y, out, held):
    exp_pos = ids[1]
    rows, width = 2 * tok, resid.shape[1]
    info, gates = info_ref[...], gates_ref[...]
    route0, route1 = info[0:1].astype(jnp.int32), info[1:2].astype(jnp.int32)
    before = block_before(rows, tok, quarter)
    block = (iota((1, rows), 1) % tok) // quarter
    weights = []
    for e in range(parts):
        named = ((route0 == e) | (route1 == e)) & (block == exp_pos)
        flags = jnp.broadcast_to(jnp.where(named, 1.0, 0.0), (16, rows)).astype(BF16)
        rank = jnp.where(named, nn(flags, before)[0:1].astype(jnp.int32), -1)
        gate = jnp.where(route0 == e, gates[0:1], gates[1:2])
        weights.append(jnp.where(iota((cap, rows), 0) == rank, gate, 0.0))
    weights = jnp.concatenate(weights, axis=0)
    hi = weights.astype(BF16)
    low = (weights - hi.astype(F32)).astype(BF16)
    held[...] = resid[...] + tn(hi, y[...]) + tn(low, y[...])
    for s in range(2):
        spot = pl.ds(pl.multiple_of(s * tok + exp_pos * quarter, quarter), quarter)
        out[:, s * width : (s + 1) * width] = held[spot, :].astype(BF16)


def attend_back_body(heads, tok, quarter, cap, parts, buckets, ids, *refs):
    pieces = refs[:parts]
    (
        resid_ref, cot, gain, info_ref, low, o, out_t, q, kv, p, rev,
        own_out, dq_out, near_out, far_out, dout_t, small_out, held, dkv,
    ) = refs[parts:]
    ctx_pos, exp_pos = ids[0], ids[1]
    rows, width = resid_ref.shape
    hl = heads * HD
    count = kv.shape[0]
    seq_len = count * tok
    start = ctx_pos * tok
    info = info_ref[...]
    route0, route1 = info[0:1].astype(jnp.int32), info[1:2].astype(jnp.int32)
    before = block_before(rows, tok, quarter)
    grad = jnp.zeros((rows, width), F32)
    for d, piece in enumerate(pieces):
        hot, _ = slot_hot(route0, route1, exp_pos ^ d, before, tok, quarter, cap, parts)
        grad = grad + tn(jnp.where(hot, 1.0, 0.0).astype(BF16), piece[...])
    resid = resid_ref[...]
    scale = rms_scale(resid)
    centred = resid * scale
    small_out[0:1, :] = jnp.sum(grad * centred, axis=0, keepdims=True) * (1.0 / parts)
    inner = grad * gain[...]
    held[...] = cot[...].astype(F32) + scale * (
        inner - centred * jnp.mean(inner * centred, axis=-1, keepdims=True)
    )
    for s in range(2):
        spot = pl.ds(pl.multiple_of(s * tok + exp_pos * quarter, quarter), quarter)
        own_out[s * quarter : (s + 1) * quarter, :] = held[spot, :]
    attn_grad = held[...].astype(BF16)
    grad_o = nn(attn_grad, out_t[...]).astype(BF16)
    dout_t[...] = tn(attn_grad, low[...]).astype(BF16)
    sums = [jnp.zeros((tok, seq_len), F32) for _ in range(heads)]
    for s in range(2):
        here = slice(s * tok, (s + 1) * tok)
        keys, values, queries = [], [], []
        for h in range(heads):
            cols = slice(h * HD, (h + 1) * HD)
            probs = p[s * heads + h]
            key = kv[:, s, :, cols].reshape(seq_len, HD)
            value = kv[:, s, :, hl + h * HD : hl + (h + 1) * HD].reshape(seq_len, HD)
            do = grad_o[here, cols]
            delta = jnp.sum(do.astype(F32) * o[here, cols], axis=-1, keepdims=True)
            ds = (probs * (nt(do, value) - delta)).astype(BF16)
            sums[h] = sums[h] + ds.astype(F32)
            values.append(tn(probs.astype(BF16), do))
            keys.append(tn(ds, q[here, cols]) * (HD**-0.5))
            queries.append(nn(ds, key) * (HD**-0.5))
        dq_out[here, :] = jnp.concatenate(queries, axis=1).astype(BF16)
        dkv[:, s] = (
            jnp.concatenate(keys + values, axis=1).astype(BF16).reshape(count, tok, 2 * hl)
        )
    for j in range(count // 2):
        near_out[j] = dkv[ctx_pos ^ (2 * j)].reshape(rows, 2 * hl)
        far_out[j] = dkv[ctx_pos ^ (2 * j + 1)].reshape(rows, 2 * hl)
    table = jnp.zeros((8, width), F32)
    for h in range(heads):
        turned = sums[h]
        step = 1
        while step < tok:
            bit = (iota((tok, seq_len), 0) // step) % 2 == 1
            turned = jnp.where(bit, pltpu.roll(turned, seq_len - step, 1), turned)
            step *= 2
        line = jnp.sum(turned, axis=0, keepdims=True)
        line = pltpu.roll(line, seq_len - start - 1, 1)
        spot = (exp_pos * heads + h) * buckets
        for lead in range(0, seq_len, 512):
            cut = slice(lead, min(lead + 512, seq_len))
            here = line[:, cut]
            hot = jnp.where(iota((here.shape[1], width), 1) == spot + rev[cut, :], 1.0, 0.0)
            table = table + nn(jnp.broadcast_to(here, (8, here.shape[1])), hot, HIGH)
    small_out[1:2, :] = table[0:1]
    small_out[2:8, :] = jnp.zeros((6, width), F32)


def back_project_body(quarter, parts, ids, *refs):
    terms = refs[:-10]
    dq, w, a, dout_t, x, gain, small, rows_out, w_near, small_out = refs[-10:]
    rows, width = a.shape
    tok = rows // 2
    dkv = terms[0][...].astype(F32)
    for term in terms[1:]:
        dkv = dkv + term[...].astype(F32)
    grads = jnp.concatenate([dq[...], dkv.astype(BF16)], axis=1)
    da = nt(grads, w[...])
    total = jnp.zeros((1, width), F32)
    for s in range(2):
        piece = x[:, s * width : (s + 1) * width].astype(F32)
        here = da[s * tok : (s + 1) * tok]
        total = total + jnp.sum(piece * rms_scale(piece) * here, axis=0, keepdims=True)
        for z in range(parts):
            rows_out[z, s * quarter : (s + 1) * quarter, :] = here[
                z * quarter : (z + 1) * quarter
            ].astype(BF16)
    wide = tn(a[...], grads)
    cut = grads.shape[1]
    w_near[:, :cut] = wide.astype(BF16)
    w_near[:, cut:] = dout_t[...]
    small_out[0:1, :] = total
    small_out[1:8, :] = small[1:8, :]


def finish_body(tok, quarter, ids, x, gain, own, mine, *refs):
    pieces, out = refs[:-1], refs[-1]
    exp_pos = ids[1]
    width = gain.shape[1]
    for s in range(2):
        spot = pl.ds(pl.multiple_of(exp_pos * quarter, quarter), quarter)
        rows = x[spot, s * width : (s + 1) * width].astype(F32)
        here = slice(s * quarter, (s + 1) * quarter)
        grad = mine[here, :].astype(F32)
        for piece in pieces:
            grad = grad + piece[here, :].astype(F32)
        scale = rms_scale(rows)
        centred = rows * scale
        inner = grad * gain[...]
        out[:, s * width : (s + 1) * width] = own[here, :] + scale * (
            inner - centred * jnp.mean(inner * centred, axis=-1, keepdims=True)
        )


def on_device(
    block_input,
    output_cotangent,
    attn_gain,
    query_weight,
    key_weight,
    value_weight,
    output_weight,
    bias_table,
    buckets,
    ffn_gain,
    router_weight,
    routes,
    route_prior,
    gate_weight,
    up_weight,
    down_weight,
):
    tok, seqs, width = block_input.shape
    quarter = routes.shape[0]
    ctx_size, parts = lax.axis_size("ctx"), lax.axis_size("exp")
    ctx_pos, exp_pos = lax.axis_index("ctx"), lax.axis_index("exp")
    hl = query_weight.shape[1]
    heads = hl // HD
    cap = (3 * quarter * seqs + 3) // 4
    slots = parts * cap
    rows = tok * seqs
    shard = query_weight.shape[0]
    hidden = down_weight.shape[1]
    half = ctx_size // 2
    seq_len = tok * ctx_size
    aligned = shard % 16 == 0
    ids = jnp.stack([ctx_pos, exp_pos]).astype(jnp.int32)
    x = block_input.reshape(tok, seqs * width)
    gain_one, gain_two = attn_gain.reshape(1, width), ffn_gain.reshape(1, width)
    router_t = router_weight.T
    rev = buckets[::-1].reshape(1, seq_len)

    packed = jnp.concatenate([query_weight, key_weight, value_weight, output_weight.T], axis=1)
    if aligned:
        w_near, w_far = gather_ctx(packed)
    else:
        w_near = lax.all_gather(packed, "ctx", axis=0, tiled=True)
        w_far = w_near[:8]

    sent = jnp.concatenate(
        [
            jnp.swapaxes(gate_weight.reshape(shard, ctx_size, hidden), 0, 1),
            jnp.swapaxes(up_weight.reshape(shard, ctx_size, hidden), 0, 1),
        ],
        axis=2,
    )
    w_in = lax.all_to_all(sent, "ctx", split_axis=0, concat_axis=0, tiled=True)
    w_in = w_in.reshape(width, 2 * hidden)
    down = down_weight.reshape(hidden, width)

    info = jnp.concatenate([routes.astype(F32), route_prior], axis=2)
    info = jnp.transpose(info, (2, 1, 0)).reshape(4, seqs * quarter)
    cot_pack = call(
        functools.partial(pack_body, quarter),
        "pack",
        ((2 * quarter + 16, width), BF16),
        ids,
        output_cotangent.reshape(quarter, seqs * width),
        info,
    )
    cot_block, info_block, cot_slots = call(
        functools.partial(early_body, tok, quarter, cap),
        "early_slots",
        [((rows, width), BF16), ((8, rows), F32), ((slots, width), BF16)],
        ids,
        *spread_exp(cot_pack),
    )

    q, kv, normed, w_qkv, out_t = call(
        functools.partial(project_body, aligned, hl),
        "project",
        [
            ((rows, hl), BF16),
            ((rows, 2 * hl), BF16),
            ((rows, width), BF16),
            ((width, 3 * hl), BF16),
            ((width, hl), BF16),
        ],
        ids, x, gain_one, w_near, w_far,
    )
    kv_near, kv_far = gather_ctx(kv)
    out_mats = spread_exp(out_t)
    c_near, c_far = gather_ctx(cot_slots)
    o, low, p, kv_all = call(
        functools.partial(attend_body, heads),
        "attend",
        [
            ((rows, hl), F32),
            ((rows, hl), BF16),
            ((seqs * heads, tok, seq_len), F32),
            ((ctx_size, seqs, tok, 2 * hl), BF16),
        ],
        ids, q, kv_near, kv_far, bias_table, rev,
    )
    lows = spread_exp(low)
    resid, gates, x_slots = call(
        functools.partial(route_body, tok, quarter, cap, parts),
        "route",
        [((rows, width), F32), ((8, rows), F32), ((slots, width + LANES), BF16)],
        ids, x, *lows, *out_mats, gain_two, router_t, info_block,
    )
    x_near, x_far = gather_ctx(x_slots)
    side = half * slots
    x_near, x_far = x_near.reshape(side, width + LANES), x_far.reshape(side, width + LANES)
    c_near, c_far = c_near.reshape(side, width), c_far.reshape(side, width)
    step = min(side, 4 * slots)
    (
        dx_near, dx_far, hid_near, hid_far, dg_near, dg_far, du_near, du_far, router_part,
    ) = call(
        functools.partial(expert_back_body, step),
        "expert_back",
        [((side, width), BF16)] * 2 + [((side, hidden), BF16)] * 6 + [((8, width), F32)],
        ids, x_near, x_far, c_near, c_far, w_in, down, router_t,
    )
    dx_terms = reduce_ctx(
        dx_near.reshape(half, slots, width), dx_far.reshape(half, slots, width)
    )
    y_near, y_far, down_grad, w_grad = call(
        functools.partial(expert_rest_body, step),
        "expert_rest",
        [
            ((side, width), BF16),
            ((side, width), BF16),
            ((hidden, width), F32),
            ((width, 2 * hidden), BF16),
        ],
        ids, x_near, x_far, c_near, c_far, down, hid_near, hid_far, dg_near, dg_far, du_near, du_far,
    )
    dx = sum(term.astype(F32) for term in dx_terms).astype(BF16)
    dx_pieces = spread_exp(dx)

    y_terms = reduce_ctx(y_near.reshape(half, slots, width), y_far.reshape(half, slots, width))
    y = sum(term.astype(F32) for term in y_terms).astype(BF16)
    y = lax.all_to_all(
        y.reshape(parts, cap, width), "exp", split_axis=0, concat_axis=0, tiled=True
    ).reshape(slots, width)
    block_output = call(
        functools.partial(mix_body, tok, quarter, cap, parts),
        "mix",
        ((quarter, seqs * width), BF16),
        ids, resid, info_block, gates, y,
        scratch=[pltpu.VMEM((rows, width), F32)],
    ).reshape(quarter, seqs, width)
    w_back = lax.all_to_all(
        w_grad.reshape(ctx_size, shard, 2 * hidden), "ctx", split_axis=0, concat_axis=0, tiled=True
    )
    w_back = jnp.swapaxes(w_back, 0, 1).astype(F32)
    gate_grad = w_back[:, :, :hidden].reshape(1, shard, ctx_size * hidden)
    up_grad = w_back[:, :, hidden:].reshape(1, shard, ctx_size * hidden)

    resid_grad, dq, dkv_near, dkv_far, dout_t, small = call(
        functools.partial(attend_back_body, heads, tok, quarter, cap, parts, bias_table.shape[0]),
        "attend_back",
        [
            ((seqs * quarter, width), F32),
            ((rows, hl), BF16),
            ((half, rows, 2 * hl), BF16),
            ((half, rows, 2 * hl), BF16),
            ((width, hl), BF16),
            ((8, width), F32),
        ],
        ids, *dx_pieces, resid, cot_block, gain_two, info_block, low, o, out_t, q, kv_all, p,
        rev.reshape(seq_len, 1),
        scratch=[
            pltpu.VMEM((rows, width), F32),
            pltpu.VMEM((ctx_size, seqs, tok, 2 * hl), BF16),
        ],
    )
    dkv_terms = reduce_ctx(dkv_near, dkv_far)
    small = jnp.concatenate([jnp.zeros((1, width), F32), small[0:2], router_part[:4], small[2:3]])
    da_parts, proj_grad, small = call(
        functools.partial(back_project_body, quarter, parts),
        "back_project",
        [
            ((parts, seqs * quarter, width), BF16),
            ((width, 4 * hl), BF16),
            ((8, width), F32),
        ],
        ids, *dkv_terms, dq, w_qkv, normed, dout_t, x, gain_one, small,
    )
    da_parts = [
        lax.dynamic_index_in_dim(da_parts, exp_pos ^ d, 0, keepdims=False) for d in range(parts)
    ]
    da_terms = [da_parts[0]] + [swap(da_parts[d], "exp", d) for d in range(1, parts)]
    input_grad = call(
        functools.partial(finish_body, tok, quarter),
        "finish",
        ((quarter, seqs * width), F32),
        ids, x, gain_one, resid_grad, *da_terms,
    ).reshape(quarter, seqs, width)

    proj_grad = proj_grad.reshape(ctx_size, shard, 4 * hl)
    near = jnp.stack([lax.dynamic_index_in_dim(proj_grad, ctx_pos ^ (2 * j), 0, False) for j in range(half)])
    far = jnp.stack(
        [lax.dynamic_index_in_dim(proj_grad, ctx_pos ^ (2 * j + 1), 0, False) for j in range(half)]
    )
    proj = sum(term.astype(F32) for term in reduce_ctx(near, far))

    small = sum(spread_exp(small))
    small = small + swap(small, "ctx", 1)
    small = small + sum(swap(small, "ctx", 2 * j) for j in range(1, half))
    head_total = bias_table.shape[1]
    table_grad = small[2, : head_total * bias_table.shape[0]].reshape(head_total, -1).T
    return (
        block_output,
        input_grad,
        small[0],
        proj[:, :hl],
        proj[:, hl : 2 * hl],
        proj[:, 2 * hl : 3 * hl],
        proj[:, 3 * hl :].T,
        table_grad,
        small[1],
        small[3:7].T,
        gate_grad,
        up_grad,
        down_grad.reshape(1, hidden, width),
    )


def solution(mesh):
    return jax.shard_map(
        on_device,
        mesh=mesh,
        in_specs=(
            P("ctx", None, None),
            P(("ctx", "exp"), None, None),
            P(),
            P("ctx", "exp"),
            P("ctx", "exp"),
            P("ctx", "exp"),
            P("exp", "ctx"),
            P(),
            P(),
            P(),
            P(),
            P(("ctx", "exp"), None, None),
            P(("ctx", "exp"), None, None),
            P("exp", "ctx", None),
            P("exp", "ctx", None),
            P("exp", "ctx", None),
        ),
        out_specs=(
            P(("ctx", "exp"), None, None),
            P(("ctx", "exp"), None, None),
            P(),
            P("ctx", "exp"),
            P("ctx", "exp"),
            P("ctx", "exp"),
            P("exp", "ctx"),
            P(),
            P(),
            P(),
            P("exp", "ctx", None),
            P("exp", "ctx", None),
            P("exp", "ctx", None),
        ),
        check_vma=False,
    )
```

time: 1170 us -> 260 us (0.22)
  waiting for transfers between devices: 544 us -> 94.5 us
  starting transfers between devices: 247 us -> 76 us
  local copies, waits for them, and re-layouts: 153 us -> 28.2 us
  blocking collectives: 112 us -> 0 us
  matrix products: 61.6 us -> 0 us
  Pallas kernels: 0 us -> 47 us
  other arithmetic: 37.5 us -> 11.6 us
  between operations: 16.5 us -> 1.37 us
    reduce_scatter x8 -> x0, waiting for transfers between devices: 327 us -> none  [the longest x1 80.5 us: on_device(): lax.psum_scatter(down_part, 'ctx', scatter_dimension=0, tiled=True)]
    ppermute x32 -> x54, starting transfers between devices: 231 us -> 64.6 us  [swap(): return lax.ppermute(value, axis, [(i, i ^ bits) for i in range(devices)])]
    gather x4 -> x0, local copies, waits for them, and re-layouts: 130 us -> none  [scores_for(): raw_scores = raw_scores + distance_bias[:, places][None]]
    all_gather x3 -> x0, waiting for transfers between devices: 83.5 us -> none  [the longest x1 37.4 us: on_device(): lax.all_gather(up_weight, 'ctx', axis=1, tiled=True)]
    all_gather x7 -> x0, blocking collectives: 70.7 us -> none  [the longest x1 13.8 us: on_device(): attn_grad_all = lax.all_gather(attn_grad_low, 'exp', axis=0, tiled=True)]
    dot_general x38 -> x0, matrix products: 61.6 us -> none  [the longest x7 20 us: lead_product(): lax.dot_general(left, right, (((0,), (0,)), ((), ())), preferred_element_...]
    pallas_call x0 -> x11, Pallas kernels: none -> 47 us  [call(): pl.pallas_call(body, out_shape=shapes[0] if single else shapes, in_specs=...]
    psum x1 -> x0, blocking collectives: 40.9 us -> none  [on_device(): lax.psum((attn_gain_part, ffn_gain_part, router_part, table_full), ('ctx'...]
  transfers between devices with their start and end apart: 48 -> 57, of which waited for: 25 -> 22; matrix products, arithmetic and copies ran while one was open for 4% -> 11% of each run, Pallas kernels for 0% -> 9%
where the time goes in v1:
time: 260 us; the launch traced here: 259 us
  waiting for transfers between devices  94.5 us (36%)
  starting transfers between devices  76 us (29%)
  Pallas kernels  47 us (18%)
  local copies, waits for them, and re-layouts  28.2 us (11%)
  other arithmetic  11.6 us (4%)
    ppermute x54, waiting for transfers between devices, swap(): return lax.ppermute(value, axis, [(i, i ^ bits) for i in range(devices)])  92.1 us
    ppermute x54, starting transfers between devices, swap(): return lax.ppermute(value, axis, [(i, i ^ bits) for i in range(devices)])  64.6 us
    pallas_call x11, Pallas kernels, call(): pl.pallas_call(body, out_shape=shapes[0] if single else shapes, in_specs=...  47 us
    unnamed x95, local copies, waits for them, and re-layouts  9.8 us
  transfers between devices with their start and end apart: 57, of which 22 were waited for; matrix products, arithmetic and copies ran while one was open for 11% of the time, Pallas kernels for 9%

profile of v1, /device:TPU:0, one launch (start us, length us, event | category | flops | bytes accessed | tf_op | source)
XLA Modules:
  0.0 258.6 jit_solution(18304409094013307552)
XLA Ops:
  2.6 3.0 %collective-permute-start = (bf16[96,768]{1,0:T(8,128)(2,1)S(1)}, bf16[96,768]{1,0:T(8,128)(2,1)S(1)}, u32[]{:S(2)}, u32[]{:S(2)}) collective-permute-start(bf16[96,768]{1,0:T(8,128)(2,1)S(1)} %pad_maximum_fusion.6), channel_id=1, source_target_pairs={{0,8},{4,12},{8,0},{12,4},{16,24},{20,28},{24,16},{28,20},{1,9},{5... | collective-permute-start | bytes 442376 | tf_op jit(solution)/shard_map/ppermute | solution.py:23
  5.6 1.5 collective-permute-start.1
  8.1 1.8 collective-permute-done
  9.9 4.2 %collective-permute-done.1 = bf16[96,768]{1,0:T(8,128)(2,1)S(1)} collective-permute-done((bf16[96,768]{1,0:T(8,128)(2,1)S(1)}, bf16[96,768]{1,0:T(8,128)(2,1)S(1)}, u32[]{:S(2)}, u32[]{:S(2)}) %collective-permute-start.1) | collective-permute-done | bytes 147488 | tf_op jit(solution)/shard_map/ppermute | solution.py:23
  17.0 2.7 %project.1 = (bf16[128,192]{1,0:T(8,128)(2,1)}, bf16[128,384]{1,0:T(8,128)(2,1)}, bf16[128,768]{1,0:T(8,128)(2,1)}, bf16[768,576]{1,0:T(8,128)(2,1)}, bf16[768,192]{1,0:T(8,128)(2,1)}) custom-call(s32[2]{0:T(128)} %pad_add_fusion.ids, bf16[64,1536]{1,0:T(8,128)(2,1)} %bitcast.117, f32[1,768]{1,0:T(1,128)} %reshape.114.gain.refs_9_, ...), custom_call_target="tpu_custom_call" | custom-call | tf_op jit(solution)/shard_map/project/pallas_call | solution.py:68
  19.8 1.5 collective-permute-start.6
  21.3 1.5 collective-permute-start.4
  23.3 3.2 %collective-permute-done.6 = bf16[128,384]{1,0:T(8,128)(2,1)S(1)} collective-permute-done((bf16[128,384]{1,0:T(8,128)(2,1)}, bf16[128,384]{1,0:T(8,128)(2,1)S(1)}, u32[]{:S(2)}, u32[]{:S(2)}) %collective-permute-start.6) | collective-permute-done | bytes 98336 | tf_op jit(solution)/shard_map/ppermute | solution.py:23
  26.5 1.7 collective-permute-done.4
  29.2 1.6 collective-permute-start.11
  32.2 1.6 pack.1.refs_0_
  34.2 2.6 collective-permute-start.15
  36.8 1.4 collective-permute-start.16
  38.1 6.0 %collective-permute-done.14.refs_1_ = bf16[48,768]{1,0:T(8,128)(2,1)S(1)} collective-permute-done((bf16[48,768]{1,0:T(8,128)(2,1)}, bf16[48,768]{1,0:T(8,128)(2,1)S(1)}, u32[]{:S(2)}, u32[]{:S(2)}) %collective-permute-start.14) | collective-permute-done | bytes 73760 | tf_op jit(solution)/shard_map/ppermute | solution.py:23
  44.1 2.3 collective-permute-start.12
  46.4 3.0 %collective-permute-start.13 = (bf16[768,192]{1,0:T(8,128)(2,1)}, bf16[768,192]{1,0:T(8,128)(2,1)S(1)}, u32[]{:S(2)}, u32[]{:S(2)}) collective-permute-start(bf16[768,192]{1,0:T(8,128)(2,1)} %get-tuple-element.53.refs_5_.refs_10_), channel_id=1, source_target_pairs={{0,3},{1,2},{2,1},{3,0},{4,7},{5,6},{6,5},{7,4},{8,11},{9,10},{10,... | collective-permute-start | bytes 884744 | tf_op jit(solution)/shard_map/ppermute | solution.py:23
  51.0 4.7 %attend.1 = (f32[128,192]{1,0:T(8,128)}, bf16[128,192]{1,0:T(8,128)(2,1)}, f32[6,64,512]{2,1,0:T(8,128)}, bf16[8,2,64,384]{3,2,1,0:T(8,128)(2,1)}) custom-call(s32[2]{0:T(128)} %pad_add_fusion.ids, bf16[128,192]{1,0:T(8,128)(2,1)} %get-tuple-element.50.q.refs_11_, bf16[4,128,384]{2,1,0:T(8,128)(2,1)} %copy-done.5, bf16[4,128,384]{2,1,0:T(8,128)(2,1)} %copy-done.15, ...), custom_call_target="tpu_custom_call" | custom-call | tf_op jit(solution)/shard_map/attend/pallas_call | solution.py:68
  56.6 1.7 collective-permute-start.8
  58.3 1.9 collective-permute-start.9
  61.4 2.1 early_slots.1
  63.5 13.4 %collective-permute-done.12.refs_7_ = bf16[768,192]{1,0:T(8,128)(2,1)S(1)} collective-permute-done((bf16[768,192]{1,0:T(8,128)(2,1)}, bf16[768,192]{1,0:T(8,128)(2,1)S(1)}, u32[]{:S(2)}, u32[]{:S(2)}) %collective-permute-start.12) | collective-permute-done | bytes 294944 | tf_op jit(solution)/shard_map/ppermute | solution.py:23
  77.0 10.1 %collective-permute-done.9.refs_3_ = bf16[128,192]{1,0:T(8,128)(2,1)S(1)} collective-permute-done((bf16[128,192]{1,0:T(8,128)(2,1)}, bf16[128,192]{1,0:T(8,128)(2,1)S(1)}, u32[]{:S(2)}, u32[]{:S(2)}) %collective-permute-start.9) | collective-permute-done | bytes 49184 | tf_op jit(solution)/shard_map/ppermute | solution.py:23
  87.7 4.0 %route.1 = (f32[128,768]{1,0:T(8,128)}, f32[8,128]{1,0:T(8,128)}, bf16[96,896]{1,0:T(8,128)(2,1)}) custom-call(s32[2]{0:T(128)} %pad_add_fusion.ids, bf16[64,1536]{1,0:T(8,128)(2,1)} %bitcast.118, bf16[128,192]{1,0:T(8,128)(2,1)} %get-tuple-element.52.refs_1_.refs_8_, bf16[128,192]{1,0:T(8,128)(2,1)} %copy-done.29, bf16[128,192]{1,0:T(8,128)(2,1)} %copy-done.30, ...), custom_call_target="tpu_custom_call" | custom-call | tf_op jit(solution)/shard_map/route/pallas_call | solution.py:68
  94.0 3.9 %all-to-all-start = ((bf16[8,96,768]{2,1,0:T(8,128)(2,1)}), bf16[8,96,768]{2,1,0:T(8,128)(2,1)S(1)}, u32[]{:S(2)}, u32[]{:S(2)}) async-start(bf16[8,96,768]{2,1,0:T(8,128)(2,1)} %pad_maximum_fusion), calls=%async_computation | async-start | bytes 2359296 | tf_op jit(solution)/shard_map/all_to_all | solution.py:543
  97.9 1.8 collective-permute-start.18
  99.7 1.4 collective-permute-start.19
  101.5 1.7 collective-permute-start.22
  103.2 1.4 collective-permute-start.23
  104.6 17.2 %collective-permute-done.18 = bf16[96,896]{1,0:T(8,128)(2,1)S(1)} collective-permute-done((bf16[96,896]{1,0:T(8,128)(2,1)S(1)}, bf16[96,896]{1,0:T(8,128)(2,1)S(1)}, u32[]{:S(2)}, u32[]{:S(2)}) %collective-permute-start.18) | collective-permute-done | bytes 172064 | tf_op jit(solution)/shard_map/ppermute | solution.py:23
  122.0 5.2 %collective-permute-done.22 = bf16[96,768]{1,0:T(8,128)(2,1)S(1)} collective-permute-done((bf16[96,768]{1,0:T(8,128)(2,1)S(1)}, bf16[96,768]{1,0:T(8,128)(2,1)S(1)}, u32[]{:S(2)}, u32[]{:S(2)}) %collective-permute-start.22) | collective-permute-done | bytes 147488 | tf_op jit(solution)/shard_map/ppermute | solution.py:23
  127.4 2.1 collective-permute-done.24
  130.7 8.7 %expert_back.1 = (bf16[384,768]{1,0:T(8,128)(2,1)}, bf16[384,768]{1,0:T(8,128)(2,1)}, bf16[384,384]{1,0:T(8,128)(2,1)}, bf16[384,384]{1,0:T(8,128)(2,1)}, bf16[3...) custom-call(s32[2]{0:T(128)} %pad_add_fusion.ids, ...), custom_call_target="tpu_custom_call" | custom-call | tf_op jit(solution)/shard_map/expert_back/pallas_call | solution.py:68
  139.4 6.3 %expert_rest.1 = (bf16[384,768]{1,0:T(8,128)(2,1)}, bf16[384,768]{1,0:T(8,128)(2,1)}, f32[384,768]{1,0:T(8,128)}, bf16[768,768]{1,0:T(8,128)(2,1)}) custom-call(s32[2]{0:T(128)} %pad_add_fusion.ids, bf16[384,896]{1,0:T(8,128)(2,1)} %bitcast.114, bf16[384,896]{1,0:T(8,128)(2,1)} %bitcast.123, bf16[384,768]{1,0:T(8,128)(2,1)} %bitcast.116, ...), custom_call_target="tpu_custom_call" | custom-call | tf_op jit(solution)/shard_map/expert_rest/pallas_call | solution.py:68
  146.2 1.7 collective-permute-done.25
  149.2 1.5 collective-permute-start.26
  151.0 1.7 collective-permute-start.28
  152.9 3.0 %collective-permute-done.26 = bf16[96,768]{1,0:T(8,128)(2,1)S(1)} collective-permute-done((bf16[96,768]{1,0:T(8,128)(2,1)S(1)}, bf16[96,768]{1,0:T(8,128)(2,1)S(1)}, u32[]{:S(2)}, u32[]{:S(2)}) %collective-permute-start.26) | collective-permute-done | bytes 147488 | tf_op jit(solution)/shard_map/ppermute | solution.py:23
  155.9 3.6 %collective-permute-done.27 = bf16[96,768]{1,0:T(8,128)(2,1)S(1)} collective-permute-done((bf16[96,768]{1,0:T(8,128)(2,1)S(1)}, bf16[96,768]{1,0:T(8,128)(2,1)S(1)}, u32[]{:S(2)}, u32[]{:S(2)}) %collective-permute-start.27) | collective-permute-done | bytes 147488 | tf_op jit(solution)/shard_map/ppermute | solution.py:23
  160.2 3.7 %all-to-all-start.1 = ((bf16[4,24,768]{2,1,0:T(8,128)(2,1)}), bf16[4,24,768]{2,1,0:T(8,128)(2,1)S(1)}, u32[]{:S(2)}, u32[]{:S(2)}) async-start(bf16[4,24,768]{2,1,0:T(8,128)(2,1)} %bitcast.36), calls=%async_computation.1 | async-start | bytes 294912 | tf_op jit(solution)/shard_map/all_to_all | solution.py:630
  165.8 1.8 collective-permute-start.32
  167.5 2.4 all-to-all-done.1
  170.6 3.8 %all-to-all-start.2 = ((bf16[8,96,768]{2,1,0:T(8,128)(2,1)}), bf16[8,96,768]{2,1,0:T(8,128)(2,1)S(1)}, u32[]{:S(2)}, u32[]{:S(2)}) async-start(bf16[8,96,768]{2,1,0:T(8,128)(2,1)} %bitcast.61), calls=%async_computation.2 | async-start | bytes 2359296 | tf_op jit(solution)/shard_map/all_to_all | solution.py:640
  174.5 1.4 collective-permute-start.33
  177.1 1.8 collective-permute-start.35
  179.8 2.3 collective-permute-done.33.refs_1_
  182.2 7.5 %collective-permute-done.34.refs_2_ = bf16[96,768]{1,0:T(8,128)(2,1)S(1)} collective-permute-done((bf16[96,768]{1,0:T(8,128)(2,1)S(1)}, bf16[96,768]{1,0:T(8,128)(2,1)S(1)}, u32[]{:S(2)}, u32[]{:S(2)}) %collective-permute-start.34) | collective-permute-done | bytes 147488 | tf_op jit(solution)/shard_map/ppermute | solution.py:23
  190.4 9.6 %attend_back.1 = (f32[32,768]{1,0:T(8,128)}, bf16[128,192]{1,0:T(8,128)(2,1)}, bf16[4,128,384]{2,1,0:T(8,128)(2,1)}, bf16[4,128,384]{2,1,0:T(8,128)(2,1)}, bf16[768,192]{1,0:T(8,128)(2,1)}, /*index=5*/f32[8,768]{1,0:T(8,128)}) custom-call(s32[2]{0:T(128)} %pad_add_fusion.ids, bf16[96,768]{1,0:T(8,128)(2,1)} %copy-done.7, bf16[96,768]{1,0:T(8,128)(2,1)} %copy-done.19, ...), custom_call_target="tpu_custom_call" | custom-call | tf_op jit(solution)/shard_map/attend_back/pallas_call | solution.py:68
  202.3 2.1 mix.1
  204.5 1.4 reshape.130
  207.7 1.7 collective-permute-start.37
  209.4 1.5 collective-permute-start.38
  212.8 2.6 collective-permute-done.38.refs_2_
  217.1 3.4 %back_project.1 = (bf16[4,32,768]{2,1,0:T(8,128)(2,1)}, bf16[768,768]{1,0:T(8,128)(2,1)}, f32[8,768]{1,0:T(8,128)}) custom-call(s32[2]{0:T(128)} %pad_add_fusion.ids, bf16[128,384]{1,0:T(8,128)(2,1)} %get-tuple-element.150.refs_0_, bf16[128,384]{1,0:T(8,128)(2,1)} %copy-done.22, bf16[128,384]{1,0:T(8,128)(2,1)} %copy-done.23, bf16[128,384]{1,0:T(8,128)(2,1)} %copy-done.24, ...), custom_call_target="tpu_custom_call" | custom-call | tf_op jit(solution)/shard_map/back_project/pallas_call | solution.py:68
  220.4 2.7 %collective-permute-start.43 = (f32[8,768]{1,0:T(8,128)}, f32[8,768]{1,0:T(8,128)S(1)}, u32[]{:S(2)}, u32[]{:S(2)}) collective-permute-start(f32[8,768]{1,0:T(8,128)} %get-tuple-element.83), channel_id=1, source_target_pairs={{0,1},{1,0},{2,3},{3,2},{4,5},{5,4},{6,7},{7,6},{8,9},{9,8},{10,11... | collective-permute-start | bytes 73736 | tf_op jit(solution)/shard_map/ppermute | solution.py:23
  223.2 2.4 collective-permute-start.45
  225.5 1.5 dynamic-slice_bitcast_fusion
  229.1 1.4 constant_dynamic-slice_fusion.7
  232.1 2.4 collective-permute-start.42
  237.6 1.5 collective-permute-start.49
  243.1 1.9 finish.1
  245.0 1.6 reshape.132
  250.2 1.5 collective-permute-start.53
  253.1 1.8 collective-permute-done.51
  255.4 1.6 collective-permute-done.53
  (208 shorter events, 51.3 us)
Async XLA Ops:
  2.6 7.3 %collective-permute-start = (bf16[96,768]{1,0:T(8,128)(2,1)S(1)}, bf16[96,768]{1,0:T(8,128)(2,1)S(1)}, u32[]{:S(2)}, u32[]{:S(2)}) collective-permute-start(bf16[96,768]{1,0:T(8,128)(2,1)S(1)} %pad_maximum_fusion.6), channel_id=1, source_target_pairs={{0,8},{4,12},{8,0},{12,4},{16,24},{20,28},{24,16},{28,20},{1,9},{5... | collective-permute-start | bytes 442376 | tf_op jit(solution)/shard_map/ppermute | solution.py:23
  5.6 8.5 %collective-permute-start.1 = (bf16[96,768]{1,0:T(8,128)(2,1)S(1)}, bf16[96,768]{1,0:T(8,128)(2,1)S(1)}, u32[]{:S(2)}, u32[]{:S(2)}) collective-permute-start(bf16[96,768]{1,0:T(8,128)(2,1)S(1)} %pad_maximum_fusion.6), channel_id=1, source_target_pairs={{0,16},{4,20},{8,24},{12,28},{16,0},{20,4},{24,8},{28,12},{1,17},{... | collective-permute-start | bytes 442376 | tf_op jit(solution)/shard_map/ppermute | solution.py:23
  7.1 7.0 %collective-permute-start.2 = (bf16[96,768]{1,0:T(8,128)(2,1)S(1)}, bf16[96,768]{1,0:T(8,128)(2,1)S(1)}, u32[]{:S(2)}, u32[]{:S(2)}) collective-permute-start(bf16[96,768]{1,0:T(8,128)(2,1)S(1)} %pad_maximum_fusion.6), channel_id=1, source_target_pairs={{0,24},{4,28},{8,16},{12,20},{16,8},{20,12},{24,0},{28,4},{1,25},{... | collective-permute-start | bytes 442376 | tf_op jit(solution)/shard_map/ppermute | solution.py:23
  14.1 2.1 collective-permute-start.3
  15.0 16.5 %copy-start.40 = (s32[16,2,2]{0,2,1:T(2,128)S(1)}, s32[16,2,2]{0,2,1:T(2,128)}, u32[]{:S(2)}) copy-start(s32[16,2,2]{0,2,1:T(2,128)} %param.27) | copy-start | bytes 772
  15.0 16.5 %copy-start.42 = (f32[16,2,2]{0,2,1:T(2,128)S(1)}, f32[16,2,2]{0,2,1:T(2,128)}, u32[]{:S(2)}) copy-start(f32[16,2,2]{0,2,1:T(2,128)} %param.28) | copy-start | bytes 772
  17.0 32.4 %copy-start.41 = (s32[512]{0:T(512)S(1)}, s32[512]{0:T(512)}, u32[]{:S(2)}) copy-start(s32[512]{0:T(512)} %param.24) | copy-start | bytes 6148
  17.0 33.0 %copy-start.36 = (f32[32,12]{0,1:T(8,128)S(1)}, f32[32,12]{0,1:T(8,128)}, u32[]{:S(2)}) copy-start(f32[32,12]{0,1:T(8,128)} %param.23) | copy-start | bytes 4612
  17.0 33.7 %copy-start.8 = (bf16[1,96,3072]{2,1,0:T(8,128)(2,1)S(1)}, bf16[1,96,3072]{2,1,0:T(8,128)(2,1)}, u32[]{:S(2)}) copy-start(bf16[1,96,3072]{2,1,0:T(8,128)(2,1)} %param.29) | copy-start | bytes 1769476
  19.8 31.1 %copy-start.9 = (bf16[1,96,3072]{2,1,0:T(8,128)(2,1)S(1)}, bf16[1,96,3072]{2,1,0:T(8,128)(2,1)}, u32[]{:S(2)}) copy-start(bf16[1,96,3072]{2,1,0:T(8,128)(2,1)} %param.30) | copy-start | bytes 1769476
  19.8 6.7 %collective-permute-start.6 = (bf16[128,384]{1,0:T(8,128)(2,1)}, bf16[128,384]{1,0:T(8,128)(2,1)S(1)}, u32[]{:S(2)}, u32[]{:S(2)}) collective-permute-start(bf16[128,384]{1,0:T(8,128)(2,1)} %get-tuple-element.51), channel_id=1, source_target_pairs={{0,24},{4,28},{8,16},{12,20},{16,8},{20,12},{24,0},{28,4},{1,25},{... | collective-permute-start | bytes 294920 | tf_op jit(solution)/shard_map/ppermute | solution.py:23
  21.3 6.9 %collective-permute-start.4 = (bf16[128,384]{1,0:T(8,128)(2,1)}, bf16[128,384]{1,0:T(8,128)(2,1)S(1)}, u32[]{:S(2)}, u32[]{:S(2)}) collective-permute-start(bf16[128,384]{1,0:T(8,128)(2,1)} %get-tuple-element.51), channel_id=1, source_target_pairs={{0,8},{4,12},{8,0},{12,4},{16,24},{20,28},{24,16},{28,20},{1,9},{5... | collective-permute-start | bytes 294920 | tf_op jit(solution)/shard_map/ppermute | solution.py:23
  22.8 5.4 %collective-permute-start.5 = (bf16[128,384]{1,0:T(8,128)(2,1)}, bf16[128,384]{1,0:T(8,128)(2,1)S(1)}, u32[]{:S(2)}, u32[]{:S(2)}) collective-permute-start(bf16[128,384]{1,0:T(8,128)(2,1)} %get-tuple-element.51), channel_id=1, source_target_pairs={{0,16},{4,20},{8,24},{12,28},{16,0},{20,4},{24,8},{28,12},{1,17},{... | collective-permute-start | bytes 294920 | tf_op jit(solution)/shard_map/ppermute | solution.py:23
  29.1 21.8 %copy-start.5 = (bf16[4,128,384]{2,1,0:T(8,128)(2,1)}, bf16[4,128,384]{2,1,0:T(8,128)(2,1)S(1)}, u32[]{:S(2)}) copy-start(bf16[4,128,384]{2,1,0:T(8,128)(2,1)S(1)} %pad_maximum_fusion.5.near) | copy-start | bytes 1179652
  29.2 17.3 %collective-permute-start.7 = (bf16[4,128,384]{2,1,0:T(8,128)(2,1)S(1)}, bf16[4,128,384]{2,1,0:T(8,128)(2,1)S(1)}, u32[]{:S(2)}, u32[]{:S(2)}) collective-permute-start(bf16[4,128,384]{2,1,0:T(8,128)(2,1)S(1)} %pad_maximum_fusion.5.near), channel_id=1, source_target_pairs={{0,4},{4,0},{8,12},{12,8},{16,20},{20,16},{24,28},{28,24},{1,5},{5... | collective-permute-start | bytes 1179656 | tf_op jit(solution)/shard_map/ppermute | solution.py:23
  29.2 29.0 %collective-permute-start.11 = (bf16[768,192]{1,0:T(8,128)(2,1)}, bf16[768,192]{1,0:T(8,128)(2,1)S(1)}, u32[]{:S(2)}, u32[]{:S(2)}) collective-permute-start(bf16[768,192]{1,0:T(8,128)(2,1)} %get-tuple-element.53.refs_5_.refs_10_), channel_id=1, source_target_pairs={{0,1},{1,0},{2,3},{3,2},{4,5},{5,4},{6,7},{7,6},{8,9},{9,8},{10,11... | collective-permute-start | bytes 884744 | tf_op jit(solution)/shard_map/ppermute | solution.py:23
  33.8 10.4 %collective-permute-start.14 = (bf16[48,768]{1,0:T(8,128)(2,1)}, bf16[48,768]{1,0:T(8,128)(2,1)S(1)}, u32[]{:S(2)}, u32[]{:S(2)}) collective-permute-start(bf16[48,768]{1,0:T(8,128)(2,1)} %pack.1.refs_0_), channel_id=1, source_target_pairs={{0,1},{1,0},{2,3},{3,2},{4,5},{5,4},{6,7},{7,6},{8,9},{9,8},{10,11... | collective-permute-start | bytes 221192 | tf_op jit(solution)/shard_map/ppermute | solution.py:23
  34.2 21.5 %collective-permute-start.15 = (bf16[48,768]{1,0:T(8,128)(2,1)}, bf16[48,768]{1,0:T(8,128)(2,1)S(1)}, u32[]{:S(2)}, u32[]{:S(2)}) collective-permute-start(bf16[48,768]{1,0:T(8,128)(2,1)} %pack.1.refs_0_), channel_id=1, source_target_pairs={{0,2},{1,3},{2,0},{3,1},{4,6},{5,7},{6,4},{7,5},{8,10},{9,11},{10,... | collective-permute-start | bytes 221192 | tf_op jit(solution)/shard_map/ppermute | solution.py:23
  36.8 19.8 %collective-permute-start.16 = (bf16[48,768]{1,0:T(8,128)(2,1)}, bf16[48,768]{1,0:T(8,128)(2,1)S(1)}, u32[]{:S(2)}, u32[]{:S(2)}) collective-permute-start(bf16[48,768]{1,0:T(8,128)(2,1)} %pack.1.refs_0_), channel_id=1, source_target_pairs={{0,3},{1,2},{2,1},{3,0},{4,7},{5,6},{6,5},{7,4},{8,11},{9,10},{10,... | collective-permute-start | bytes 221192 | tf_op jit(solution)/shard_map/ppermute | solution.py:23
  44.1 32.8 %collective-permute-start.12 = (bf16[768,192]{1,0:T(8,128)(2,1)}, bf16[768,192]{1,0:T(8,128)(2,1)S(1)}, u32[]{:S(2)}, u32[]{:S(2)}) collective-permute-start(bf16[768,192]{1,0:T(8,128)(2,1)} %get-tuple-element.53.refs_5_.refs_10_), channel_id=1, source_target_pairs={{0,2},{1,3},{2,0},{3,1},{4,6},{5,7},{6,4},{7,5},{8,10},{9,11},{10,... | collective-permute-start | bytes 884744 | tf_op jit(solution)/shard_map/ppermute | solution.py:23
  46.4 30.5 %collective-permute-start.13 = (bf16[768,192]{1,0:T(8,128)(2,1)}, bf16[768,192]{1,0:T(8,128)(2,1)S(1)}, u32[]{:S(2)}, u32[]{:S(2)}) collective-permute-start(bf16[768,192]{1,0:T(8,128)(2,1)} %get-tuple-element.53.refs_5_.refs_10_), channel_id=1, source_target_pairs={{0,3},{1,2},{2,1},{3,0},{4,7},{5,6},{6,5},{7,4},{8,11},{9,10},{10,... | collective-permute-start | bytes 884744 | tf_op jit(solution)/shard_map/ppermute | solution.py:23
  55.7 21.2 %collective-permute-start.10 = (bf16[128,192]{1,0:T(8,128)(2,1)}, bf16[128,192]{1,0:T(8,128)(2,1)S(1)}, u32[]{:S(2)}, u32[]{:S(2)}) collective-permute-start(bf16[128,192]{1,0:T(8,128)(2,1)} %get-tuple-element.52.refs_1_.refs_8_), channel_id=1, source_target_pairs={{0,3},{1,2},{2,1},{3,0},{4,7},{5,6},{6,5},{7,4},{8,11},{9,10},{10,... | collective-permute-start | bytes 147464 | tf_op jit(solution)/shard_map/ppermute | solution.py:23
  56.6 20.4 %collective-permute-start.8 = (bf16[128,192]{1,0:T(8,128)(2,1)}, bf16[128,192]{1,0:T(8,128)(2,1)S(1)}, u32[]{:S(2)}, u32[]{:S(2)}) collective-permute-start(bf16[128,192]{1,0:T(8,128)(2,1)} %get-tuple-element.52.refs_1_.refs_8_), channel_id=1, source_target_pairs={{0,1},{1,0},{2,3},{3,2},{4,5},{5,4},{6,7},{7,6},{8,9},{9,8},{10,11... | collective-permute-start | bytes 147464 | tf_op jit(solution)/shard_map/ppermute | solution.py:23
  58.3 28.8 %collective-permute-start.9 = (bf16[128,192]{1,0:T(8,128)(2,1)}, bf16[128,192]{1,0:T(8,128)(2,1)S(1)}, u32[]{:S(2)}, u32[]{:S(2)}) collective-permute-start(bf16[128,192]{1,0:T(8,128)(2,1)} %get-tuple-element.52.refs_1_.refs_8_), channel_id=1, source_target_pairs={{0,2},{1,3},{2,0},{3,1},{4,6},{5,7},{6,4},{7,5},{8,10},{9,11},{10,... | collective-permute-start | bytes 147464 | tf_op jit(solution)/shard_map/ppermute | solution.py:23
  91.7 11.4 %collective-permute-start.17 = (bf16[96,896]{1,0:T(8,128)(2,1)}, bf16[96,896]{1,0:T(8,128)(2,1)S(1)}, u32[]{:S(2)}, u32[]{:S(2)}) collective-permute-start(bf16[96,896]{1,0:T(8,128)(2,1)} %get-tuple-element.57), channel_id=1, source_target_pairs={{0,8},{4,12},{8,0},{12,4},{16,24},{20,28},{24,16},{28,20},{1,9},{5... | collective-permute-start | bytes 516104 | tf_op jit(solution)/shard_map/ppermute | solution.py:23
  94.0 35.5 %all-to-all-start = ((bf16[8,96,768]{2,1,0:T(8,128)(2,1)}), bf16[8,96,768]{2,1,0:T(8,128)(2,1)S(1)}, u32[]{:S(2)}, u32[]{:S(2)}) async-start(bf16[8,96,768]{2,1,0:T(8,128)(2,1)} %pad_maximum_fusion), calls=%async_computation | async-start | bytes 2359296 | tf_op jit(solution)/shard_map/all_to_all | solution.py:543
  97.9 23.9 %collective-permute-start.18 = (bf16[96,896]{1,0:T(8,128)(2,1)S(1)}, bf16[96,896]{1,0:T(8,128)(2,1)S(1)}, u32[]{:S(2)}, u32[]{:S(2)}) collective-permute-start(bf16[96,896]{1,0:T(8,128)(2,1)S(1)} %copy-done.17), channel_id=1, source_target_pairs={{0,16},{4,20},{8,24},{12,28},{16,0},{20,4},{24,8},{28,12},{1,17},{... | collective-permute-start | bytes 516104 | tf_op jit(solution)/shard_map/ppermute | solution.py:23
  99.7 22.2 %collective-permute-start.19 = (bf16[96,896]{1,0:T(8,128)(2,1)S(1)}, bf16[96,896]{1,0:T(8,128)(2,1)S(1)}, u32[]{:S(2)}, u32[]{:S(2)}) collective-permute-start(bf16[96,896]{1,0:T(8,128)(2,1)S(1)} %copy-done.17), channel_id=1, source_target_pairs={{0,24},{4,28},{8,16},{12,20},{16,8},{20,12},{24,0},{28,4},{1,25},{... | collective-permute-start | bytes 516104 | tf_op jit(solution)/shard_map/ppermute | solution.py:23
  101.1 20.9 %collective-permute-start.21 = (bf16[96,768]{1,0:T(8,128)(2,1)S(1)}, bf16[96,768]{1,0:T(8,128)(2,1)S(1)}, u32[]{:S(2)}, u32[]{:S(2)}) collective-permute-start(bf16[96,768]{1,0:T(8,128)(2,1)S(1)} %copy-done.18), channel_id=1, source_target_pairs={{0,8},{4,12},{8,0},{12,4},{16,24},{20,28},{24,16},{28,20},{1,9},{5... | collective-permute-start | bytes 442376 | tf_op jit(solution)/shard_map/ppermute | solution.py:23
  101.5 25.7 %collective-permute-start.22 = (bf16[96,768]{1,0:T(8,128)(2,1)S(1)}, bf16[96,768]{1,0:T(8,128)(2,1)S(1)}, u32[]{:S(2)}, u32[]{:S(2)}) collective-permute-start(bf16[96,768]{1,0:T(8,128)(2,1)S(1)} %copy-done.18), channel_id=1, source_target_pairs={{0,16},{4,20},{8,24},{12,28},{16,0},{20,4},{24,8},{28,12},{1,17},{... | collective-permute-start | bytes 442376 | tf_op jit(solution)/shard_map/ppermute | solution.py:23
  103.2 24.0 %collective-permute-start.23 = (bf16[96,768]{1,0:T(8,128)(2,1)S(1)}, bf16[96,768]{1,0:T(8,128)(2,1)S(1)}, u32[]{:S(2)}, u32[]{:S(2)}) collective-permute-start(bf16[96,768]{1,0:T(8,128)(2,1)S(1)} %copy-done.18), channel_id=1, source_target_pairs={{0,24},{4,28},{8,16},{12,20},{16,8},{20,12},{24,0},{28,4},{1,25},{... | collective-permute-start | bytes 442376 | tf_op jit(solution)/shard_map/ppermute | solution.py:23
  121.9 7.6 %collective-permute-start.20 = (bf16[4,96,896]{2,1,0:T(8,128)(2,1)S(1)}, bf16[4,96,896]{2,1,0:T(8,128)(2,1)S(1)}, u32[]{:S(2)}, u32[]{:S(2)}) collective-permute-start(bf16[4,96,896]{2,1,0:T(8,128)(2,1)S(1)} %pad_maximum_fusion.1), channel_id=1, source_target_pairs={{0,4},{4,0},{8,12},{12,8},{16,20},{20,16},{24,28},{28,24},{1,5},{5... | collective-permute-start | bytes 2064392 | tf_op jit(solution)/shard_map/ppermute | solution.py:23
  127.3 2.2 collective-permute-start.24
  145.7 2.2 collective-permute-start.25
  145.8 6.9 %collective-permute-start.29 = (bf16[4,96,768]{2,1,0:T(8,128)(2,1)S(1)}, bf16[4,96,768]{2,1,0:T(8,128)(2,1)S(1)}, u32[]{:S(2)}, u32[]{:S(2)}) collective-permute-start(bf16[4,96,768]{2,1,0:T(8,128)(2,1)S(1)} %bitcast.160), channel_id=1, source_target_pairs={{0,4},{4,0},{8,12},{12,8},{16,20},{20,16},{24,28},{28,24},{1,5},{5... | collective-permute-start | bytes 1769480 | tf_op jit(solution)/shard_map/ppermute | solution.py:23
  149.2 6.7 %collective-permute-start.26 = (bf16[96,768]{1,0:T(8,128)(2,1)S(1)}, bf16[96,768]{1,0:T(8,128)(2,1)S(1)}, u32[]{:S(2)}, u32[]{:S(2)}) collective-permute-start(bf16[96,768]{1,0:T(8,128)(2,1)S(1)} %get-tuple-element.144), channel_id=1, source_target_pairs={{0,8},{4,12},{8,0},{12,4},{16,24},{20,28},{24,16},{28,20},{1,9},{5... | collective-permute-start | bytes 442376 | tf_op jit(solution)/shard_map/ppermute | solution.py:23
  150.7 8.8 %collective-permute-start.27 = (bf16[96,768]{1,0:T(8,128)(2,1)S(1)}, bf16[96,768]{1,0:T(8,128)(2,1)S(1)}, u32[]{:S(2)}, u32[]{:S(2)}) collective-permute-start(bf16[96,768]{1,0:T(8,128)(2,1)S(1)} %get-tuple-element.146), channel_id=1, source_target_pairs={{0,16},{4,20},{8,24},{12,28},{16,0},{20,4},{24,8},{28,12},{1,17},{... | collective-permute-start | bytes 442376 | tf_op jit(solution)/shard_map/ppermute | solution.py:23
  151.0 8.4 %collective-permute-start.28 = (bf16[96,768]{1,0:T(8,128)(2,1)S(1)}, bf16[96,768]{1,0:T(8,128)(2,1)S(1)}, u32[]{:S(2)}, u32[]{:S(2)}) collective-permute-start(bf16[96,768]{1,0:T(8,128)(2,1)S(1)} %get-tuple-element.145), channel_id=1, source_target_pairs={{0,24},{4,28},{8,16},{12,20},{16,8},{20,12},{24,0},{28,4},{1,25},{... | collective-permute-start | bytes 442376 | tf_op jit(solution)/shard_map/ppermute | solution.py:23
  160.2 9.7 %all-to-all-start.1 = ((bf16[4,24,768]{2,1,0:T(8,128)(2,1)}), bf16[4,24,768]{2,1,0:T(8,128)(2,1)S(1)}, u32[]{:S(2)}, u32[]{:S(2)}) async-start(bf16[4,24,768]{2,1,0:T(8,128)(2,1)} %bitcast.36), calls=%async_computation.1 | async-start | bytes 294912 | tf_op jit(solution)/shard_map/all_to_all | solution.py:630
  164.0 10.4 %collective-permute-start.30 = (bf16[96,768]{1,0:T(8,128)(2,1)S(1)}, bf16[96,768]{1,0:T(8,128)(2,1)S(1)}, u32[]{:S(2)}, u32[]{:S(2)}) collective-permute-start(bf16[96,768]{1,0:T(8,128)(2,1)S(1)} %get-tuple-element.141), channel_id=1, source_target_pairs={{0,8},{4,12},{8,0},{12,4},{16,24},{20,28},{24,16},{28,20},{1,9},{5... | collective-permute-start | bytes 442376 | tf_op jit(solution)/shard_map/ppermute | solution.py:23
  164.6 9.8 %collective-permute-start.31 = (bf16[96,768]{1,0:T(8,128)(2,1)S(1)}, bf16[96,768]{1,0:T(8,128)(2,1)S(1)}, u32[]{:S(2)}, u32[]{:S(2)}) collective-permute-start(bf16[96,768]{1,0:T(8,128)(2,1)S(1)} %get-tuple-element.143), channel_id=1, source_target_pairs={{0,16},{4,20},{8,24},{12,28},{16,0},{20,4},{24,8},{28,12},{1,17},{... | collective-permute-start | bytes 442376 | tf_op jit(solution)/shard_map/ppermute | solution.py:23
  165.8 8.6 %collective-permute-start.32 = (bf16[96,768]{1,0:T(8,128)(2,1)S(1)}, bf16[96,768]{1,0:T(8,128)(2,1)S(1)}, u32[]{:S(2)}, u32[]{:S(2)}) collective-permute-start(bf16[96,768]{1,0:T(8,128)(2,1)S(1)} %get-tuple-element.142), channel_id=1, source_target_pairs={{0,24},{4,28},{8,16},{12,20},{16,8},{20,12},{24,0},{28,4},{1,25},{... | collective-permute-start | bytes 442376 | tf_op jit(solution)/shard_map/ppermute | solution.py:23
  170.6 40.6 %all-to-all-start.2 = ((bf16[8,96,768]{2,1,0:T(8,128)(2,1)}), bf16[8,96,768]{2,1,0:T(8,128)(2,1)S(1)}, u32[]{:S(2)}, u32[]{:S(2)}) async-start(bf16[8,96,768]{2,1,0:T(8,128)(2,1)} %bitcast.61), calls=%async_computation.2 | async-start | bytes 2359296 | tf_op jit(solution)/shard_map/all_to_all | solution.py:640
  174.5 7.7 %collective-permute-start.33 = (bf16[96,768]{1,0:T(8,128)(2,1)S(1)}, bf16[96,768]{1,0:T(8,128)(2,1)S(1)}, u32[]{:S(2)}, u32[]{:S(2)}) collective-permute-start(bf16[96,768]{1,0:T(8,128)(2,1)S(1)} %fusion.6.refs_0_), channel_id=1, source_target_pairs={{0,1},{1,0},{2,3},{3,2},{4,5},{5,4},{6,7},{7,6},{8,9},{9,8},{10,11... | collective-permute-start | bytes 442376 | tf_op jit(solution)/shard_map/ppermute | solution.py:23
  175.9 13.8 %collective-permute-start.34 = (bf16[96,768]{1,0:T(8,128)(2,1)S(1)}, bf16[96,768]{1,0:T(8,128)(2,1)S(1)}, u32[]{:S(2)}, u32[]{:S(2)}) collective-permute-start(bf16[96,768]{1,0:T(8,128)(2,1)S(1)} %fusion.6.refs_0_), channel_id=1, source_target_pairs={{0,2},{1,3},{2,0},{3,1},{4,6},{5,7},{6,4},{7,5},{8,10},{9,11},{10,... | collective-permute-start | bytes 442376 | tf_op jit(solution)/shard_map/ppermute | solution.py:23
  177.1 12.6 %collective-permute-start.35 = (bf16[96,768]{1,0:T(8,128)(2,1)S(1)}, bf16[96,768]{1,0:T(8,128)(2,1)S(1)}, u32[]{:S(2)}, u32[]{:S(2)}) collective-permute-start(bf16[96,768]{1,0:T(8,128)(2,1)S(1)} %fusion.6.refs_0_), channel_id=1, source_target_pairs={{0,3},{1,2},{2,1},{3,0},{4,7},{5,6},{6,5},{7,4},{8,11},{9,10},{10,... | collective-permute-start | bytes 442376 | tf_op jit(solution)/shard_map/ppermute | solution.py:23
  199.9 6.0 %collective-permute-start.36 = (bf16[4,128,384]{2,1,0:T(8,128)(2,1)}, bf16[4,128,384]{2,1,0:T(8,128)(2,1)S(1)}, u32[]{:S(2)}, u32[]{:S(2)}) collective-permute-start(bf16[4,128,384]{2,1,0:T(8,128)(2,1)} %get-tuple-element.75), channel_id=1, source_target_pairs={{0,4},{4,0},{8,12},{12,8},{16,20},{20,16},{24,28},{28,24},{1,5},{5... | collective-permute-start | bytes 1179656 | tf_op jit(solution)/shard_map/ppermute | solution.py:23
  207.7 5.1 %collective-permute-start.37 = (bf16[128,384]{1,0:T(8,128)(2,1)S(1)}, bf16[128,384]{1,0:T(8,128)(2,1)S(1)}, u32[]{:S(2)}, u32[]{:S(2)}) collective-permute-start(bf16[128,384]{1,0:T(8,128)(2,1)S(1)} %get-tuple-element.149), channel_id=1, source_target_pairs={{0,8},{4,12},{8,0},{12,4},{16,24},{20,28},{24,16},{28,20},{1,9},{5... | collective-permute-start | bytes 294920 | tf_op jit(solution)/shard_map/ppermute | solution.py:23
  209.4 5.9 %collective-permute-start.38 = (bf16[128,384]{1,0:T(8,128)(2,1)S(1)}, bf16[128,384]{1,0:T(8,128)(2,1)S(1)}, u32[]{:S(2)}, u32[]{:S(2)}) collective-permute-start(bf16[128,384]{1,0:T(8,128)(2,1)S(1)} %get-tuple-element.148), channel_id=1, source_target_pairs={{0,16},{4,20},{8,24},{12,28},{16,0},{20,4},{24,8},{28,12},{1,17},{... | collective-permute-start | bytes 294920 | tf_op jit(solution)/shard_map/ppermute | solution.py:23
  210.9 5.5 %collective-permute-start.39 = (bf16[128,384]{1,0:T(8,128)(2,1)S(1)}, bf16[128,384]{1,0:T(8,128)(2,1)S(1)}, u32[]{:S(2)}, u32[]{:S(2)}) collective-permute-start(bf16[128,384]{1,0:T(8,128)(2,1)S(1)} %get-tuple-element.147), channel_id=1, source_target_pairs={{0,24},{4,28},{8,16},{12,20},{16,8},{20,12},{24,0},{28,4},{1,25},{... | collective-permute-start | bytes 294920 | tf_op jit(solution)/shard_map/ppermute | solution.py:23
  220.4 10.1 %collective-permute-start.43 = (f32[8,768]{1,0:T(8,128)}, f32[8,768]{1,0:T(8,128)S(1)}, u32[]{:S(2)}, u32[]{:S(2)}) collective-permute-start(f32[8,768]{1,0:T(8,128)} %get-tuple-element.83), channel_id=1, source_target_pairs={{0,1},{1,0},{2,3},{3,2},{4,5},{5,4},{6,7},{7,6},{8,9},{9,8},{10,11... | collective-permute-start | bytes 73736 | tf_op jit(solution)/shard_map/ppermute | solution.py:23
  223.2 7.3 %collective-permute-start.44 = (f32[8,768]{1,0:T(8,128)}, f32[8,768]{1,0:T(8,128)S(1)}, u32[]{:S(2)}, u32[]{:S(2)}) collective-permute-start(f32[8,768]{1,0:T(8,128)} %get-tuple-element.83), channel_id=1, source_target_pairs={{0,2},{1,3},{2,0},{3,1},{4,6},{5,7},{6,4},{7,5},{8,10},{9,11},{10,... | collective-permute-start | bytes 73736 | tf_op jit(solution)/shard_map/ppermute | solution.py:23
  223.2 7.4 %collective-permute-start.45 = (f32[8,768]{1,0:T(8,128)}, f32[8,768]{1,0:T(8,128)S(1)}, u32[]{:S(2)}, u32[]{:S(2)}) collective-permute-start(f32[8,768]{1,0:T(8,128)} %get-tuple-element.83), channel_id=1, source_target_pairs={{0,3},{1,2},{2,1},{3,0},{4,7},{5,6},{6,5},{7,4},{8,11},{9,10},{10,... | collective-permute-start | bytes 73736 | tf_op jit(solution)/shard_map/ppermute | solution.py:23
  227.1 9.1 %collective-permute-start.40 = (bf16[32,768]{1,0:T(8,128)(2,1)S(1)}, bf16[32,768]{1,0:T(8,128)(2,1)S(1)}, u32[]{:S(2)}, u32[]{:S(2)}) collective-permute-start(bf16[32,768]{1,0:T(8,128)(2,1)S(1)} %get-tuple-element.157), channel_id=1, source_target_pairs={{0,1},{1,0},{2,3},{3,2},{4,5},{5,4},{6,7},{7,6},{8,9},{9,8},{10,11... | collective-permute-start | bytes 147464 | tf_op jit(solution)/shard_map/ppermute | solution.py:23
  228.2 8.8 %collective-permute-start.41 = (bf16[32,768]{1,0:T(8,128)(2,1)S(1)}, bf16[32,768]{1,0:T(8,128)(2,1)S(1)}, u32[]{:S(2)}, u32[]{:S(2)}) collective-permute-start(bf16[32,768]{1,0:T(8,128)(2,1)S(1)} %get-tuple-element.156), channel_id=1, source_target_pairs={{0,2},{1,3},{2,0},{3,1},{4,6},{5,7},{6,4},{7,5},{8,10},{9,11},{10,... | collective-permute-start | bytes 147464 | tf_op jit(solution)/shard_map/ppermute | solution.py:23
  230.6 3.9 %collective-permute-start.46 = (f32[8,768]{1,0:T(8,128)S(1)}, f32[8,768]{1,0:T(8,128)S(1)}, u32[]{:S(2)}, u32[]{:S(2)}) collective-permute-start(f32[8,768]{1,0:T(8,128)S(1)} %add_add_fusion.1), channel_id=1, source_target_pairs={{0,4},{4,0},{8,12},{12,8},{16,20},{20,16},{24,28},{28,24},{1,5},{5... | collective-permute-start | bytes 73736 | tf_op jit(solution)/shard_map/ppermute | solution.py:23
  231.6 16.5 %collective-permute-start.50 = (bf16[4,96,768]{2,1,0:T(8,128)(2,1)}, bf16[4,96,768]{2,1,0:T(8,128)(2,1)S(1)}, u32[]{:S(2)}, u32[]{:S(2)}) collective-permute-start(bf16[4,96,768]{2,1,0:T(8,128)(2,1)} %pad_maximum_fusion.4), channel_id=1, source_target_pairs={{0,4},{4,0},{8,12},{12,8},{16,20},{20,16},{24,28},{28,24},{1,5},{5... | collective-permute-start | bytes 1769480 | tf_op jit(solution)/shard_map/ppermute | solution.py:23
  232.1 11.0 %collective-permute-start.42 = (bf16[32,768]{1,0:T(8,128)(2,1)}, bf16[32,768]{1,0:T(8,128)(2,1)}, u32[]{:S(2)}, u32[]{:S(2)}) collective-permute-start(bf16[32,768]{1,0:T(8,128)(2,1)} %get-tuple-element.155), channel_id=1, source_target_pairs={{0,3},{1,2},{2,1},{3,0},{4,7},{5,6},{6,5},{7,4},{8,11},{9,10},{10,... | collective-permute-start | bytes 147464 | tf_op jit(solution)/shard_map/ppermute | solution.py:23
  235.0 11.6 %collective-permute-start.47 = (f32[8,768]{1,0:T(8,128)}, f32[8,768]{1,0:T(8,128)}, u32[]{:S(2)}, u32[]{:S(2)}) collective-permute-start(f32[8,768]{1,0:T(8,128)} %add.114), channel_id=1, source_target_pairs={{0,8},{4,12},{8,0},{12,4},{16,24},{20,28},{24,16},{28,20},{1,9},{5... | collective-permute-start | bytes 73736 | tf_op jit(solution)/shard_map/ppermute | solution.py:23
  236.1 10.5 %collective-permute-start.48 = (f32[8,768]{1,0:T(8,128)}, f32[8,768]{1,0:T(8,128)}, u32[]{:S(2)}, u32[]{:S(2)}) collective-permute-start(f32[8,768]{1,0:T(8,128)} %add.114), channel_id=1, source_target_pairs={{0,16},{4,20},{8,24},{12,28},{16,0},{20,4},{24,8},{28,12},{1,17},{... | collective-permute-start | bytes 73736 | tf_op jit(solution)/shard_map/ppermute | solution.py:23
  237.6 9.0 %collective-permute-start.49 = (f32[8,768]{1,0:T(8,128)}, f32[8,768]{1,0:T(8,128)}, u32[]{:S(2)}, u32[]{:S(2)}) collective-permute-start(f32[8,768]{1,0:T(8,128)} %add.114), channel_id=1, source_target_pairs={{0,24},{4,28},{8,16},{12,20},{16,8},{20,12},{24,0},{28,4},{1,25},{... | collective-permute-start | bytes 73736 | tf_op jit(solution)/shard_map/ppermute | solution.py:23
  248.2 6.7 %collective-permute-start.51 = (bf16[96,768]{1,0:T(8,128)(2,1)S(1)}, bf16[96,768]{1,0:T(8,128)(2,1)S(1)}, u32[]{:S(2)}, u32[]{:S(2)}) collective-permute-start(bf16[96,768]{1,0:T(8,128)(2,1)S(1)} %get-tuple-element.138), channel_id=1, source_target_pairs={{0,8},{4,12},{8,0},{12,4},{16,24},{20,28},{24,16},{28,20},{1,9},{5... | collective-permute-start | bytes 442376 | tf_op jit(solution)/shard_map/ppermute | solution.py:23
  249.3 6.1 %collective-permute-start.52 = (bf16[96,768]{1,0:T(8,128)(2,1)S(1)}, bf16[96,768]{1,0:T(8,128)(2,1)S(1)}, u32[]{:S(2)}, u32[]{:S(2)}) collective-permute-start(bf16[96,768]{1,0:T(8,128)(2,1)S(1)} %get-tuple-element.140), channel_id=1, source_target_pairs={{0,16},{4,20},{8,24},{12,28},{16,0},{20,4},{24,8},{28,12},{1,17},{... | collective-permute-start | bytes 442376 | tf_op jit(solution)/shard_map/ppermute | solution.py:23
  250.2 6.8 %collective-permute-start.53 = (bf16[96,768]{1,0:T(8,128)(2,1)S(1)}, bf16[96,768]{1,0:T(8,128)(2,1)S(1)}, u32[]{:S(2)}, u32[]{:S(2)}) collective-permute-start(bf16[96,768]{1,0:T(8,128)(2,1)S(1)} %get-tuple-element.139), channel_id=1, source_target_pairs={{0,24},{4,28},{8,16},{12,20},{16,8},{20,12},{24,0},{28,4},{1,25},{... | collective-permute-start | bytes 442376 | tf_op jit(solution)/shard_map/ppermute | solution.py:23
  (37 other events, 196.8 us)

commit v2 on v1

v2 whole, which is shorter than its diff:
```python
import functools

import jax
import jax.numpy as jnp
from jax import lax
from jax.experimental import pallas as pl
from jax.experimental.pallas import tpu as pltpu
from jax.sharding import PartitionSpec as P

HD = 64
EPS = 1e-06
FLOOR = -1e30
HIGH = lax.Precision.HIGHEST
F32 = jnp.float32
BF16 = jnp.bfloat16
LANES = 128
GELU_C = 0.7978845608028654
GELU_A = 0.044715


def swap(value, axis, bits):
    devices = lax.axis_size(axis)
    return lax.ppermute(value, axis, [(i, i ^ bits) for i in range(devices)])


def gather_ctx(value, after=()):
    devices = lax.axis_size("ctx")
    near = [value[None]] + [swap(value, "ctx", 2 * j)[None] for j in range(1, devices // 2)]
    if after:
        near = [hold(block, *after) for block in near]
    if devices > 8:
        near = [jnp.concatenate(near, axis=0)]
    return near + [swap(block, "ctx", 1) for block in near]


def each_block(refs):
    half = sum(ref.shape[0] for ref in refs) // 2
    listed = [(ref, i) for ref in refs for i in range(ref.shape[0])]
    return [(ref, i, 2 * (t % half) + t // half) for t, (ref, i) in enumerate(listed)]


def grouped(refs):
    listed = [(ref, i) for ref in refs for i in range(ref.shape[0])]
    return [listed[t : t + 4] for t in range(0, len(listed), 4)]


def stack(group, rows=slice(None), cols=slice(None)):
    return jnp.concatenate([ref[i, rows, cols] for ref, i in group], axis=0)


def trade_exp(value):
    return lax.all_to_all(value, "exp", split_axis=0, concat_axis=0, tiled=True)


def spread_exp(value):
    return [value] + [swap(value, "exp", d) for d in range(1, lax.axis_size("exp"))]


def nn(left, right, precision=None):
    return lax.dot_general(
        left, right, (((1,), (0,)), ((), ())), precision=precision, preferred_element_type=F32
    )


def nt(left, right, precision=None):
    return lax.dot_general(
        left, right, (((1,), (1,)), ((), ())), precision=precision, preferred_element_type=F32
    )


def tn(left, right, precision=None):
    return lax.dot_general(
        left, right, (((0,), (0,)), ((), ())), precision=precision, preferred_element_type=F32
    )


def room(shape, dtype):
    *lead, rows, cols = (1, 1, *shape)
    size = jnp.dtype(dtype).itemsize
    tile = 32 // size
    total = -(-rows // tile) * tile * -(-cols // LANES) * LANES * size
    for extent in lead:
        total *= extent
    return total


def call(body, name, outs, *args, us=2.0, scratch=(), after=(), wide=False, token=False):
    single = not isinstance(outs, list)
    outs = ([outs] if single else outs) + ([((8, LANES), F32)] if token else [])
    single = len(outs) == 1
    specs = [pl.BlockSpec(memory_space=pltpu.VMEM)] * len(args)
    specs += [
        pl.BlockSpec(memory_space=pltpu.VMEM if room(a.shape, a.dtype) <= 2**16 else pl.ANY)
        for a in after
    ]
    shapes = [jax.ShapeDtypeStruct(*o) for o in outs]
    out_specs = [pl.BlockSpec(memory_space=pltpu.VMEM)] * len(shapes)

    held = sum(room(a.shape, a.dtype) for a in (*args, *shapes))
    held += sum(room(a.shape, a.dtype) for a in scratch)
    limit = min(62 * 2**20, max(16 * 2**20 + 2 * held, 60 * 2**20 if wide else 0))

    def run(*refs):
        rest = refs[len(args) + len(after) :]
        if token:
            place = len(shapes) - 1
            rest[place][...] = jnp.zeros(rest[place].shape, F32)
            rest = rest[:place] + rest[place + 1 :]
        body(*refs[: len(args)], *rest)

    return pl.pallas_call(
        run,
        out_shape=shapes[0] if single else shapes,
        in_specs=specs,
        out_specs=out_specs[0] if single else out_specs,
        scratch_shapes=list(scratch),
        compiler_params=pltpu.CompilerParams(vmem_limit_bytes=limit),
        cost_estimate=pl.CostEstimate(flops=0, bytes_accessed=int(us * 3.0e4), transcendentals=0),
        name=name,
    )(*args, *after)


def hold(value, *after):
    return pl.pallas_call(
        lambda *refs: None,
        out_shape=jax.ShapeDtypeStruct(value.shape, value.dtype),
        in_specs=[pl.BlockSpec(memory_space=pl.ANY)] * (1 + len(after)),
        out_specs=pl.BlockSpec(memory_space=pl.ANY),
        input_output_aliases={0: 0},
        name="hold",
    )(value, *after)


def back_sum_body(cap, *refs):
    terms, out = refs[:-1], refs[-1]
    width = out.shape[2]
    total = terms[0][...].astype(F32)
    for ref in terms[1:]:
        total = total + ref[...].astype(F32)
    for z in range(out.shape[0]):
        y = total[z * cap : (z + 1) * cap, width:]
        out[z] = jnp.concatenate([total[:, :width], y], axis=0).astype(BF16)


def add_pair(near, far):
    got = swap(far, "ctx", 1)
    return [
        (near[j].astype(F32) + got[j].astype(F32)).astype(BF16) for j in range(near.shape[0])
    ]


def send_direct(both):
    return [both[0]] + [swap(block, "ctx", 2 * j) for j, block in enumerate(both) if j > 0]


def rms_scale(values):
    return lax.rsqrt(jnp.mean(values * values, axis=-1, keepdims=True) + EPS)


def iota(shape, axis):
    return lax.broadcasted_iota(jnp.int32, shape, axis)


def block_before(rows, tok, quarter):
    early, late = iota((rows, rows), 0), iota((rows, rows), 1)
    same = (early % tok) // quarter == (late % tok) // quarter
    return jnp.where(same & (early < late), 1.0, 0.0).astype(BF16)


def slot_hot(route0, route1, expert, before, tok, quarter, cap, parts):
    rows = route0.shape[1]
    named = (route0 == expert) | (route1 == expert)
    flags = jnp.broadcast_to(jnp.where(named, 1.0, 0.0), (16, rows)).astype(BF16)
    rank = nn(flags, before)[0:1].astype(jnp.int32)
    block = (iota((1, rows), 1) % tok) // quarter
    place = jnp.where(named, block * cap + rank, -1)
    return iota((parts * cap, rows), 0) == place, named


def pack_body(folded, wo, cot, info, x, *refs):
    weights, (out, message) = refs[:-2], refs[-2:]
    quarter, shard = cot.shape[0], wo.shape[1]
    width = cot.shape[2]
    tok = x.shape[0]
    wide = x[...].astype(F32)
    for s in range(2):
        message[s * tok : (s + 1) * tok, :] = wide[:, s, :].astype(BF16)
    if folded:
        rest = shard - folded
        cols = 3 * wo.shape[0]
        side = jnp.concatenate([w[folded:, :] for w in weights], axis=0)
        side = jnp.concatenate(
            [side, jnp.zeros((folded - 3 * rest, side.shape[1]), BF16)], axis=0
        )
        message[2 * tok :, :] = jnp.concatenate([w[:folded, :] for w in weights] + [side], axis=1)
    third = width // 3
    rows = 2 * quarter
    out[...] = jnp.zeros(out.shape, BF16)
    first = out.at[0]
    flat = cot[...].astype(F32)
    for s in range(2):
        piece = flat[:, s, :].astype(BF16)
        for c in range(3):
            lead = c * rows + s * quarter
            first[lead : lead + quarter, :third] = piece[:, c * third : (c + 1) * third]
    eye = (iota((shard, shard), 0) == iota((shard, shard), 1)).astype(F32).astype(BF16)
    first[:shard, third:] = nt(eye, wo[...]).astype(BF16)
    values = info[...]
    hi = values.astype(BF16).astype(F32)
    mid = (values - hi).astype(BF16).astype(F32)
    low = values - hi - mid
    total = jnp.zeros((16, LANES), F32)
    for s in range(2):
        terms = [term[:, 4 * s : 4 * s + 4] for term in (hi, mid, low)]
        stacked = jnp.concatenate(terms + [jnp.zeros((quarter, 4), F32)], axis=1).astype(BF16)
        spot = iota((quarter, LANES), 0) + s * quarter == iota((quarter, LANES), 1)
        total = total + tn(stacked, jnp.where(spot, 1.0, 0.0).astype(BF16))
    first[out.shape[1] - 16 :, :LANES] = total.astype(BF16)
    for z in range(1, out.shape[0]):
        out[z] = first[...]


def sent_body(hidden, gate, up, out):
    for c in range(out.shape[0]):
        out[c, :, :hidden] = gate[:, c * hidden : (c + 1) * hidden]
        out[c, :, hidden:] = up[:, c * hidden : (c + 1) * hidden]


def early_body(tok, quarter, *refs):
    pieces, cot_out, info_out, mats_out = refs
    exp_pos = lax.axis_index("exp")
    parts = pieces.shape[0]
    rows = 2 * tok
    third = cot_out.shape[1] // 3
    shard = mats_out.shape[0]
    info = jnp.zeros((16, rows), F32)
    for z in range(parts):
        for s in range(2):
            spot = s * tok + z * quarter
            for c in range(3):
                lead = c * 2 * quarter + s * quarter
                cot_out[spot : spot + quarter, c * third : (c + 1) * third] = pieces[
                    z, lead : lead + quarter, :third
                ]
        lane, row = iota((LANES, rows), 0), iota((LANES, rows), 1)
        target = (lane // quarter) * tok + z * quarter + lane % quarter
        spot = jnp.where((target == row) & (lane < 2 * quarter), 1.0, 0.0).astype(BF16)
        info = info + nn(pieces[z, pieces.shape[1] - 16 :, :LANES], spot)
    mats_out[...] = jnp.concatenate(
        [pieces[exp_pos ^ d, :shard, third:] for d in range(parts)], axis=1
    )
    low = info[0:4] + (info[4:8] + info[8:12])
    info_out[...] = jnp.concatenate([low, jnp.zeros((4, rows), F32)], axis=0)


def lay_rows(refs, out):
    if len(refs) == 1:
        out[...] = refs[0][...]
        return
    ctx_pos = lax.axis_index("ctx")
    for ref, i, d in each_block(refs):
        rows = ref.shape[1]
        out[pl.ds(pl.multiple_of((ctx_pos ^ d) * rows, rows), rows), :] = ref[i]


def lay_body(*refs):
    blocks, (mats_out, own_out) = refs[:-2], refs[-2:]
    lay_rows(blocks, mats_out)
    own_out[...] = mats_out[:, : own_out.shape[1]]


def project_body(hl, tok, folded, gain, *refs):
    q_out, kv_out, a_out, w = refs[-4:]
    blocks = refs[:-4]
    ctx_pos = lax.axis_index("ctx")
    rows = 2 * tok
    if folded:
        listed = each_block(blocks)
        for ref, i, d in listed:
            shard = w.shape[0] // len(listed)
            rest = shard - folded
            lead = (ctx_pos ^ d) * shard
            w[pl.ds(pl.multiple_of(lead, 16), folded), :] = ref[i, rows:, : 3 * hl]
            side = ref[i, rows:, 3 * hl :]
            w[pl.ds(pl.multiple_of(lead + folded, 16), rest), :] = jnp.concatenate(
                [side[t * rest : (t + 1) * rest] for t in range(3)], axis=1
            )
    else:
        w[...] = blocks[-1][...]
        blocks = blocks[:-1]
    listed = each_block(blocks)
    for lead in range(0, len(listed), 4):
        group = listed[lead : lead + 4]
        x = jnp.concatenate([ref[i, :rows, :] for ref, i, _ in group], axis=0).astype(F32)
        normed = (x * rms_scale(x) * gain[...]).astype(BF16)
        full = nn(normed, w[...] if lead == 0 else w[:, hl:]).astype(BF16)
        if lead == 0:
            a_out[...] = normed[:rows]
            q_out[...] = full[:rows, :hl]
            full = full[:, hl:]
        for t, (_, _, d) in enumerate(group):
            kv_out[ctx_pos ^ d] = full[t * rows : (t + 1) * rows].reshape(2, tok, 2 * hl)


def fold_lanes(value):
    rows, cols = value.shape
    if cols % LANES != LANES // 2:
        return value
    whole = [value[:, c : c + LANES] for c in range(0, cols - LANES // 2, LANES)]
    tail = value[:, cols - LANES // 2 :]
    tail = jnp.concatenate([tail[: rows // 2], tail[rows // 2 :]], axis=1)
    return jnp.concatenate(whole + [tail], axis=0)


def unfold_lanes(value, rows, cols):
    if cols % LANES != LANES // 2:
        return value
    count = cols // LANES
    whole = [value[c * rows : (c + 1) * rows] for c in range(count)]
    tail = value[count * rows :]
    tail = jnp.concatenate([tail[:, : LANES // 2], tail[:, LANES // 2 :]], axis=0)
    return jnp.concatenate(whole + [tail], axis=1)


def attend_body(heads, q, table, rev, kv_out, o_out, low_out, p_out):
    ctx_pos, exp_pos = lax.axis_index("ctx"), lax.axis_index("exp")
    rows = q.shape[0]
    tok = rows // 2
    hl = heads * HD
    seq_len = rev.shape[1]
    start = ctx_pos * tok
    buckets, head_total = table.shape
    pick = jnp.where(
        iota((8, head_total), 1) == exp_pos * heads + iota((8, head_total), 0), 1.0, 0.0
    )
    own_table = nt(pick, table[...], HIGH)
    hot = jnp.where(iota((buckets, seq_len), 0) == rev[...], 1.0, 0.0)
    bias = pltpu.roll(nn(own_table, hot, HIGH), start + 1, 1)
    open_keys = iota((tok, seq_len), 1) <= start + iota((tok, seq_len), 0)
    skewed = []
    for h in range(heads):
        wide = jnp.broadcast_to(bias[h : h + 1, :], (tok, seq_len))
        turned = pltpu.roll(wide, 0, 1, stride=1, stride_axis=0)
        skewed.append(jnp.where(open_keys, turned, FLOOR))
    halves = []
    for s in range(2):
        outs = []
        for h in range(heads):
            query = q[s * tok : (s + 1) * tok, h * HD : (h + 1) * HD]
            key = kv_out[:, s, :, h * HD : (h + 1) * HD].reshape(seq_len, HD)
            value = kv_out[:, s, :, hl + h * HD : hl + (h + 1) * HD].reshape(seq_len, HD)
            scores = nt(query, key) * (HD**-0.5) + skewed[h]
            top = jnp.max(scores, axis=-1, keepdims=True)
            weights = jnp.exp(scores - top)
            probs = weights * (1.0 / jnp.sum(weights, axis=-1, keepdims=True))
            p_out[s * heads + h] = probs
            outs.append(nn(probs.astype(BF16), value))
        out = jnp.concatenate(outs, axis=1)
        o_out[s * tok : (s + 1) * tok, :] = out
        halves.append(out.astype(BF16))
    packed = fold_lanes(jnp.concatenate(halves, axis=0))
    low_out[...] = packed


def gate_values(logits, info):
    route0, route1 = info[0:1].astype(jnp.int32), info[1:2].astype(jnp.int32)
    choice0 = jnp.zeros_like(info[0:1])
    choice1 = jnp.zeros_like(info[0:1])
    for e in range(logits.shape[0]):
        choice0 = choice0 + jnp.where(route0 == e, logits[e : e + 1], 0.0)
        choice1 = choice1 + jnp.where(route1 == e, logits[e : e + 1], 0.0)
    top = jnp.maximum(choice0, choice1)
    up0, up1 = jnp.exp(choice0 - top), jnp.exp(choice1 - top)
    total = up0 + up1
    return up0 / total, up1 / total


def route_body(tok, quarter, cap, parts, *refs):
    x, mats = refs[:2]
    lows = refs[2 : 2 + parts]
    gain, router_t, info_ref, cot, resid_out, gates_out, slots_out = refs[2 + parts :]
    exp_pos = lax.axis_index("exp")
    rows, width = 2 * tok, gain.shape[1]
    attn = nt(
        jnp.concatenate(
            [unfold_lanes(low[...], rows, mats.shape[1] // parts) for low in lows], axis=1
        ),
        mats[...],
    )
    for s in range(2):
        resid_out[s * tok : (s + 1) * tok, :] = (
            x[s * tok : (s + 1) * tok, :].astype(F32) + attn[s * tok : (s + 1) * tok]
        )
    resid = resid_out[...]
    normed = (resid * rms_scale(resid) * gain[...]).astype(BF16)
    logits = nt(router_t[...], normed.astype(F32), HIGH)
    info = info_ref[...]
    soft0, soft1 = gate_values(logits, info)
    gate0, gate1 = info[2:3] * soft0, info[3:4] * soft1
    gates_out[...] = jnp.concatenate([gate0, gate1, jnp.zeros((6, rows), F32)], axis=0)
    route0, route1 = info[0:1].astype(jnp.int32), info[1:2].astype(jnp.int32)
    before = block_before(rows, tok, quarter)
    hot, _ = slot_hot(route0, route1, exp_pos, before, tok, quarter, cap, parts)
    hot = jnp.where(hot, 1.0, 0.0).astype(BF16)
    first = route0 == exp_pos
    gate = jnp.where(first, gate0, gate1)
    slope = soft0 * soft1 * jnp.where(first, info[2:3], info[3:4])
    other = jnp.where(first, info[1:2], info[0:1])
    gate_hi, slope_hi = gate.astype(BF16).astype(F32), slope.astype(BF16).astype(F32)
    extras = jnp.concatenate(
        [gate_hi, gate - gate_hi, slope_hi, slope - slope_hi, other, jnp.zeros((LANES - 5, rows), F32)],
        axis=0,
    ).astype(BF16)
    slots_out[:, :width] = nn(hot, normed).astype(BF16)
    slots_out[:, width : width + LANES] = nt(hot, extras).astype(BF16)
    slots_out[:, width + LANES :] = nn(hot, cot[...]).astype(BF16)


def expert_back_body(count, *refs):
    xs = refs[:count]
    w_in, down, router_t, near_out, far_out, hid, dg_out, du_out, spread_out = refs[count:]
    exp_pos = lax.axis_index("exp")
    width, hidden = w_in.shape[0], down.shape[0]
    experts = router_t.shape[0]
    gate_w, up_w = w_in[:, :hidden], w_in[:, hidden:]
    down_w = down[...]
    done = 0
    side = near_out.shape[0]
    for x_group in grouped(xs):
        rows = stack(x_group, cols=slice(0, width))
        extras = stack(x_group, cols=slice(width, width + LANES)).astype(F32)
        step = rows.shape[0]
        part = slice(done, done + step)
        done = done + step
        gate = extras[:, 0:1] + extras[:, 1:2]
        slope = extras[:, 2:3] + extras[:, 3:4]
        other = extras[:, 4:5].astype(jnp.int32)
        pre = nn(rows, gate_w)
        up = nn(rows, up_w)
        raw = nt(stack(x_group, cols=slice(width + LANES, None)), down_w)
        squared = pre * pre
        tanh = jnp.tanh(GELU_C * (pre + GELU_A * pre * squared))
        half = 0.5 * (1.0 + tanh)
        act = pre * half
        hidden_low = (act * up).astype(BF16)
        hid[part, :] = hidden_low
        slope_act = half + 0.5 * pre * (1.0 - tanh * tanh) * (
            GELU_C * (1.0 + 3.0 * GELU_A * squared)
        )
        gate_grad = jnp.sum(hidden_low.astype(F32) * raw, axis=-1, keepdims=True)
        grad = gate * raw
        dg = (grad * up * slope_act).astype(BF16)
        du = (grad * act).astype(BF16)
        dg_out[part, :] = dg
        du_out[part, :] = du
        tilt = gate_grad * slope
        kind = iota((step, 8), 1)
        spread = jnp.where(kind == exp_pos, tilt, 0.0) - jnp.where(kind == other, tilt, 0.0)
        spread_out[part, :] = spread
        back = nt(dg, gate_w) + nt(du, up_w)
        for e in range(experts):
            back = back + spread[:, e : e + 1] * router_t[e : e + 1, :]
        out, lead = (near_out, done - step) if done <= side else (far_out, done - step - side)
        out[lead : lead + step, :width] = back.astype(BF16)
        out[lead : lead + step, width:] = nn(hidden_low, down_w).astype(BF16)


def expert_weights_body(count, *refs):
    xs = refs[:count]
    dg, du, *w_outs, wide = refs[count:]
    width = wide.shape[0] * wide.shape[1]
    gate_sum, up_sum = 0.0, 0.0
    done = 0
    for x_group in grouped(xs):
        rows = stack(x_group, cols=slice(0, width))
        part = slice(done, done + rows.shape[0])
        done = done + rows.shape[0]
        gate_sum = gate_sum + tn(rows, dg[part, :])
        up_sum = up_sum + tn(rows, du[part, :])
    w_grad = jnp.concatenate([gate_sum.astype(BF16), up_sum.astype(BF16)], axis=1)
    if len(w_outs) == 1:
        w_outs[0][...] = w_grad.reshape(w_outs[0].shape)
        return
    ctx_pos = lax.axis_index("ctx")
    wide[...] = w_grad.reshape(wide.shape)
    for d, out in enumerate(w_outs):
        out[...] = wide[ctx_pos ^ d]


def expert_rest_body(count, *refs):
    xs = refs[:count]
    hid, spread, down_out, router_out = refs[count:]
    width = down_out.shape[1]
    down_sum, router_sum = 0.0, 0.0
    done = 0
    for x_group in grouped(xs):
        rows = stack(x_group, cols=slice(0, width))
        extras = stack(x_group, cols=slice(width, width + LANES)).astype(F32)
        part = slice(done, done + rows.shape[0])
        done = done + rows.shape[0]
        gate = extras[:, 0:1] + extras[:, 1:2]
        cot = stack(x_group, cols=slice(width + LANES, None))
        dy = (gate * cot.astype(F32)).astype(BF16)
        down_sum = down_sum + tn(hid[part, :], dy)
        router_sum = router_sum + tn(spread[part, :], rows.astype(F32), HIGH)
    down_out[...] = down_sum
    router_out[...] = router_sum


def widen_body(*refs):
    blocks, (gate_out, up_out) = refs[:-2], refs[-2:]
    hidden = blocks[0].shape[-1] // 2
    if len(blocks) == 1:
        for c in range(blocks[0].shape[0]):
            gate_out[:, c * hidden : (c + 1) * hidden] = blocks[0][c, :, :hidden].astype(F32)
            up_out[:, c * hidden : (c + 1) * hidden] = blocks[0][c, :, hidden:].astype(F32)
        return
    ctx_pos = lax.axis_index("ctx")
    for d, block in enumerate(blocks):
        spot = pl.ds(pl.multiple_of((ctx_pos ^ d) * hidden, LANES), hidden)
        gate_out[:, spot] = block[:, :hidden].astype(F32)
        up_out[:, spot] = block[:, hidden:].astype(F32)


def mix_body(tok, quarter, cap, parts, resid, info_ref, gates_ref, ys, out, held, wide):
    exp_pos = lax.axis_index("exp")
    rows, width = 2 * tok, resid.shape[1]
    info, gates = info_ref[...], gates_ref[...]
    route0, route1 = info[0:1].astype(jnp.int32), info[1:2].astype(jnp.int32)
    before = block_before(rows, tok, quarter)
    block = (iota((1, rows), 1) % tok) // quarter
    weights = []
    for e in range(parts):
        named = ((route0 == e) | (route1 == e)) & (block == exp_pos)
        flags = jnp.broadcast_to(jnp.where(named, 1.0, 0.0), (16, rows)).astype(BF16)
        rank = jnp.where(named, nn(flags, before)[0:1].astype(jnp.int32), -1)
        gate = jnp.where(route0 == e, gates[0:1], gates[1:2])
        weights.append(jnp.where(iota((cap, rows), 0) == rank, gate, 0.0))
    weights = jnp.concatenate(weights, axis=0)
    hi = weights.astype(BF16)
    low = (weights - hi.astype(F32)).astype(BF16)
    y = jnp.concatenate(
        [ys[e].astype(F32)[parts * cap :] for e in range(parts)], axis=0
    ).astype(BF16)
    held[...] = resid[...] + tn(hi, y) + tn(low, y)
    for s in range(2):
        spot = pl.ds(pl.multiple_of(s * tok + exp_pos * quarter, quarter), quarter)
        wide[:, s, :] = held[spot, :]
    out[...] = wide[...].astype(BF16)


def attend_back_body(heads, tok, quarter, cap, parts, *refs):
    (
        returned, resid_ref, cot, gain, info_ref, o, out_t, q, kv, p,
        own_out, dq_out, near_out, far_out, grad_out, sums_out, small_out, held, dkv,
    ) = refs
    ctx_pos, exp_pos = lax.axis_index("ctx"), lax.axis_index("exp")
    rows, width = resid_ref.shape
    hl = heads * HD
    count = kv.shape[0]
    seq_len = count * tok
    start = ctx_pos * tok
    info = info_ref[...]
    route0, route1 = info[0:1].astype(jnp.int32), info[1:2].astype(jnp.int32)
    before = block_before(rows, tok, quarter)
    grad = jnp.zeros((rows, width), F32)
    for e in range(parts):
        hot, _ = slot_hot(route0, route1, e, before, tok, quarter, cap, parts)
        piece = returned[e].astype(F32)[: parts * cap].astype(BF16)
        grad = grad + tn(jnp.where(hot, 1.0, 0.0).astype(BF16), piece)
    resid = resid_ref[...]
    scale = rms_scale(resid)
    centred = resid * scale
    small_out[...] = jnp.broadcast_to(
        jnp.sum(grad * centred, axis=0, keepdims=True) * (1.0 / parts), small_out.shape
    )
    inner = grad * gain[...]
    held[...] = cot[...].astype(F32) + scale * (
        inner - centred * jnp.mean(inner * centred, axis=-1, keepdims=True)
    )
    for s in range(2):
        spot = pl.ds(pl.multiple_of(s * tok + exp_pos * quarter, quarter), quarter)
        own_out[s * quarter : (s + 1) * quarter, :] = held[spot, :]
    attn_grad = held[...].astype(BF16)
    grad_o = nn(attn_grad, out_t[...]).astype(BF16)
    grad_out[...] = attn_grad
    sums = [jnp.zeros((tok, seq_len), F32) for _ in range(heads)]
    for s in range(2):
        here = slice(s * tok, (s + 1) * tok)
        keys, values, queries = [], [], []
        for h in range(heads):
            cols = slice(h * HD, (h + 1) * HD)
            probs = p[s * heads + h]
            key = kv[:, s, :, cols].reshape(seq_len, HD)
            value = kv[:, s, :, hl + h * HD : hl + (h + 1) * HD].reshape(seq_len, HD)
            do = grad_o[here, cols]
            delta = jnp.sum(do.astype(F32) * o[here, cols], axis=-1, keepdims=True)
            ds = (probs * (nt(do, value) - delta)).astype(BF16)
            sums[h] = sums[h] + ds.astype(F32)
            values.append(tn(probs.astype(BF16), do).astype(BF16))
            keys.append((tn(ds, q[here, cols]) * (HD**-0.5)).astype(BF16))
            queries.append(nn(ds, key) * (HD**-0.5))
        dq_out[here, :] = jnp.concatenate(queries, axis=1).astype(BF16)
        dkv[:, s] = jnp.concatenate(keys + values, axis=1).reshape(count, tok, 2 * hl)
    for j in range(count // 2):
        near_out[j] = dkv[ctx_pos ^ (2 * j)].reshape(rows, 2 * hl)
        far_out[j] = dkv[ctx_pos ^ (2 * j + 1)].reshape(rows, 2 * hl)
    for h in range(heads):
        sums_out[h] = sums[h]


def table_body(buckets, sums, attn_grad, low, rev, table_out, dout_t):
    ctx_pos, exp_pos = lax.axis_index("ctx"), lax.axis_index("exp")
    heads, tok, seq_len = sums.shape
    width = table_out.shape[1]
    start = ctx_pos * tok
    dout_t[...] = tn(
        attn_grad[...], unfold_lanes(low[...], attn_grad.shape[0], dout_t.shape[1])
    ).astype(BF16)
    lines = []
    for h in range(heads):
        turned = sums[h]
        step = 1
        while step < tok:
            bit = (iota((tok, seq_len), 0) // step) % 2 == 1
            turned = jnp.where(bit, pltpu.roll(turned, seq_len - step, 1), turned)
            step *= 2
        lines.append(jnp.sum(turned, axis=0, keepdims=True))
    lines = jnp.concatenate(lines + [jnp.zeros((8 - heads, seq_len), F32)], axis=0)
    lines = pltpu.roll(lines, seq_len - start - 1, 1)
    counts = jnp.zeros((8, LANES), F32)
    for lead in range(0, seq_len, 512):
        cut = slice(lead, min(lead + 512, seq_len))
        here = lines[:, cut]
        hot = jnp.where(iota((here.shape[1], LANES), 1) == rev[cut, :], 1.0, 0.0)
        counts = counts + nn(here, hot, HIGH)
    table = jnp.zeros((8, width), F32)
    for h in range(heads):
        spot = (exp_pos * heads + h) * buckets
        place = jnp.where(
            (iota((LANES, width), 1) == spot + iota((LANES, width), 0))
            & (iota((LANES, width), 0) < buckets),
            1.0,
            0.0,
        )
        table = table + nn(jnp.broadcast_to(counts[h : h + 1], (8, LANES)), place, HIGH)
    table_out[...] = table


def back_project_body(quarter, parts, *refs):
    da_out, w_near, w_far, small_out, wide = refs[-5:]
    dq, w, a, dout_t, x, gain, small, table, router = refs[:9]
    terms = refs[9:-5]
    ctx_pos, exp_pos = lax.axis_index("ctx"), lax.axis_index("exp")
    rows, width = a.shape
    tok = rows // 2
    dkv = terms[0][...].astype(F32)
    for term in terms[1:]:
        dkv = dkv + term[...].astype(F32)
    grads = jnp.concatenate([dq[...], dkv.astype(BF16)], axis=1)
    da = nt(grads, w[...])
    total = jnp.zeros((1, width), F32)
    for s in range(2):
        piece = x[s * tok : (s + 1) * tok, :].astype(F32)
        here = da[s * tok : (s + 1) * tok]
        total = total + jnp.sum(piece * rms_scale(piece) * here, axis=0, keepdims=True)
        for z in range(parts):
            da_out[z, s * quarter : (s + 1) * quarter, :] = here[
                z * quarter : (z + 1) * quarter
            ].astype(BF16)
    small_out[0:1, :] = total
    small_out[1:2, :] = small[0:1, :]
    small_out[2:3, :] = table[0:1, :]
    small_out[3:7, :] = router[0:4, :]
    small_out[7:8, :] = jnp.zeros((1, width), F32)
    full = jnp.concatenate([tn(a[...], grads).astype(BF16), dout_t[...]], axis=1)
    if len(wide.shape) == 2:
        wide[...] = full
        w_near[...] = full
        w_far[...] = full
        return
    count, shard, _ = wide.shape
    wide[...] = full.reshape(wide.shape)
    for j in range(count // 2):
        w_near[j] = wide[ctx_pos ^ (2 * j)]
        w_far[j] = wide[ctx_pos ^ (2 * j + 1)]


def finish_body(tok, quarter, x, gain, own, pieces, out):
    exp_pos = lax.axis_index("exp")
    width = gain.shape[1]
    for s in range(2):
        spot = pl.ds(pl.multiple_of(s * tok + exp_pos * quarter, quarter), quarter)
        rows = x[spot, :].astype(F32)
        here = slice(s * quarter, (s + 1) * quarter)
        grad = pieces[0, here, :].astype(F32)
        for z in range(1, pieces.shape[0]):
            grad = grad + pieces[z, here, :].astype(F32)
        scale = rms_scale(rows)
        centred = rows * scale
        inner = grad * gain[...]
        out[:, s, :] = own[here, :] + scale * (
            inner - centred * jnp.mean(inner * centred, axis=-1, keepdims=True)
        )


def last_body(count, tok, quarter, x, gain, own, pieces, *refs):
    terms, smalls = refs[:count], refs[count:-9]
    finish_out, q_out, k_out, v_out, o_out, attn_out, ffn_out, table_out, router_out = refs[-9:]
    finish_body(tok, quarter, x, gain, own, pieces, finish_out)
    hl = q_out.shape[1]
    total = terms[0][...].astype(F32)
    for term in terms[1:]:
        total = total + term[...].astype(F32)
    q_out[...] = total[:, :hl]
    k_out[...] = total[:, hl : 2 * hl]
    v_out[...] = total[:, 2 * hl : 3 * hl]
    o_out[...] = total[:, 3 * hl :].T
    small = smalls[0][...]
    for term in smalls[1:]:
        small = small + term[...]
    attn_out[...] = small[0]
    ffn_out[...] = small[1]
    heads, buckets = table_out.shape
    for h in range(heads):
        table_out[h : h + 1, :] = small[2:3, h * buckets : (h + 1) * buckets]
    router_out[...] = small[3 : 3 + router_out.shape[0], :]


def on_device(
    block_input,
    output_cotangent,
    attn_gain,
    query_weight,
    key_weight,
    value_weight,
    output_weight,
    bias_table,
    buckets,
    ffn_gain,
    router_weight,
    routes,
    route_prior,
    gate_weight,
    up_weight,
    down_weight,
):
    tok, seqs, width = block_input.shape
    quarter = routes.shape[0]
    ctx_size, parts = lax.axis_size("ctx"), lax.axis_size("exp")
    hl = query_weight.shape[1]
    heads = hl // HD
    cap = (3 * quarter * seqs + 3) // 4
    slots = parts * cap
    rows = tok * seqs
    shard = query_weight.shape[0]
    hidden = down_weight.shape[1]
    half = ctx_size // 2
    seq_len = tok * ctx_size
    aligned = shard % 16 == 0
    gain_one, gain_two = attn_gain.reshape(1, width), ffn_gain.reshape(1, width)
    router_t = router_weight.T
    rev = buckets[::-1].reshape(1, seq_len)
    down = down_weight.reshape(hidden, width)

    folded = shard * 5 // 6 if shard % 96 == 0 else 0
    info = jnp.concatenate([routes.astype(F32), route_prior], axis=2).reshape(quarter, 4 * seqs)
    cot_pack, x = call(
        functools.partial(pack_body, folded),
        "pack",
        [
            ((parts, max(3 * seqs * quarter, shard) + 16, width // 3 + hl), BF16),
            ((rows + folded, width), BF16),
        ],
        output_weight, output_cotangent, info, block_input,
        *([query_weight, key_weight, value_weight] if folded else []), us=1.5, wide=True,
    )
    x_blocks = gather_ctx(x)
    if not folded:
        packed = jnp.concatenate([query_weight, key_weight, value_weight], axis=1)
        x_blocks = x_blocks + [lax.all_gather(packed, "ctx", axis=0, tiled=True)]
    cot_packs = trade_exp(cot_pack)
    cot_block, info_block, mats = call(
        functools.partial(early_body, tok, quarter),
        "early_slots",
        [
            ((rows, width), BF16),
            ((8, rows), F32),
            ((shard, parts * hl), BF16),
        ],
        cot_packs,
    )
    q, kv_all, normed, w_qkv = call(
        functools.partial(project_body, hl, tok, folded),
        "project",
        [
            ((rows, hl), BF16),
            ((ctx_size, seqs, tok, 2 * hl), BF16),
            ((rows, width), BF16),
            ((width, 3 * hl), BF16),
        ],
        gain_one, *x_blocks, us=4.0, after=[info_block], wide=True,
    )
    mats_blocks = (
        gather_ctx(mats, [q]) if aligned else [lax.all_gather(mats, "ctx", axis=0, tiled=True)]
    )

    sent = call(
        functools.partial(sent_body, hidden),
        "sent",
        ((ctx_size, shard, 2 * hidden), BF16),
        gate_weight.reshape(shard, ctx_size * hidden), up_weight.reshape(shard, ctx_size * hidden),
        us=2.0, after=[q],
    )
    mats_full, out_t, laid = call(
        lay_body, "lay_out", [((width, parts * hl), BF16), ((width, hl), BF16)], *mats_blocks,
        us=2.5, token=True,
    )
    low_shape = (rows * hl // LANES, LANES) if hl % LANES == LANES // 2 else (rows, hl)
    o, low, p = call(
        functools.partial(attend_body, heads),
        "attend",
        [
            ((rows, hl), F32),
            (low_shape, BF16),
            ((seqs * heads, tok, seq_len), F32),
        ],
        q, bias_table, rev, kv_all, us=4.8, after=[laid], wide=True,
    )
    lows = spread_exp(low)
    w_in = lax.all_to_all(hold(sent, low), "ctx", split_axis=0, concat_axis=0, tiled=True)
    w_in = w_in.reshape(width, 2 * hidden)

    resid, gates, x_slots = call(
        functools.partial(route_body, tok, quarter, cap, parts),
        "route",
        [((rows, width), F32), ((8, rows), F32), ((slots, 2 * width + LANES), BF16)],
        x, mats_full, *lows, gain_two, router_t, info_block, cot_block, us=3.7,
    )
    x_blocks = gather_ctx(x_slots)
    side = half * slots
    cut = len(x_blocks)
    back_near, back_far, hid, dg, du, spread = call(
        functools.partial(expert_back_body, cut),
        "expert_back",
        [((side, 2 * width), BF16)] * 2 + [((2 * side, hidden), BF16)] * 3 + [((2 * side, 8), F32)],
        *x_blocks, w_in, down, router_t, us=8.0, wide=True,
    )
    back_terms = send_direct(
        add_pair(
            back_near.reshape(half, slots, 2 * width), back_far.reshape(half, slots, 2 * width)
        )
    )
    back_sums, summed = call(
        functools.partial(back_sum_body, cap),
        "sum_back",
        ((parts, slots + cap, width), BF16),
        *back_terms, us=2.0, token=True,
    )
    returned = trade_exp(back_sums)
    by_permutes = ctx_size <= 8 and hidden % LANES == 0
    w_shape = (shard, 2 * hidden)
    *w_grads, weighed = call(
        functools.partial(expert_weights_body, cut),
        "expert_weights",
        [(w_shape, BF16)] * ctx_size if by_permutes else [((ctx_size, *w_shape), BF16)],
        *x_blocks, dg, du, us=4.0, after=[summed], wide=True, token=True,
        scratch=[pltpu.VMEM((ctx_size, *w_shape), BF16)],
    )
    down_grad, router = call(
        functools.partial(expert_rest_body, cut),
        "expert_rest",
        [((hidden, width), F32), ((8, width), F32)],
        *x_blocks, hid, spread, us=3.0, after=[weighed], wide=True,
    )
    if by_permutes:
        w_back = [w_grads[0]] + [swap(w_grads[d], "ctx", d) for d in range(1, ctx_size)]
    else:
        w_back = [lax.all_to_all(w_grads[0], "ctx", split_axis=0, concat_axis=0, tiled=True)]
    gate_grad, up_grad, widened = call(
        widen_body,
        "widen",
        [((shard, ctx_size * hidden), F32)] * 2,
        *w_back, us=2.0, token=True,
    )
    resid_grad, dq, dkv_near, dkv_far, attn_grad, score_sums, small = call(
        functools.partial(attend_back_body, heads, tok, quarter, cap, parts),
        "attend_back",
        [
            ((seqs * quarter, width), F32),
            ((rows, hl), BF16),
            ((half, rows, 2 * hl), BF16),
            ((half, rows, 2 * hl), BF16),
            ((rows, width), BF16),
            ((heads, tok, seq_len), F32),
            ((8, width), F32),
        ],
        returned, resid, cot_block, gain_two, info_block, o, out_t, q, kv_all, p,
        us=8.0,
        scratch=[
            pltpu.VMEM((rows, width), F32),
            pltpu.VMEM((ctx_size, seqs, tok, 2 * hl), BF16),
        ],
        after=[widened, router], wide=True,
    )
    dkv_both = add_pair(dkv_near, dkv_far)
    dkv_terms = send_direct(dkv_both)
    block_output, mixed = call(
        functools.partial(mix_body, tok, quarter, cap, parts),
        "mix",
        ((quarter, seqs, width), BF16),
        resid, info_block, gates, returned,
        scratch=[pltpu.VMEM((rows, width), F32), pltpu.VMEM((quarter, seqs, width), F32)],
        token=True,
        after=[dkv_both[0]],
    )
    table, dout_t = call(
        functools.partial(table_body, bias_table.shape[0]),
        "table",
        [((8, width), F32), ((width, hl), BF16)],
        score_sums, attn_grad, low, rev.reshape(seq_len, 1), us=3.0, after=[dkv_both[0]],
    )
    w_shape = (half, shard, 4 * hl) if aligned else (width, 4 * hl)
    da_parts, w_near, w_far, small = call(
        functools.partial(back_project_body, quarter, parts),
        "back_project",
        [((parts, seqs * quarter, width), BF16)]
        + [(w_shape, BF16), (w_shape, BF16), ((8, width), F32)],
        dq, w_qkv, normed, dout_t, x, gain_one, small, table, router, *dkv_terms, us=3.4,
        scratch=[
            pltpu.VMEM((ctx_size, shard, 4 * hl) if aligned else (width, 4 * hl), BF16),
        ],
        after=[mixed],
    )
    da_terms = trade_exp(da_parts)
    if aligned:
        w_both = add_pair(w_near, w_far)
        w_terms = send_direct(w_both)
    else:
        w_terms = [lax.psum_scatter(w_near.astype(F32), "ctx", scatter_dimension=0, tiled=True)]
    small = sum(spread_exp(small))
    small = small + swap(small, "ctx", 1)
    smalls = [small] + [swap(small, "ctx", 2 * j) for j in range(1, half)]
    buckets_total, head_total = bias_table.shape
    (
        input_grad, query_grad, key_grad, value_grad, output_grad,
        attn_gain_grad, ffn_gain_grad, table_grad, router_grad,
    ) = call(
        functools.partial(last_body, len(w_terms), tok, quarter),
        "last",
        [((quarter, seqs, width), F32)] + [((shard, hl), F32)] * 3
        + [((hl, shard), F32), ((width,), F32), ((width,), F32)]
        + [((head_total, buckets_total), F32), ((router_t.shape[0], width), F32)],
        x, gain_one, resid_grad, da_terms, *w_terms, *smalls, us=2.5,
    )
    return (
        block_output,
        input_grad,
        attn_gain_grad,
        query_grad,
        key_grad,
        value_grad,
        output_grad,
        table_grad.T,
        ffn_gain_grad,
        router_grad.T,
        gate_grad[None],
        up_grad[None],
        down_grad.reshape(1, hidden, width),
    )


def solution(mesh):
    return jax.shard_map(
        on_device,
        mesh=mesh,
        in_specs=(
            P("ctx", None, None),
            P(("ctx", "exp"), None, None),
            P(),
            P("ctx", "exp"),
            P("ctx", "exp"),
            P("ctx", "exp"),
            P("exp", "ctx"),
            P(),
            P(),
            P(),
            P(),
            P(("ctx", "exp"), None, None),
            P(("ctx", "exp"), None, None),
            P("exp", "ctx", None),
            P("exp", "ctx", None),
            P("exp", "ctx", None),
        ),
        out_specs=(
            P(("ctx", "exp"), None, None),
            P(("ctx", "exp"), None, None),
            P(),
            P("ctx", "exp"),
            P("ctx", "exp"),
            P("ctx", "exp"),
            P("exp", "ctx"),
            P(),
            P(),
            P(),
            P("exp", "ctx", None),
            P("exp", "ctx", None),
            P("exp", "ctx", None),
        ),
        check_vma=False,
    )
```

time: 260 us -> 191 us (0.73)
  waiting for transfers between devices: 94.5 us -> 68.3 us
  local copies, waits for them, and re-layouts: 28.2 us -> 11 us
  starting transfers between devices: 76 us -> 61.4 us
  other arithmetic: 11.6 us -> 4.27 us
  Pallas kernels: 47 us -> 43.7 us
    ppermute x54 -> x50, waiting for transfers between devices: 92.1 us -> 68.3 us  [swap(): return lax.ppermute(value, axis, [(i, i ^ bits) for i in range(devices)])]
    ppermute x54 -> x50, starting transfers between devices: 64.6 us -> 41.9 us  [swap(): return lax.ppermute(value, axis, [(i, i ^ bits) for i in range(devices)])]
    all_to_all x3 -> x4, starting transfers between devices: 11.4 us -> 19.5 us  [the longest x3 14.9 us: trade_exp(): return lax.all_to_all(value, 'exp', split_axis=0, concat_axis=0, tiled=True)]
    reshape x5 -> x1, local copies, waits for them, and re-layouts: 6.07 us -> 0.67 us  [on_device(): jnp.concatenate([routes.astype(F32), route_prior], axis=2)]
    slice x8 -> x0, local copies, waits for them, and re-layouts: 3.66 us -> none  [the longest x2 0.86 us: on_device(): up_grad = w_back[:, :, hidden:].reshape(1, shard, ctx_size * hidden)]
    pallas_call x11 -> x22, Pallas kernels: 47 us -> 43.7 us  [the longest x17 43.7 us: call(): pl.pallas_call(run, out_shape=shapes[0] if single else shapes, in_specs=s...]
    concatenate x7 -> x1, other arithmetic: 3.95 us -> 0.69 us  [on_device(): jnp.concatenate([routes.astype(F32), route_prior], axis=2)]
    unnamed x95 -> x115, local copies, waits for them, and re-layouts: 9.8 us -> 8.94 us
  transfers between devices with their start and end apart: 57 -> 54, of which waited for: 22 -> 18; matrix products, arithmetic and copies ran while one was open for 11% -> 1% of each run, Pallas kernels for 9% -> 10%
where the time goes in v2:
time: 191 us; the launch traced here: 190 us
  waiting for transfers between devices  68.3 us (36%)
  starting transfers between devices  61.4 us (32%)
  Pallas kernels  43.7 us (23%)
  local copies, waits for them, and re-layouts  11 us (6%)
  other arithmetic  4.27 us (2%)
    ppermute x50, waiting for transfers between devices, swap(): return lax.ppermute(value, axis, [(i, i ^ bits) for i in range(devices)])  68.3 us
    pallas_call x17, Pallas kernels, call(): pl.pallas_call(run, out_shape=shapes[0] if single else shapes, in_specs=s...  43.7 us
    ppermute x50, starting transfers between devices, swap(): return lax.ppermute(value, axis, [(i, i ^ bits) for i in range(devices)])  41.9 us
    all_to_all x3, starting transfers between devices, trade_exp(): return lax.all_to_all(value, 'exp', split_axis=0, concat_axis=0, tiled=True)  14.9 us
    unnamed x115, local copies, waits for them, and re-layouts  8.94 us
    all_to_all x1, starting transfers between devices, on_device(): lax.all_to_all(hold(sent, low), 'ctx', split_axis=0, concat_axis=0, tiled...  4.58 us
  transfers between devices with their start and end apart: 54, of which 18 were waited for; matrix products, arithmetic and copies ran while one was open for 1% of the time, Pallas kernels for 10%

profile of v2, /device:TPU:0, one launch (start us, length us, event | category | flops | bytes accessed | tf_op | source)
XLA Modules:
  0.0 189.9 jit_solution(8451529243020117561)
XLA Ops:
  0.7 0.7 convert_element_type.161
  1.3 0.7 pad_maximum_fusion
  2.7 2.7 %pack.1 = (bf16[4,112,448]{2,1,0:T(8,128)(2,1)}, bf16[208,768]{1,0:T(8,128)(2,1)}) custom-call(bf16[192,96]{1,0:T(8,128)(2,1)} %refs_0_.1, bf16[16,2,768]{2,1,0:T(2,128)(2,1)} %refs_1_.2, f32[16,8]{1,0:T(8,128)} %copy.36.refs_2_, bf16[64,2,768]{2,1,0:T(2,128)(2,1)} %refs_3_.1, bf16[96,192]{1,0:T(8,128)(2,1)} %refs_4_.1, bf16[96,192]{1,0:T(8,128)(2,1)} %refs_5_.1, ...), custom_call_target="tpu_custom_call" | custom-call | bytes 45000 | tf_op jit(solution)/shard_map/pack/pallas_call | solution.py:111
  5.4 2.9 %collective-permute-start = (bf16[208,768]{1,0:T(8,128)(2,1)}, bf16[208,768]{1,0:T(8,128)(2,1)S(1)}, u32[]{:S(2)}, u32[]{:S(2)}) collective-permute-start(bf16[208,768]{1,0:T(8,128)(2,1)} %get-tuple-element.77.refs_0_.refs_4_), channel_id=1, source_target_pairs={{0,8},{4,12},{8,0},{12,4},{16,24},{20,28},{24,16},{28,20},{1,9},{5... | collective-permute-start | bytes 958472 | tf_op jit(solution)/shard_map/ppermute | solution.py:23
  8.4 4.9 %all-to-all-start = ((bf16[4,112,448]{2,1,0:T(8,128)(2,1)}), bf16[4,112,448]{2,1,0:T(8,128)(2,1)S(1)}, u32[]{:S(2)}, u32[]{:S(2)}) async-start(bf16[4,112,448]{2,1,0:T(8,128)(2,1)} %get-tuple-element.78), calls=%async_computation | async-start | bytes 917504 | tf_op jit(solution)/shard_map/all_to_all | solution.py:52
  13.3 1.5 collective-permute-start.1
  15.3 1.0 collective-permute-done
  16.2 12.8 %collective-permute-done.1 = bf16[208,768]{1,0:T(8,128)(2,1)S(1)} collective-permute-done((bf16[208,768]{1,0:T(8,128)(2,1)}, bf16[208,768]{1,0:T(8,128)(2,1)S(1)}, u32[]{:S(2)}, u32[]{:S(2)}) %collective-permute-start.1) | collective-permute-done | bytes 319520 | tf_op jit(solution)/shard_map/ppermute | solution.py:23
  30.8 1.5 collective-permute-start.8
  32.4 1.4 collective-permute-start.9
  34.4 0.7 copy-done.51
  35.1 4.0 %project.1 = (bf16[128,192]{1,0:T(8,128)(2,1)}, bf16[8,2,64,384]{3,2,1,0:T(8,128)(2,1)}, bf16[128,768]{1,0:T(8,128)(2,1)}, bf16[768,576]{1,0:T(8,128)(2,1)}) custom-call(f32[1,768]{1,0:T(1,128)} %reshape.106.refs_0_.refs_5_.refs_1_, bf16[1,208,768]{2,1,0:T(8,128)(2,1)} %bitcast.63, bf16[1,208,768]{2,1,0:T(8,128)(2,1)} %bitcast.90, ...), custom_call_target="tpu_custom_call" | custom-call | bytes 120000 | tf_op jit(solution)/shard_map/project/pallas_call | solution.py:111
  42.2 0.7 copy.37.refs_1_
  43.7 1.0 copy-done
  45.1 0.7 copy-done.21
  46.4 4.7 %attend.1 = (f32[128,192]{1,0:T(8,128)}, bf16[192,128]{1,0:T(8,128)(2,1)}, f32[6,64,512]{2,1,0:T(8,128)}) custom-call(bf16[128,192]{1,0:T(8,128)(2,1)} %get-tuple-element.81.refs_1_.refs_0_.refs_2_.refs_7_, f32[32,12]{1,0:T(8,128)} %copy.37.refs_1_, s32[1,512]{1,0:T(1,128)} %bitcast.95, bf16[8,2,64,384]{3,2,1,0:T(8,128)(2,1)} %get-tuple-element.83.refs_3_.refs_8_, ...), custom_call_target="tpu_custom_call" | custom-call | bytes 144000 | tf_op jit(solution)/shard_map/attend/pallas_call | solution.py:111
  51.1 4.6 %all-to-all-start.1 = ((bf16[8,96,768]{2,1,0:T(8,128)(2,1)}), bf16[8,96,768]{2,1,0:T(8,128)(2,1)}, u32[]{:S(2)}, u32[]{:S(2)}) async-start(bf16[8,96,768]{2,1,0:T(8,128)(2,1)} %hold.9), calls=%async_computation.1 | async-start | bytes 2359296 | tf_op jit(solution)/shard_map/all_to_all | solution.py:831
  55.7 1.8 collective-permute-start.14
  57.6 2.4 %collective-permute-start.15 = (bf16[192,128]{1,0:T(8,128)(2,1)S(1)}, bf16[192,128]{1,0:T(8,128)(2,1)S(1)}, u32[]{:S(2)}, u32[]{:S(2)}) collective-permute-start(bf16[192,128]{1,0:T(8,128)(2,1)S(1)} %copy-done.20), channel_id=1, source_target_pairs={{0,2},{1,3},{2,0},{3,1},{4,6},{5,7},{6,4},{7,5},{8,10},{9,11},{10,... | collective-permute-start | bytes 147464 | tf_op jit(solution)/shard_map/ppermute | solution.py:23
  60.2 3.3 %collective-permute-done.15.refs_4_ = bf16[192,128]{1,0:T(8,128)(2,1)S(1)} collective-permute-done((bf16[192,128]{1,0:T(8,128)(2,1)S(1)}, bf16[192,128]{1,0:T(8,128)(2,1)S(1)}, u32[]{:S(2)}, u32[]{:S(2)}) %collective-permute-start.15) | collective-permute-done | bytes 49184 | tf_op jit(solution)/shard_map/ppermute | solution.py:23
  63.5 2.3 %collective-permute-done.16.refs_5_ = bf16[192,128]{1,0:T(8,128)(2,1)S(1)} collective-permute-done((bf16[192,128]{1,0:T(8,128)(2,1)S(1)}, bf16[192,128]{1,0:T(8,128)(2,1)S(1)}, u32[]{:S(2)}, u32[]{:S(2)}) %collective-permute-start.16) | collective-permute-done | bytes 49184 | tf_op jit(solution)/shard_map/ppermute | solution.py:23
  65.8 1.7 route.1
  67.5 0.7 copy-done.6
  68.3 1.6 collective-permute-start.17
  69.9 1.5 collective-permute-start.18
  71.8 7.0 %collective-permute-done.17 = bf16[96,1664]{1,0:T(8,128)(2,1)S(1)} collective-permute-done((bf16[96,1664]{1,0:T(8,128)(2,1)S(1)}, bf16[96,1664]{1,0:T(8,128)(2,1)S(1)}, u32[]{:S(2)}, u32[]{:S(2)}) %collective-permute-start.17) | collective-permute-done | bytes 319520 | tf_op jit(solution)/shard_map/ppermute | solution.py:23
  78.7 1.1 collective-permute-done.18
  79.8 6.1 %collective-permute-done.19 = bf16[96,1664]{1,0:T(8,128)(2,1)S(1)} collective-permute-done((bf16[96,1664]{1,0:T(8,128)(2,1)S(1)}, bf16[96,1664]{1,0:T(8,128)(2,1)S(1)}, u32[]{:S(2)}, u32[]{:S(2)}) %collective-permute-start.19) | collective-permute-done | bytes 319520 | tf_op jit(solution)/shard_map/ppermute | solution.py:23
  86.0 1.6 collective-permute-done.23.refs_7_
  88.3 7.7 %expert_back.1 = (bf16[384,1536]{1,0:T(8,128)(2,1)}, bf16[384,1536]{1,0:T(8,128)(2,1)}, bf16[768,384]{1,0:T(8,128)(2,1)}, bf16[768,384]{1,0:T(8,128)(2,1)}, bf16[768,384]{1,0:T(8,128)(2,1)}, /*index=5*/f32[768,8]{1,0:T(8,128)}) custom-call(bf16[1,96,1664]{2,1,0:T(8,128)(2,1)} %bitcast.65, bf16[1,96,1664]{2,1,0:T(8,128)(2,1)} %bitcast.77, ...), custom_call_target="tpu_custom_call" | custom-call | bytes 240000 | tf_op jit(solution)/shard_map/expert_back/pallas_call | solution.py:111
  96.3 2.9 %collective-permute-done.24 = bf16[4,96,1536]{2,1,0:T(8,128)(2,1)S(1)} collective-permute-done((bf16[4,96,1536]{2,1,0:T(8,128)(2,1)}, bf16[4,96,1536]{2,1,0:T(8,128)(2,1)S(1)}, u32[]{:S(2)}, u32[]{:S(2)}) %collective-permute-start.24) | collective-permute-done | bytes 1179680 | tf_op jit(solution)/shard_map/ppermute | solution.py:23
  99.2 1.5 fusion
  101.7 2.6 %collective-permute-start.27 = (bf16[96,1536]{1,0:T(8,128)(2,1)S(1)}, bf16[96,1536]{1,0:T(8,128)(2,1)S(1)}, u32[]{:S(2)}, u32[]{:S(2)}) collective-permute-start(bf16[96,1536]{1,0:T(8,128)(2,1)S(1)} %get-tuple-element.141), channel_id=1, source_target_pairs={{0,24},{4,28},{8,16},{12,20},{16,8},{20,12},{24,0},{28,4},{1,25},{... | collective-permute-start | bytes 884744 | tf_op jit(solution)/shard_map/ppermute | solution.py:23
  104.3 6.4 %collective-permute-done.25.refs_1_ = bf16[96,1536]{1,0:T(8,128)(2,1)S(1)} collective-permute-done((bf16[96,1536]{1,0:T(8,128)(2,1)S(1)}, bf16[96,1536]{1,0:T(8,128)(2,1)S(1)}, u32[]{:S(2)}, u32[]{:S(2)}) %collective-permute-start.25) | collective-permute-done | bytes 294944 | tf_op jit(solution)/shard_map/ppermute | solution.py:23
  110.6 5.8 %collective-permute-done.26.refs_2_ = bf16[96,1536]{1,0:T(8,128)(2,1)S(1)} collective-permute-done((bf16[96,1536]{1,0:T(8,128)(2,1)S(1)}, bf16[96,1536]{1,0:T(8,128)(2,1)S(1)}, u32[]{:S(2)}, u32[]{:S(2)}) %collective-permute-start.26) | collective-permute-done | bytes 294944 | tf_op jit(solution)/shard_map/ppermute | solution.py:23
  116.5 1.0 sum_back.1
  117.5 4.8 %all-to-all-start.2 = ((bf16[4,120,768]{2,1,0:T(8,128)(2,1)}), bf16[4,120,768]{2,1,0:T(8,128)(2,1)S(1)}, u32[]{:S(2)}, u32[]{:S(2)}) async-start(bf16[4,120,768]{2,1,0:T(8,128)(2,1)} %get-tuple-element.92), calls=%async_computation.2 | async-start | bytes 1474560 | tf_op jit(solution)/shard_map/all_to_all | solution.py:52
  122.3 4.7 %expert_weights.1 = (bf16[96,768]{1,0:T(8,128)(2,1)}, bf16[96,768]{1,0:T(8,128)(2,1)}, bf16[96,768]{1,0:T(8,128)(2,1)}, bf16[96,768]{1,0:T(8,128)(2,1)}, bf16[96...) custom-call(bf16[1,96,1664]{2,1,0:T(8,128)(2,1)} %bitcast.66, ...), custom_call_target="tpu_custom_call" | custom-call | bytes 120000 | tf_op jit(solution)/shard_map/expert_weights/pallas_call | solution.py:111
  127.0 1.5 collective-permute-start.29
  128.9 1.2 collective-permute-start.31
  130.6 1.5 collective-permute-start.33
  132.0 1.9 %collective-permute-done.29.refs_2_ = bf16[96,768]{1,0:T(8,128)(2,1)S(1)} collective-permute-done((bf16[96,768]{1,0:T(8,128)(2,1)}, bf16[96,768]{1,0:T(8,128)(2,1)S(1)}, u32[]{:S(2)}, u32[]{:S(2)}) %collective-permute-start.29) | collective-permute-done | bytes 147488 | tf_op jit(solution)/shard_map/ppermute | solution.py:23
  134.2 4.6 %expert_rest.1 = (f32[384,768]{1,0:T(8,128)}, f32[8,768]{1,0:T(8,128)}) custom-call(bf16[1,96,1664]{2,1,0:T(8,128)(2,1)} %bitcast.67, bf16[1,96,1664]{2,1,0:T(8,128)(2,1)} %bitcast.79, bf16[1,96,1664]{2,1,0:T(8,128)(2,1)} %bitcast.83, bf16[1,96,1664]{2,1,0:T(8,128)(2,1)} %bitcast.87, bf16[1,96,1664]{2,1,0:T(8,128)(2,1)} %copy-done.42, ...), custom_call_target="tpu_custom_call" | custom-call | bytes 90000 | tf_op jit(solution)/shard_map/expert_rest/pallas_call | solution.py:111
  138.8 5.3 %collective-permute-done.32.refs_5_ = bf16[96,768]{1,0:T(8,128)(2,1)S(1)} collective-permute-done((bf16[96,768]{1,0:T(8,128)(2,1)}, bf16[96,768]{1,0:T(8,128)(2,1)S(1)}, u32[]{:S(2)}, u32[]{:S(2)}) %collective-permute-start.32) | collective-permute-done | bytes 147488 | tf_op jit(solution)/shard_map/ppermute | solution.py:23
  144.1 1.6 widen.1
  146.6 6.0 %attend_back.1 = (f32[32,768]{1,0:T(8,128)}, bf16[128,192]{1,0:T(8,128)(2,1)}, bf16[4,128,384]{2,1,0:T(8,128)(2,1)}, bf16[4,128,384]{2,1,0:T(8,128)(2,1)}, bf16[...) custom-call(bf16[4,120,768]{2,1,0:T(8,128)(2,1)} %copy-done.1, f32[128,768]{1,0:T(8,128)} %copy-done.6, ...), custom_call_target="tpu_custom_call" | custom-call | bytes 240000 | tf_op jit(solution)/shard_map/attend_back/pallas_call | solution.py:111
  153.1 1.6 collective-permute-done.35
  154.7 1.2 fusion.11
  155.9 1.6 collective-permute-start.36
  158.0 1.5 collective-permute-start.38
  159.7 1.3 table.1
  161.0 1.1 mix.1
  162.1 2.2 %collective-permute-done.37.refs_11_ = bf16[128,384]{1,0:T(8,128)(2,1)S(1)} collective-permute-done((bf16[128,384]{1,0:T(8,128)(2,1)S(1)}, bf16[128,384]{1,0:T(8,128)(2,1)S(1)}, u32[]{:S(2)}, u32[]{:S(2)}) %collective-permute-start.37) | collective-permute-done | bytes 98336 | tf_op jit(solution)/shard_map/ppermute | solution.py:23
  164.4 1.2 back_project.1
  165.6 3.8 %collective-permute-start.45 = (f32[8,768]{1,0:T(8,128)S(1)}, f32[8,768]{1,0:T(8,128)S(1)}, u32[]{:S(2)}, u32[]{:S(2)}) collective-permute-start(f32[8,768]{1,0:T(8,128)S(1)} %get-tuple-element.128), channel_id=1, source_target_pairs={{0,3},{1,2},{2,1},{3,0},{4,7},{5,6},{6,5},{7,4},{8,11},{9,10},{10,... | collective-permute-start | bytes 73736 | tf_op jit(solution)/shard_map/ppermute | solution.py:23
  170.0 5.2 %all-to-all-start.3 = ((bf16[4,32,768]{2,1,0:T(8,128)(2,1)}), bf16[4,32,768]{2,1,0:T(8,128)(2,1)S(1)}, u32[]{:S(2)}, u32[]{:S(2)}) async-start(bf16[4,32,768]{2,1,0:T(8,128)(2,1)} %get-tuple-element.125), calls=%async_computation.3 | async-start | bytes 393216 | tf_op jit(solution)/shard_map/all_to_all | solution.py:52
  176.0 1.2 collective-permute-start.41
  177.2 1.8 collective-permute-start.42
  179.0 1.2 collective-permute-done.46
  180.7 1.2 collective-permute-start.48
  181.9 2.3 %collective-permute-done.47.refs_9_ = f32[8,768]{1,0:T(8,128)S(1)} collective-permute-done((f32[8,768]{1,0:T(8,128)S(1)}, f32[8,768]{1,0:T(8,128)S(1)}, u32[]{:S(2)}, u32[]{:S(2)}) %collective-permute-start.47) | collective-permute-done | bytes 24608 | tf_op jit(solution)/shard_map/ppermute | solution.py:23
  184.2 1.2 collective-permute-start.49
  185.5 3.5 %collective-permute-done.49.refs_11_ = f32[8,768]{1,0:T(8,128)S(1)} collective-permute-done((f32[8,768]{1,0:T(8,128)S(1)}, f32[8,768]{1,0:T(8,128)S(1)}, u32[]{:S(2)}, u32[]{:S(2)}) %collective-permute-start.49) | collective-permute-done | bytes 24608 | tf_op jit(solution)/shard_map/ppermute | solution.py:23
  189.0 0.9 last.1
  (193 shorter events, 16.0 us)
Async XLA Ops:
  0.6 33.2 %copy-start.54 = (f32[768]{0:T(1024)S(1)}, f32[768]{0:T(1024)}, u32[]{:S(2)}) copy-start(f32[768]{0:T(1024)} %param.18) | copy-start | bytes 9220
  5.4 10.8 %collective-permute-start = (bf16[208,768]{1,0:T(8,128)(2,1)}, bf16[208,768]{1,0:T(8,128)(2,1)S(1)}, u32[]{:S(2)}, u32[]{:S(2)}) collective-permute-start(bf16[208,768]{1,0:T(8,128)(2,1)} %get-tuple-element.77.refs_0_.refs_4_), channel_id=1, source_target_pairs={{0,8},{4,12},{8,0},{12,4},{16,24},{20,28},{24,16},{28,20},{1,9},{5... | collective-permute-start | bytes 958472 | tf_op jit(solution)/shard_map/ppermute | solution.py:23
  8.4 21.2 %all-to-all-start = ((bf16[4,112,448]{2,1,0:T(8,128)(2,1)}), bf16[4,112,448]{2,1,0:T(8,128)(2,1)S(1)}, u32[]{:S(2)}, u32[]{:S(2)}) async-start(bf16[4,112,448]{2,1,0:T(8,128)(2,1)} %get-tuple-element.78), calls=%async_computation | async-start | bytes 917504 | tf_op jit(solution)/shard_map/all_to_all | solution.py:52
  13.3 15.8 %collective-permute-start.1 = (bf16[208,768]{1,0:T(8,128)(2,1)}, bf16[208,768]{1,0:T(8,128)(2,1)S(1)}, u32[]{:S(2)}, u32[]{:S(2)}) collective-permute-start(bf16[208,768]{1,0:T(8,128)(2,1)} %get-tuple-element.77.refs_0_.refs_4_), channel_id=1, source_target_pairs={{0,16},{4,20},{8,24},{12,28},{16,0},{20,4},{24,8},{28,12},{1,17},{... | collective-permute-start | bytes 958472 | tf_op jit(solution)/shard_map/ppermute | solution.py:23
  14.8 14.3 %collective-permute-start.2 = (bf16[208,768]{1,0:T(8,128)(2,1)}, bf16[208,768]{1,0:T(8,128)(2,1)S(1)}, u32[]{:S(2)}, u32[]{:S(2)}) collective-permute-start(bf16[208,768]{1,0:T(8,128)(2,1)} %get-tuple-element.77.refs_0_.refs_4_), channel_id=1, source_target_pairs={{0,24},{4,28},{8,16},{12,20},{16,8},{20,12},{24,0},{28,4},{1,25},{... | collective-permute-start | bytes 958472 | tf_op jit(solution)/shard_map/ppermute | solution.py:23
  15.3 15.6 %collective-permute-start.3 = (bf16[1,208,768]{2,1,0:T(8,128)(2,1)}, bf16[1,208,768]{2,1,0:T(8,128)(2,1)S(1)}, u32[]{:S(2)}, u32[]{:S(2)}) collective-permute-start(bf16[1,208,768]{2,1,0:T(8,128)(2,1)} %bitcast.62), channel_id=1, source_target_pairs={{0,4},{4,0},{8,12},{12,8},{16,20},{20,16},{24,28},{28,24},{1,5},{5... | collective-permute-start | bytes 958472 | tf_op jit(solution)/shard_map/ppermute | solution.py:23
  16.2 18.2 %copy-start.46 = (bf16[208,768]{1,0:T(8,128)(2,1)}, bf16[208,768]{1,0:T(8,128)(2,1)S(1)}, u32[]{:S(2)}) copy-start(bf16[208,768]{1,0:T(8,128)(2,1)S(1)} %collective-permute-done) | copy-start | bytes 958468
  16.2 16.1 %collective-permute-start.4 = (bf16[1,208,768]{2,1,0:T(8,128)(2,1)S(1)}, bf16[1,208,768]{2,1,0:T(8,128)(2,1)S(1)}, u32[]{:S(2)}, u32[]{:S(2)}) collective-permute-start(bf16[1,208,768]{2,1,0:T(8,128)(2,1)S(1)} %bitcast.89), channel_id=1, source_target_pairs={{0,4},{4,0},{8,12},{12,8},{16,20},{20,16},{24,28},{28,24},{1,5},{5... | collective-permute-start | bytes 958472 | tf_op jit(solution)/shard_map/ppermute | solution.py:23
  29.0 5.4 %collective-permute-start.5 = (bf16[1,208,768]{2,1,0:T(8,128)(2,1)S(1)}, bf16[1,208,768]{2,1,0:T(8,128)(2,1)S(1)}, u32[]{:S(2)}, u32[]{:S(2)}) collective-permute-start(bf16[1,208,768]{2,1,0:T(8,128)(2,1)S(1)} %bitcast.91), channel_id=1, source_target_pairs={{0,4},{4,0},{8,12},{12,8},{16,20},{20,16},{24,28},{28,24},{1,5},{5... | collective-permute-start | bytes 958472 | tf_op jit(solution)/shard_map/ppermute | solution.py:23
  29.1 5.3 %collective-permute-start.6 = (bf16[1,208,768]{2,1,0:T(8,128)(2,1)S(1)}, bf16[1,208,768]{2,1,0:T(8,128)(2,1)}, u32[]{:S(2)}, u32[]{:S(2)}) collective-permute-start(bf16[1,208,768]{2,1,0:T(8,128)(2,1)S(1)} %bitcast.93), channel_id=1, source_target_pairs={{0,4},{4,0},{8,12},{12,8},{16,20},{20,16},{24,28},{28,24},{1,5},{5... | collective-permute-start | bytes 958472 | tf_op jit(solution)/shard_map/ppermute | solution.py:23
  30.3 35.5 %copy-start.9 = (bf16[128,768]{1,0:T(8,128)(2,1)}, bf16[128,768]{1,0:T(8,128)(2,1)S(1)}, u32[]{:S(2)}) copy-start(bf16[128,768]{1,0:T(8,128)(2,1)S(1)} %get-tuple-element.86.refs_9_.refs_2_) | copy-start | bytes 589828
  30.3 8.9 %collective-permute-start.7 = (bf16[96,768]{1,0:T(8,128)(2,1)S(1)}, bf16[96,768]{1,0:T(8,128)(2,1)S(1)}, u32[]{:S(2)}, u32[]{:S(2)}) collective-permute-start(bf16[96,768]{1,0:T(8,128)(2,1)S(1)} %get-tuple-element.79), channel_id=1, source_target_pairs={{0,8},{4,12},{8,0},{12,4},{16,24},{20,28},{24,16},{28,20},{1,9},{5... | collective-permute-start | bytes 442376 | tf_op jit(solution)/shard_map/ppermute | solution.py:23
  30.8 9.0 %collective-permute-start.8 = (bf16[96,768]{1,0:T(8,128)(2,1)S(1)}, bf16[96,768]{1,0:T(8,128)(2,1)S(1)}, u32[]{:S(2)}, u32[]{:S(2)}) collective-permute-start(bf16[96,768]{1,0:T(8,128)(2,1)S(1)} %get-tuple-element.79), channel_id=1, source_target_pairs={{0,16},{4,20},{8,24},{12,28},{16,0},{20,4},{24,8},{28,12},{1,17},{... | collective-permute-start | bytes 442376 | tf_op jit(solution)/shard_map/ppermute | solution.py:23
  32.4 8.2 %collective-permute-start.9 = (bf16[96,768]{1,0:T(8,128)(2,1)S(1)}, bf16[96,768]{1,0:T(8,128)(2,1)S(1)}, u32[]{:S(2)}, u32[]{:S(2)}) collective-permute-start(bf16[96,768]{1,0:T(8,128)(2,1)S(1)} %get-tuple-element.79), channel_id=1, source_target_pairs={{0,24},{4,28},{8,16},{12,20},{16,8},{20,12},{24,0},{28,4},{1,25},{... | collective-permute-start | bytes 442376 | tf_op jit(solution)/shard_map/ppermute | solution.py:23
  41.2 3.5 %collective-permute-start.10 = (bf16[1,96,768]{2,1,0:T(8,128)(2,1)}, bf16[1,96,768]{2,1,0:T(8,128)(2,1)S(1)}, u32[]{:S(2)}, u32[]{:S(2)}) collective-permute-start(bf16[1,96,768]{2,1,0:T(8,128)(2,1)} %hold.5.refs_0_), channel_id=1, source_target_pairs={{0,4},{4,0},{8,12},{12,8},{16,20},{20,16},{24,28},{28,24},{1,5},{5... | collective-permute-start | bytes 442376 | tf_op jit(solution)/shard_map/ppermute | solution.py:23
  41.2 3.5 %collective-permute-start.11 = (bf16[1,96,768]{2,1,0:T(8,128)(2,1)}, bf16[1,96,768]{2,1,0:T(8,128)(2,1)S(1)}, u32[]{:S(2)}, u32[]{:S(2)}) collective-permute-start(bf16[1,96,768]{2,1,0:T(8,128)(2,1)} %hold.6.refs_1_), channel_id=1, source_target_pairs={{0,4},{4,0},{8,12},{12,8},{16,20},{20,16},{24,28},{28,24},{1,5},{5... | collective-permute-start | bytes 442376 | tf_op jit(solution)/shard_map/ppermute | solution.py:23
  41.7 3.0 %collective-permute-start.12 = (bf16[1,96,768]{2,1,0:T(8,128)(2,1)}, bf16[1,96,768]{2,1,0:T(8,128)(2,1)S(1)}, u32[]{:S(2)}, u32[]{:S(2)}) collective-permute-start(bf16[1,96,768]{2,1,0:T(8,128)(2,1)} %hold.7.refs_2_), channel_id=1, source_target_pairs={{0,4},{4,0},{8,12},{12,8},{16,20},{20,16},{24,28},{28,24},{1,5},{5... | collective-permute-start | bytes 442376 | tf_op jit(solution)/shard_map/ppermute | solution.py:23
  41.7 3.0 %collective-permute-start.13 = (bf16[1,96,768]{2,1,0:T(8,128)(2,1)}, bf16[1,96,768]{2,1,0:T(8,128)(2,1)S(1)}, u32[]{:S(2)}, u32[]{:S(2)}) collective-permute-start(bf16[1,96,768]{2,1,0:T(8,128)(2,1)} %hold.8.refs_3_), channel_id=1, source_target_pairs={{0,4},{4,0},{8,12},{12,8},{16,20},{20,16},{24,28},{28,24},{1,5},{5... | collective-permute-start | bytes 442376 | tf_op jit(solution)/shard_map/ppermute | solution.py:23
  51.1 14.7 %copy-start.3 = (bf16[208,768]{1,0:T(8,128)(2,1)S(1)}, bf16[208,768]{1,0:T(8,128)(2,1)}, u32[]{:S(2)}) copy-start(bf16[208,768]{1,0:T(8,128)(2,1)} %get-tuple-element.77.refs_0_.refs_4_) | copy-start | bytes 958468
  51.1 14.7 %copy-start.29 = (f32[8,128]{1,0:T(8,128)S(1)}, f32[8,128]{1,0:T(8,128)}, u32[]{:S(2)}) copy-start(f32[8,128]{1,0:T(8,128)} %copy-done.28) | copy-start | bytes 12292
  51.1 14.7 %copy-start.32 = (f32[768,4]{0,1:T(4,128)S(1)}, f32[768,4]{0,1:T(4,128)}, u32[]{:S(2)}) copy-start(f32[768,4]{0,1:T(4,128)} %param.26) | copy-start | bytes 36868
  51.1 36.4 %all-to-all-start.1 = ((bf16[8,96,768]{2,1,0:T(8,128)(2,1)}), bf16[8,96,768]{2,1,0:T(8,128)(2,1)}, u32[]{:S(2)}, u32[]{:S(2)}) async-start(bf16[8,96,768]{2,1,0:T(8,128)(2,1)} %hold.9), calls=%async_computation.1 | async-start | bytes 2359296 | tf_op jit(solution)/shard_map/all_to_all | solution.py:831
  55.7 4.5 %collective-permute-start.14 = (bf16[192,128]{1,0:T(8,128)(2,1)S(1)}, bf16[192,128]{1,0:T(8,128)(2,1)S(1)}, u32[]{:S(2)}, u32[]{:S(2)}) collective-permute-start(bf16[192,128]{1,0:T(8,128)(2,1)S(1)} %copy-done.20), channel_id=1, source_target_pairs={{0,1},{1,0},{2,3},{3,2},{4,5},{5,4},{6,7},{7,6},{8,9},{9,8},{10,11... | collective-permute-start | bytes 147464 | tf_op jit(solution)/shard_map/ppermute | solution.py:23
  57.6 6.0 %collective-permute-start.15 = (bf16[192,128]{1,0:T(8,128)(2,1)S(1)}, bf16[192,128]{1,0:T(8,128)(2,1)S(1)}, u32[]{:S(2)}, u32[]{:S(2)}) collective-permute-start(bf16[192,128]{1,0:T(8,128)(2,1)S(1)} %copy-done.20), channel_id=1, source_target_pairs={{0,2},{1,3},{2,0},{3,1},{4,6},{5,7},{6,4},{7,5},{8,10},{9,11},{10,... | collective-permute-start | bytes 147464 | tf_op jit(solution)/shard_map/ppermute | solution.py:23
  59.9 5.9 %collective-permute-start.16 = (bf16[192,128]{1,0:T(8,128)(2,1)S(1)}, bf16[192,128]{1,0:T(8,128)(2,1)S(1)}, u32[]{:S(2)}, u32[]{:S(2)}) collective-permute-start(bf16[192,128]{1,0:T(8,128)(2,1)S(1)} %copy-done.20), channel_id=1, source_target_pairs={{0,3},{1,2},{2,1},{3,0},{4,7},{5,6},{6,5},{7,4},{8,11},{9,10},{10,... | collective-permute-start | bytes 147464 | tf_op jit(solution)/shard_map/ppermute | solution.py:23
  60.2 35.9 %copy-start.34 = (f32[1,768]{1,0:T(1,128)}, f32[1,768]{1,0:T(1,128)S(1)}, u32[]{:S(2)}) copy-start(f32[1,768]{1,0:T(1,128)S(1)} %reshape.108.refs_6_.refs_3_) | copy-start | bytes 9220
  68.3 19.3 %copy-start.5 = (bf16[96,1664]{1,0:T(8,128)(2,1)}, bf16[96,1664]{1,0:T(8,128)(2,1)S(1)}, u32[]{:S(2)}) copy-start(bf16[96,1664]{1,0:T(8,128)(2,1)S(1)} %get-tuple-element.89) | copy-start | bytes 958468
  68.3 10.5 %collective-permute-start.17 = (bf16[96,1664]{1,0:T(8,128)(2,1)S(1)}, bf16[96,1664]{1,0:T(8,128)(2,1)S(1)}, u32[]{:S(2)}, u32[]{:S(2)}) collective-permute-start(bf16[96,1664]{1,0:T(8,128)(2,1)S(1)} %get-tuple-element.89), channel_id=1, source_target_pairs={{0,8},{4,12},{8,0},{12,4},{16,24},{20,28},{24,16},{28,20},{1,9},{5... | collective-permute-start | bytes 958472 | tf_op jit(solution)/shard_map/ppermute | solution.py:23
  69.9 9.9 %collective-permute-start.18 = (bf16[96,1664]{1,0:T(8,128)(2,1)S(1)}, bf16[96,1664]{1,0:T(8,128)(2,1)S(1)}, u32[]{:S(2)}, u32[]{:S(2)}) collective-permute-start(bf16[96,1664]{1,0:T(8,128)(2,1)S(1)} %get-tuple-element.89), channel_id=1, source_target_pairs={{0,16},{4,20},{8,24},{12,28},{16,0},{20,4},{24,8},{28,12},{1,17},{... | collective-permute-start | bytes 958472 | tf_op jit(solution)/shard_map/ppermute | solution.py:23
  71.4 14.6 %collective-permute-start.19 = (bf16[96,1664]{1,0:T(8,128)(2,1)S(1)}, bf16[96,1664]{1,0:T(8,128)(2,1)S(1)}, u32[]{:S(2)}, u32[]{:S(2)}) collective-permute-start(bf16[96,1664]{1,0:T(8,128)(2,1)S(1)} %get-tuple-element.89), channel_id=1, source_target_pairs={{0,24},{4,28},{8,16},{12,20},{16,8},{20,12},{24,0},{28,4},{1,25},{... | collective-permute-start | bytes 958472 | tf_op jit(solution)/shard_map/ppermute | solution.py:23
  71.8 14.2 %collective-permute-start.20 = (bf16[1,96,1664]{2,1,0:T(8,128)(2,1)S(1)}, bf16[1,96,1664]{2,1,0:T(8,128)(2,1)S(1)}, u32[]{:S(2)}, u32[]{:S(2)}) collective-permute-start(bf16[1,96,1664]{2,1,0:T(8,128)(2,1)S(1)} %bitcast.64), channel_id=1, source_target_pairs={{0,4},{4,0},{8,12},{12,8},{16,20},{20,16},{24,28},{28,24},{1,5},{5... | collective-permute-start | bytes 958472 | tf_op jit(solution)/shard_map/ppermute | solution.py:23
  78.7 7.2 %collective-permute-start.21 = (bf16[1,96,1664]{2,1,0:T(8,128)(2,1)S(1)}, bf16[1,96,1664]{2,1,0:T(8,128)(2,1)S(1)}, u32[]{:S(2)}, u32[]{:S(2)}) collective-permute-start(bf16[1,96,1664]{2,1,0:T(8,128)(2,1)S(1)} %bitcast.76), channel_id=1, source_target_pairs={{0,4},{4,0},{8,12},{12,8},{16,20},{20,16},{24,28},{28,24},{1,5},{5... | collective-permute-start | bytes 958472 | tf_op jit(solution)/shard_map/ppermute | solution.py:23
  79.8 6.2 %collective-permute-start.22 = (bf16[1,96,1664]{2,1,0:T(8,128)(2,1)S(1)}, bf16[1,96,1664]{2,1,0:T(8,128)(2,1)S(1)}, u32[]{:S(2)}, u32[]{:S(2)}) collective-permute-start(bf16[1,96,1664]{2,1,0:T(8,128)(2,1)S(1)} %bitcast.80), channel_id=1, source_target_pairs={{0,4},{4,0},{8,12},{12,8},{16,20},{20,16},{24,28},{28,24},{1,5},{5... | collective-permute-start | bytes 958472 | tf_op jit(solution)/shard_map/ppermute | solution.py:23
  86.0 1.6 collective-permute-start.23
  96.1 3.1 %collective-permute-start.24 = (bf16[4,96,1536]{2,1,0:T(8,128)(2,1)}, bf16[4,96,1536]{2,1,0:T(8,128)(2,1)S(1)}, u32[]{:S(2)}, u32[]{:S(2)}) collective-permute-start(bf16[4,96,1536]{2,1,0:T(8,128)(2,1)} %bitcast.101), channel_id=1, source_target_pairs={{0,4},{4,0},{8,12},{12,8},{16,20},{20,16},{24,28},{28,24},{1,5},{5... | collective-permute-start | bytes 3538952 | tf_op jit(solution)/shard_map/ppermute | solution.py:23
  100.7 9.9 %collective-permute-start.25 = (bf16[96,1536]{1,0:T(8,128)(2,1)S(1)}, bf16[96,1536]{1,0:T(8,128)(2,1)S(1)}, u32[]{:S(2)}, u32[]{:S(2)}) collective-permute-start(bf16[96,1536]{1,0:T(8,128)(2,1)S(1)} %get-tuple-element.143), channel_id=1, source_target_pairs={{0,8},{4,12},{8,0},{12,4},{16,24},{20,28},{24,16},{28,20},{1,9},{5... | collective-permute-start | bytes 884744 | tf_op jit(solution)/shard_map/ppermute | solution.py:23
  101.4 15.1 %collective-permute-start.26 = (bf16[96,1536]{1,0:T(8,128)(2,1)S(1)}, bf16[96,1536]{1,0:T(8,128)(2,1)S(1)}, u32[]{:S(2)}, u32[]{:S(2)}) collective-permute-start(bf16[96,1536]{1,0:T(8,128)(2,1)S(1)} %get-tuple-element.142), channel_id=1, source_target_pairs={{0,16},{4,20},{8,24},{12,28},{16,0},{20,4},{24,8},{28,12},{1,17},{... | collective-permute-start | bytes 884744 | tf_op jit(solution)/shard_map/ppermute | solution.py:23
  101.7 14.8 %collective-permute-start.27 = (bf16[96,1536]{1,0:T(8,128)(2,1)S(1)}, bf16[96,1536]{1,0:T(8,128)(2,1)S(1)}, u32[]{:S(2)}, u32[]{:S(2)}) collective-permute-start(bf16[96,1536]{1,0:T(8,128)(2,1)S(1)} %get-tuple-element.141), channel_id=1, source_target_pairs={{0,24},{4,28},{8,16},{12,20},{16,8},{20,12},{24,0},{28,4},{1,25},{... | collective-permute-start | bytes 884744 | tf_op jit(solution)/shard_map/ppermute | solution.py:23
  117.5 28.2 %all-to-all-start.2 = ((bf16[4,120,768]{2,1,0:T(8,128)(2,1)}), bf16[4,120,768]{2,1,0:T(8,128)(2,1)S(1)}, u32[]{:S(2)}, u32[]{:S(2)}) async-start(bf16[4,120,768]{2,1,0:T(8,128)(2,1)} %get-tuple-element.92), calls=%async_computation.2 | async-start | bytes 1474560 | tf_op jit(solution)/shard_map/all_to_all | solution.py:52
  127.0 3.6 %collective-permute-start.28 = (bf16[96,768]{1,0:T(8,128)(2,1)}, bf16[96,768]{1,0:T(8,128)(2,1)S(1)}, u32[]{:S(2)}, u32[]{:S(2)}) collective-permute-start(bf16[96,768]{1,0:T(8,128)(2,1)} %get-tuple-element.100), channel_id=1, source_target_pairs={{0,4},{4,0},{8,12},{12,8},{16,20},{20,16},{24,28},{28,24},{1,5},{5... | collective-permute-start | bytes 442376 | tf_op jit(solution)/shard_map/ppermute | solution.py:23
  127.0 6.9 %collective-permute-start.29 = (bf16[96,768]{1,0:T(8,128)(2,1)}, bf16[96,768]{1,0:T(8,128)(2,1)S(1)}, u32[]{:S(2)}, u32[]{:S(2)}) collective-permute-start(bf16[96,768]{1,0:T(8,128)(2,1)} %get-tuple-element.101), channel_id=1, source_target_pairs={{0,8},{4,12},{8,0},{12,4},{16,24},{20,28},{24,16},{28,20},{1,9},{5... | collective-permute-start | bytes 442376 | tf_op jit(solution)/shard_map/ppermute | solution.py:23
  128.5 10.2 %collective-permute-start.30 = (bf16[96,768]{1,0:T(8,128)(2,1)}, bf16[96,768]{1,0:T(8,128)(2,1)S(1)}, u32[]{:S(2)}, u32[]{:S(2)}) collective-permute-start(bf16[96,768]{1,0:T(8,128)(2,1)} %get-tuple-element.102), channel_id=1, source_target_pairs={{0,12},{4,8},{8,4},{12,0},{16,28},{20,24},{24,20},{28,16},{1,13},{... | collective-permute-start | bytes 442376 | tf_op jit(solution)/shard_map/ppermute | solution.py:23
  128.9 9.9 %collective-permute-start.31 = (bf16[96,768]{1,0:T(8,128)(2,1)}, bf16[96,768]{1,0:T(8,128)(2,1)S(1)}, u32[]{:S(2)}, u32[]{:S(2)}) collective-permute-start(bf16[96,768]{1,0:T(8,128)(2,1)} %get-tuple-element.103), channel_id=1, source_target_pairs={{0,16},{4,20},{8,24},{12,28},{16,0},{20,4},{24,8},{28,12},{1,17},{... | collective-permute-start | bytes 442376 | tf_op jit(solution)/shard_map/ppermute | solution.py:23
  130.1 14.0 %collective-permute-start.32 = (bf16[96,768]{1,0:T(8,128)(2,1)}, bf16[96,768]{1,0:T(8,128)(2,1)S(1)}, u32[]{:S(2)}, u32[]{:S(2)}) collective-permute-start(bf16[96,768]{1,0:T(8,128)(2,1)} %get-tuple-element.104), channel_id=1, source_target_pairs={{0,20},{4,16},{8,28},{12,24},{16,4},{20,0},{24,12},{28,8},{1,21},{... | collective-permute-start | bytes 442376 | tf_op jit(solution)/shard_map/ppermute | solution.py:23
  130.6 13.5 %collective-permute-start.33 = (bf16[96,768]{1,0:T(8,128)(2,1)}, bf16[96,768]{1,0:T(8,128)(2,1)S(1)}, u32[]{:S(2)}, u32[]{:S(2)}) collective-permute-start(bf16[96,768]{1,0:T(8,128)(2,1)} %get-tuple-element.105), channel_id=1, source_target_pairs={{0,24},{4,28},{8,16},{12,20},{16,8},{20,12},{24,0},{28,4},{1,25},{... | collective-permute-start | bytes 442376 | tf_op jit(solution)/shard_map/ppermute | solution.py:23
  133.9 10.2 %collective-permute-start.34 = (bf16[96,768]{1,0:T(8,128)(2,1)}, bf16[96,768]{1,0:T(8,128)(2,1)S(1)}, u32[]{:S(2)}, u32[]{:S(2)}) collective-permute-start(bf16[96,768]{1,0:T(8,128)(2,1)} %get-tuple-element.106), channel_id=1, source_target_pairs={{0,28},{4,24},{8,20},{12,16},{16,12},{20,8},{24,4},{28,0},{1,29},{... | collective-permute-start | bytes 442376 | tf_op jit(solution)/shard_map/ppermute | solution.py:23
  134.2 9.9 %copy-start.25 = (bf16[96,768]{1,0:T(8,128)(2,1)S(1)}, bf16[96,768]{1,0:T(8,128)(2,1)}, u32[]{:S(2)}) copy-start(bf16[96,768]{1,0:T(8,128)(2,1)} %get-tuple-element.99.refs_0_) | copy-start | bytes 442372
  152.6 2.0 %collective-permute-start.35 = (bf16[4,128,384]{2,1,0:T(8,128)(2,1)}, bf16[4,128,384]{2,1,0:T(8,128)(2,1)S(1)}, u32[]{:S(2)}, u32[]{:S(2)}) collective-permute-start(bf16[4,128,384]{2,1,0:T(8,128)(2,1)} %get-tuple-element.113), channel_id=1, source_target_pairs={{0,4},{4,0},{8,12},{12,8},{16,20},{20,16},{24,28},{28,24},{1,5},{5... | collective-permute-start | bytes 1179656 | tf_op jit(solution)/shard_map/ppermute | solution.py:23
  155.9 6.2 %collective-permute-start.36 = (bf16[128,384]{1,0:T(8,128)(2,1)S(1)}, bf16[128,384]{1,0:T(8,128)(2,1)S(1)}, u32[]{:S(2)}, u32[]{:S(2)}) collective-permute-start(bf16[128,384]{1,0:T(8,128)(2,1)S(1)} %get-tuple-element.151), channel_id=1, source_target_pairs={{0,8},{4,12},{8,0},{12,4},{16,24},{20,28},{24,16},{28,20},{1,9},{5... | collective-permute-start | bytes 294920 | tf_op jit(solution)/shard_map/ppermute | solution.py:23
  157.4 6.9 %collective-permute-start.37 = (bf16[128,384]{1,0:T(8,128)(2,1)S(1)}, bf16[128,384]{1,0:T(8,128)(2,1)S(1)}, u32[]{:S(2)}, u32[]{:S(2)}) collective-permute-start(bf16[128,384]{1,0:T(8,128)(2,1)S(1)} %get-tuple-element.150), channel_id=1, source_target_pairs={{0,16},{4,20},{8,24},{12,28},{16,0},{20,4},{24,8},{28,12},{1,17},{... | collective-permute-start | bytes 294920 | tf_op jit(solution)/shard_map/ppermute | solution.py:23
  158.0 6.4 %collective-permute-start.38 = (bf16[128,384]{1,0:T(8,128)(2,1)S(1)}, bf16[128,384]{1,0:T(8,128)(2,1)S(1)}, u32[]{:S(2)}, u32[]{:S(2)}) collective-permute-start(bf16[128,384]{1,0:T(8,128)(2,1)S(1)} %get-tuple-element.149), channel_id=1, source_target_pairs={{0,24},{4,28},{8,16},{12,20},{16,8},{20,12},{24,0},{28,4},{1,25},{... | collective-permute-start | bytes 294920 | tf_op jit(solution)/shard_map/ppermute | solution.py:23
  165.6 9.6 %collective-permute-start.39 = (bf16[4,96,768]{2,1,0:T(8,128)(2,1)S(1)}, bf16[4,96,768]{2,1,0:T(8,128)(2,1)S(1)}, u32[]{:S(2)}, u32[]{:S(2)}) collective-permute-start(bf16[4,96,768]{2,1,0:T(8,128)(2,1)S(1)} %get-tuple-element.127), channel_id=1, source_target_pairs={{0,4},{4,0},{8,12},{12,8},{16,20},{20,16},{24,28},{28,24},{1,5},{5... | collective-permute-start | bytes 1769480 | tf_op jit(solution)/shard_map/ppermute | solution.py:23
  165.6 11.6 %collective-permute-start.45 = (f32[8,768]{1,0:T(8,128)S(1)}, f32[8,768]{1,0:T(8,128)S(1)}, u32[]{:S(2)}, u32[]{:S(2)}) collective-permute-start(f32[8,768]{1,0:T(8,128)S(1)} %get-tuple-element.128), channel_id=1, source_target_pairs={{0,3},{1,2},{2,1},{3,0},{4,7},{5,6},{6,5},{7,4},{8,11},{9,10},{10,... | collective-permute-start | bytes 73736 | tf_op jit(solution)/shard_map/ppermute | solution.py:23
  169.4 9.5 %collective-permute-start.44 = (f32[8,768]{1,0:T(8,128)S(1)}, f32[8,768]{1,0:T(8,128)S(1)}, u32[]{:S(2)}, u32[]{:S(2)}) collective-permute-start(f32[8,768]{1,0:T(8,128)S(1)} %get-tuple-element.128), channel_id=1, source_target_pairs={{0,2},{1,3},{2,0},{3,1},{4,6},{5,7},{6,4},{7,5},{8,10},{9,11},{10,... | collective-permute-start | bytes 73736 | tf_op jit(solution)/shard_map/ppermute | solution.py:23
  169.4 9.5 %collective-permute-start.43 = (f32[8,768]{1,0:T(8,128)S(1)}, f32[8,768]{1,0:T(8,128)S(1)}, u32[]{:S(2)}, u32[]{:S(2)}) collective-permute-start(f32[8,768]{1,0:T(8,128)S(1)} %get-tuple-element.128), channel_id=1, source_target_pairs={{0,1},{1,0},{2,3},{3,2},{4,5},{5,4},{6,7},{7,6},{8,9},{9,8},{10,11... | collective-permute-start | bytes 73736 | tf_op jit(solution)/shard_map/ppermute | solution.py:23
  170.0 19.0 %copy-start.27 = (f32[32,768]{1,0:T(8,128)S(1)}, f32[32,768]{1,0:T(8,128)}, u32[]{:S(2)}) copy-start(f32[32,768]{1,0:T(8,128)} %get-tuple-element.115.refs_2_) | copy-start | bytes 294916
  170.0 19.0 %all-to-all-start.3 = ((bf16[4,32,768]{2,1,0:T(8,128)(2,1)}), bf16[4,32,768]{2,1,0:T(8,128)(2,1)S(1)}, u32[]{:S(2)}, u32[]{:S(2)}) async-start(bf16[4,32,768]{2,1,0:T(8,128)(2,1)} %get-tuple-element.125), calls=%async_computation.3 | async-start | bytes 393216 | tf_op jit(solution)/shard_map/all_to_all | solution.py:52
  175.4 13.6 %collective-permute-start.40 = (bf16[96,768]{1,0:T(8,128)(2,1)S(1)}, bf16[96,768]{1,0:T(8,128)(2,1)S(1)}, u32[]{:S(2)}, u32[]{:S(2)}) collective-permute-start(bf16[96,768]{1,0:T(8,128)(2,1)S(1)} %get-tuple-element.147), channel_id=1, source_target_pairs={{0,8},{4,12},{8,0},{12,4},{16,24},{20,28},{24,16},{28,20},{1,9},{5... | collective-permute-start | bytes 442376 | tf_op jit(solution)/shard_map/ppermute | solution.py:23
  176.0 13.0 %collective-permute-start.41 = (bf16[96,768]{1,0:T(8,128)(2,1)S(1)}, bf16[96,768]{1,0:T(8,128)(2,1)S(1)}, u32[]{:S(2)}, u32[]{:S(2)}) collective-permute-start(bf16[96,768]{1,0:T(8,128)(2,1)S(1)} %get-tuple-element.146), channel_id=1, source_target_pairs={{0,16},{4,20},{8,24},{12,28},{16,0},{20,4},{24,8},{28,12},{1,17},{... | collective-permute-start | bytes 442376 | tf_op jit(solution)/shard_map/ppermute | solution.py:23
  177.2 11.8 %collective-permute-start.42 = (bf16[96,768]{1,0:T(8,128)(2,1)S(1)}, bf16[96,768]{1,0:T(8,128)(2,1)S(1)}, u32[]{:S(2)}, u32[]{:S(2)}) collective-permute-start(bf16[96,768]{1,0:T(8,128)(2,1)S(1)} %get-tuple-element.145), channel_id=1, source_target_pairs={{0,24},{4,28},{8,16},{12,20},{16,8},{20,12},{24,0},{28,4},{1,25},{... | collective-permute-start | bytes 442376 | tf_op jit(solution)/shard_map/ppermute | solution.py:23
  178.9 1.3 collective-permute-start.46
  180.2 4.0 %collective-permute-start.47 = (f32[8,768]{1,0:T(8,128)S(1)}, f32[8,768]{1,0:T(8,128)S(1)}, u32[]{:S(2)}, u32[]{:S(2)}) collective-permute-start(f32[8,768]{1,0:T(8,128)S(1)} %add.71.refs_8_), channel_id=1, source_target_pairs={{0,8},{4,12},{8,0},{12,4},{16,24},{20,28},{24,16},{28,20},{1,9},{5... | collective-permute-start | bytes 73736 | tf_op jit(solution)/shard_map/ppermute | solution.py:23
  180.7 4.7 %collective-permute-start.48 = (f32[8,768]{1,0:T(8,128)S(1)}, f32[8,768]{1,0:T(8,128)S(1)}, u32[]{:S(2)}, u32[]{:S(2)}) collective-permute-start(f32[8,768]{1,0:T(8,128)S(1)} %add.71.refs_8_), channel_id=1, source_target_pairs={{0,16},{4,20},{8,24},{12,28},{16,0},{20,4},{24,8},{28,12},{1,17},{... | collective-permute-start | bytes 73736 | tf_op jit(solution)/shard_map/ppermute | solution.py:23
  184.2 4.7 %collective-permute-start.49 = (f32[8,768]{1,0:T(8,128)S(1)}, f32[8,768]{1,0:T(8,128)S(1)}, u32[]{:S(2)}, u32[]{:S(2)}) collective-permute-start(f32[8,768]{1,0:T(8,128)S(1)} %add.71.refs_8_), channel_id=1, source_target_pairs={{0,24},{4,28},{8,16},{12,20},{16,8},{20,12},{24,0},{28,4},{1,25},{... | collective-permute-start | bytes 73736 | tf_op jit(solution)/shard_map/ppermute | solution.py:23
  (47 other events, 168.7 us)

commit v3 on v2

--- a/solution.py
+++ b/solution.py
@@ -23,14 +23,34 @@
     return lax.ppermute(value, axis, [(i, i ^ bits) for i in range(devices)])
 
 
+def hold_with_token(value, *after):
+    def body(*refs):
+        refs[-1][...] = jnp.zeros(refs[-1].shape, F32)
+
+    return pl.pallas_call(
+        body,
+        out_shape=[
+            jax.ShapeDtypeStruct(value.shape, value.dtype),
+            jax.ShapeDtypeStruct((8, LANES), F32),
+        ],
+        in_specs=[pl.BlockSpec(memory_space=pl.ANY)] * (1 + len(after)),
+        out_specs=[pl.BlockSpec(memory_space=pl.ANY), pl.BlockSpec(memory_space=pltpu.VMEM)],
+        input_output_aliases={0: 0},
+        name="hold",
+    )(value, *after)
+
+
 def gather_ctx(value, after=()):
     devices = lax.axis_size("ctx")
     near = [value[None]] + [swap(value, "ctx", 2 * j)[None] for j in range(1, devices // 2)]
+    tokens = []
     if after:
-        near = [hold(block, *after) for block in near]
+        held = [hold_with_token(block, *after) for block in near[1:]]
+        near, tokens = near[:1] + [block for block, _ in held], [token for _, token in held]
     if devices > 8:
         near = [jnp.concatenate(near, axis=0)]
-    return near + [swap(block, "ctx", 1) for block in near]
+    blocks = near + [swap(block, "ctx", 1) for block in near]
+    return (blocks, tokens) if after else blocks
 
 
 def each_block(refs):
@@ -89,13 +109,9 @@
     outs = ([outs] if single else outs) + ([((8, LANES), F32)] if token else [])
     single = len(outs) == 1
     specs = [pl.BlockSpec(memory_space=pltpu.VMEM)] * len(args)
-    specs += [
-        pl.BlockSpec(memory_space=pltpu.VMEM if room(a.shape, a.dtype) <= 2**16 else pl.ANY)
-        for a in after
-    ]
+    specs += [pl.BlockSpec(memory_space=pl.ANY)] * len(after)
     shapes = [jax.ShapeDtypeStruct(*o) for o in outs]
     out_specs = [pl.BlockSpec(memory_space=pltpu.VMEM)] * len(shapes)
-
     held = sum(room(a.shape, a.dtype) for a in (*args, *shapes))
     held += sum(room(a.shape, a.dtype) for a in scratch)
     limit = min(62 * 2**20, max(16 * 2**20 + 2 * held, 60 * 2**20 if wide else 0))
@@ -226,13 +242,14 @@
         out[c, :, hidden:] = up[:, c * hidden : (c + 1) * hidden]
 
 
-def early_body(tok, quarter, *refs):
-    pieces, cot_out, info_out, mats_out = refs
+def early_body(tok, quarter, cap, *refs):
+    pieces, cot_out, info_out, both_out = refs
     exp_pos = lax.axis_index("exp")
     parts = pieces.shape[0]
     rows = 2 * tok
     third = cot_out.shape[1] // 3
-    shard = mats_out.shape[0]
+    slots = parts * cap
+    shard = both_out.shape[0] - slots
     info = jnp.zeros((16, rows), F32)
     for z in range(parts):
         for s in range(2):
@@ -246,27 +263,51 @@
         target = (lane // quarter) * tok + z * quarter + lane % quarter
         spot = jnp.where((target == row) & (lane < 2 * quarter), 1.0, 0.0).astype(BF16)
         info = info + nn(pieces[z, pieces.shape[1] - 16 :, :LANES], spot)
-    mats_out[...] = jnp.concatenate(
+    both_out[slots:, :] = jnp.concatenate(
         [pieces[exp_pos ^ d, :shard, third:] for d in range(parts)], axis=1
     )
     low = info[0:4] + (info[4:8] + info[8:12])
     info_out[...] = jnp.concatenate([low, jnp.zeros((4, rows), F32)], axis=0)
-
-
-def lay_rows(refs, out):
+    before = block_before(rows, tok, quarter)
+    route0, route1 = low[0:1].astype(jnp.int32), low[1:2].astype(jnp.int32)
+    hot, _ = slot_hot(route0, route1, exp_pos, before, tok, quarter, cap, parts)
+    both_out[:slots, :] = nn(jnp.where(hot, 1.0, 0.0).astype(BF16), cot_out[...]).astype(BF16)
+
+
+def lay_rows(refs, out, lead=0):
     if len(refs) == 1:
         out[...] = refs[0][...]
         return
     ctx_pos = lax.axis_index("ctx")
     for ref, i, d in each_block(refs):
-        rows = ref.shape[1]
-        out[pl.ds(pl.multiple_of((ctx_pos ^ d) * rows, rows), rows), :] = ref[i]
-
-
-def lay_body(*refs):
+        rows = ref.shape[1] - lead
+        out[pl.ds(pl.multiple_of((ctx_pos ^ d) * rows, rows), rows), :] = ref[i, lead:, :]
+
+
+def lay_body(lead, *refs):
     blocks, (mats_out, own_out) = refs[:-2], refs[-2:]
-    lay_rows(blocks, mats_out)
+    lay_rows(blocks, mats_out, lead)
     own_out[...] = mats_out[:, : own_out.shape[1]]
+
+
+def fold_lanes(value):
+    rows, cols = value.shape
+    if cols % LANES != LANES // 2:
+        return value
+    whole = [value[:, c : c + LANES] for c in range(0, cols - LANES // 2, LANES)]
+    tail = value[:, cols - LANES // 2 :]
+    tail = jnp.concatenate([tail[: rows // 2], tail[rows // 2 :]], axis=1)
+    return jnp.concatenate(whole + [tail], axis=0)
+
+
+def unfold_lanes(value, rows, cols):
+    if cols % LANES != LANES // 2:
+        return value
+    count = cols // LANES
+    whole = [value[c * rows : (c + 1) * rows] for c in range(count)]
+    tail = value[count * rows :]
+    tail = jnp.concatenate([tail[:, : LANES // 2], tail[:, LANES // 2 :]], axis=0)
+    return jnp.concatenate(whole + [tail], axis=1)
 
 
 def project_body(hl, tok, folded, gain, *refs):
@@ -292,7 +333,7 @@
     for lead in range(0, len(listed), 4):
         group = listed[lead : lead + 4]
         x = jnp.concatenate([ref[i, :rows, :] for ref, i, _ in group], axis=0).astype(F32)
-        normed = (x * rms_scale(x) * gain[...]).astype(BF16)
+        normed = (x * rms_scale(x) * gain[...].reshape(1, -1)).astype(BF16)
         full = nn(normed, w[...] if lead == 0 else w[:, hl:]).astype(BF16)
         if lead == 0:
             a_out[...] = normed[:rows]
@@ -302,26 +343,6 @@
             kv_out[ctx_pos ^ d] = full[t * rows : (t + 1) * rows].reshape(2, tok, 2 * hl)
 
 
-def fold_lanes(value):
-    rows, cols = value.shape
-    if cols % LANES != LANES // 2:
-        return value
-    whole = [value[:, c : c + LANES] for c in range(0, cols - LANES // 2, LANES)]
-    tail = value[:, cols - LANES // 2 :]
-    tail = jnp.concatenate([tail[: rows // 2], tail[rows // 2 :]], axis=1)
-    return jnp.concatenate(whole + [tail], axis=0)
-
-
-def unfold_lanes(value, rows, cols):
-    if cols % LANES != LANES // 2:
-        return value
-    count = cols // LANES
-    whole = [value[c * rows : (c + 1) * rows] for c in range(count)]
-    tail = value[count * rows :]
-    tail = jnp.concatenate([tail[:, : LANES // 2], tail[:, LANES // 2 :]], axis=0)
-    return jnp.concatenate(whole + [tail], axis=1)
-
-
 def attend_body(heads, q, table, rev, kv_out, o_out, low_out, p_out):
     ctx_pos, exp_pos = lax.axis_index("ctx"), lax.axis_index("exp")
     rows = q.shape[0]
@@ -329,11 +350,11 @@
     hl = heads * HD
     seq_len = rev.shape[1]
     start = ctx_pos * tok
-    buckets, head_total = table.shape
+    head_total, buckets = table.shape
     pick = jnp.where(
         iota((8, head_total), 1) == exp_pos * heads + iota((8, head_total), 0), 1.0, 0.0
     )
-    own_table = nt(pick, table[...], HIGH)
+    own_table = nn(pick, table[...], HIGH)
     hot = jnp.where(iota((buckets, seq_len), 0) == rev[...], 1.0, 0.0)
     bias = pltpu.roll(nn(own_table, hot, HIGH), start + 1, 1)
     open_keys = iota((tok, seq_len), 1) <= start + iota((tok, seq_len), 0)
@@ -378,9 +399,9 @@
 def route_body(tok, quarter, cap, parts, *refs):
     x, mats = refs[:2]
     lows = refs[2 : 2 + parts]
-    gain, router_t, info_ref, cot, resid_out, gates_out, slots_out = refs[2 + parts :]
+    gain, router_t, info_ref, resid_out, gates_out, slots_out = refs[2 + parts :]
     exp_pos = lax.axis_index("exp")
-    rows, width = 2 * tok, gain.shape[1]
+    rows, width = 2 * tok, gain.shape[0]
     attn = nt(
         jnp.concatenate(
             [unfold_lanes(low[...], rows, mats.shape[1] // parts) for low in lows], axis=1
@@ -392,7 +413,7 @@
             x[s * tok : (s + 1) * tok, :].astype(F32) + attn[s * tok : (s + 1) * tok]
         )
     resid = resid_out[...]
-    normed = (resid * rms_scale(resid) * gain[...]).astype(BF16)
+    normed = (resid * rms_scale(resid) * gain[...].reshape(1, -1)).astype(BF16)
     logits = nt(router_t[...], normed.astype(F32), HIGH)
     info = info_ref[...]
     soft0, soft1 = gate_values(logits, info)
@@ -412,13 +433,12 @@
         axis=0,
     ).astype(BF16)
     slots_out[:, :width] = nn(hot, normed).astype(BF16)
-    slots_out[:, width : width + LANES] = nt(hot, extras).astype(BF16)
-    slots_out[:, width + LANES :] = nn(hot, cot[...]).astype(BF16)
+    slots_out[:, width:] = nt(hot, extras).astype(BF16)
 
 
 def expert_back_body(count, *refs):
-    xs = refs[:count]
-    w_in, down, router_t, near_out, far_out, hid, dg_out, du_out, spread_out = refs[count:]
+    xs, cs = refs[:count], refs[count : 2 * count]
+    w_in, down, router_t, near_out, far_out, hid, dg_out, du_out, spread_out = refs[2 * count :]
     exp_pos = lax.axis_index("exp")
     width, hidden = w_in.shape[0], down.shape[0]
     experts = router_t.shape[0]
@@ -426,9 +446,9 @@
     down_w = down[...]
     done = 0
     side = near_out.shape[0]
-    for x_group in grouped(xs):
+    for x_group, c_group in zip(grouped(xs), grouped(cs)):
         rows = stack(x_group, cols=slice(0, width))
-        extras = stack(x_group, cols=slice(width, width + LANES)).astype(F32)
+        extras = stack(x_group, cols=slice(width, None)).astype(F32)
         step = rows.shape[0]
         part = slice(done, done + step)
         done = done + step
@@ -437,7 +457,7 @@
         other = extras[:, 4:5].astype(jnp.int32)
         pre = nn(rows, gate_w)
         up = nn(rows, up_w)
-        raw = nt(stack(x_group, cols=slice(width + LANES, None)), down_w)
+        raw = nt(stack(c_group, slice(0, xs[0].shape[1])), down_w)
         squared = pre * pre
         tanh = jnp.tanh(GELU_C * (pre + GELU_A * pre * squared))
         half = 0.5 * (1.0 + tanh)
@@ -488,18 +508,18 @@
 
 
 def expert_rest_body(count, *refs):
-    xs = refs[:count]
-    hid, spread, down_out, router_out = refs[count:]
+    xs, cs = refs[:count], refs[count : 2 * count]
+    hid, spread, down_out, router_out = refs[2 * count :]
     width = down_out.shape[1]
     down_sum, router_sum = 0.0, 0.0
     done = 0
-    for x_group in grouped(xs):
+    for x_group, c_group in zip(grouped(xs), grouped(cs)):
         rows = stack(x_group, cols=slice(0, width))
-        extras = stack(x_group, cols=slice(width, width + LANES)).astype(F32)
+        extras = stack(x_group, cols=slice(width, None)).astype(F32)
         part = slice(done, done + rows.shape[0])
         done = done + rows.shape[0]
         gate = extras[:, 0:1] + extras[:, 1:2]
-        cot = stack(x_group, cols=slice(width + LANES, None))
+        cot = stack(c_group, slice(0, xs[0].shape[1]))
         dy = (gate * cot.astype(F32)).astype(BF16)
         down_sum = down_sum + tn(hid[part, :], dy)
         router_sum = router_sum + tn(spread[part, :], rows.astype(F32), HIGH)
@@ -574,7 +594,7 @@
     small_out[...] = jnp.broadcast_to(
         jnp.sum(grad * centred, axis=0, keepdims=True) * (1.0 / parts), small_out.shape
     )
-    inner = grad * gain[...]
+    inner = grad * gain[...].reshape(1, -1)
     held[...] = cot[...].astype(F32) + scale * (
         inner - centred * jnp.mean(inner * centred, axis=-1, keepdims=True)
     )
@@ -688,7 +708,7 @@
 
 def finish_body(tok, quarter, x, gain, own, pieces, out):
     exp_pos = lax.axis_index("exp")
-    width = gain.shape[1]
+    width = gain.shape[0]
     for s in range(2):
         spot = pl.ds(pl.multiple_of(s * tok + exp_pos * quarter, quarter), quarter)
         rows = x[spot, :].astype(F32)
@@ -698,7 +718,7 @@
             grad = grad + pieces[z, here, :].astype(F32)
         scale = rms_scale(rows)
         centred = rows * scale
-        inner = grad * gain[...]
+        inner = grad * gain[...].reshape(1, -1)
         out[:, s, :] = own[here, :] + scale * (
             inner - centred * jnp.mean(inner * centred, axis=-1, keepdims=True)
         )
@@ -758,7 +778,7 @@
     half = ctx_size // 2
     seq_len = tok * ctx_size
     aligned = shard % 16 == 0
-    gain_one, gain_two = attn_gain.reshape(1, width), ffn_gain.reshape(1, width)
+    gain_one, gain_two = attn_gain, ffn_gain
     router_t = router_weight.T
     rev = buckets[::-1].reshape(1, seq_len)
     down = down_weight.reshape(hidden, width)
@@ -780,13 +800,13 @@
         packed = jnp.concatenate([query_weight, key_weight, value_weight], axis=1)
         x_blocks = x_blocks + [lax.all_gather(packed, "ctx", axis=0, tiled=True)]
     cot_packs = trade_exp(cot_pack)
-    cot_block, info_block, mats = call(
-        functools.partial(early_body, tok, quarter),
+    cot_block, info_block, both_slots = call(
+        functools.partial(early_body, tok, quarter, cap),
         "early_slots",
         [
             ((rows, width), BF16),
             ((8, rows), F32),
-            ((shard, parts * hl), BF16),
+            ((slots + shard, width), BF16),
         ],
         cot_packs,
     )
@@ -801,9 +821,13 @@
         ],
         gain_one, *x_blocks, us=4.0, after=[info_block], wide=True,
     )
-    mats_blocks = (
-        gather_ctx(mats, [q]) if aligned else [lax.all_gather(mats, "ctx", axis=0, tiled=True)]
-    )
+    if aligned:
+        c_blocks = gather_ctx(both_slots)
+        moved = c_blocks[1:half]
+        mats_blocks, mats_lead = c_blocks, slots
+    else:
+        c_blocks, moved = gather_ctx(both_slots[:slots]), []
+        mats_blocks, mats_lead = [lax.all_gather(both_slots[slots:], "ctx", axis=0, tiled=True)], 0
 
     sent = call(
         functools.partial(sent_body, hidden),
@@ -812,20 +836,16 @@
         gate_weight.reshape(shard, ctx_size * hidden), up_weight.reshape(shard, ctx_size * hidden),
         us=2.0, after=[q],
     )
-    mats_full, out_t, laid = call(
-        lay_body, "lay_out", [((width, parts * hl), BF16), ((width, hl), BF16)], *mats_blocks,
-        us=2.5, token=True,
+    mats_full, out_t = call(
+        functools.partial(lay_body, mats_lead), "lay_out", [((width, parts * hl), BF16), ((width, hl), BF16)], *mats_blocks,
+        us=2.5,
     )
     low_shape = (rows * hl // LANES, LANES) if hl % LANES == LANES // 2 else (rows, hl)
     o, low, p = call(
         functools.partial(attend_body, heads),
         "attend",
-        [
-            ((rows, hl), F32),
-            (low_shape, BF16),
-            ((seqs * heads, tok, seq_len), F32),
-        ],
-        q, bias_table, rev, kv_all, us=4.8, after=[laid], wide=True,
+        [((rows, hl), F32), (low_shape, BF16), ((seqs * heads, tok, seq_len), F32)],
+        q, bias_table.T, rev, kv_all, us=4.8, after=moved, wide=True,
     )
     lows = spread_exp(low)
     w_in = lax.all_to_all(hold(sent, low), "ctx", split_axis=0, concat_axis=0, tiled=True)
@@ -834,8 +854,8 @@
     resid, gates, x_slots = call(
         functools.partial(route_body, tok, quarter, cap, parts),
         "route",
-        [((rows, width), F32), ((8, rows), F32), ((slots, 2 * width + LANES), BF16)],
-        x, mats_full, *lows, gain_two, router_t, info_block, cot_block, us=3.7,
+        [((rows, width), F32), ((8, rows), F32), ((slots, width + LANES), BF16)],
+        x, mats_full, *lows, gain_two, router_t, info_block, us=3.7,
     )
     x_blocks = gather_ctx(x_slots)
     side = half * slots
@@ -844,7 +864,7 @@
         functools.partial(expert_back_body, cut),
         "expert_back",
         [((side, 2 * width), BF16)] * 2 + [((2 * side, hidden), BF16)] * 3 + [((2 * side, 8), F32)],
-        *x_blocks, w_in, down, router_t, us=8.0, wide=True,
+        *x_blocks, *c_blocks, w_in, down, router_t, us=8.0, wide=True,
     )
     back_terms = send_direct(
         add_pair(
@@ -864,14 +884,14 @@
         functools.partial(expert_weights_body, cut),
         "expert_weights",
         [(w_shape, BF16)] * ctx_size if by_permutes else [((ctx_size, *w_shape), BF16)],
-        *x_blocks, dg, du, us=4.0, after=[summed], wide=True, token=True,
+        *x_blocks, dg, du, us=4.0, after=[summed], token=True,
         scratch=[pltpu.VMEM((ctx_size, *w_shape), BF16)],
     )
     down_grad, router = call(
         functools.partial(expert_rest_body, cut),
         "expert_rest",
         [((hidden, width), F32), ((8, width), F32)],
-        *x_blocks, hid, spread, us=3.0, after=[weighed], wide=True,
+        *x_blocks, *c_blocks, hid, spread, us=3.0, after=[weighed],
     )
     if by_permutes:
         w_back = [w_grads[0]] + [swap(w_grads[d], "ctx", d) for d in range(1, ctx_size)]

time: 191 us -> 185 us (0.969)
  Pallas kernels: 43.7 us -> 39.8 us
    pallas_call x17, Pallas kernels: 43.7 us -> 39.8 us  [call(): pl.pallas_call(run, out_shape=shapes[0] if single else shapes, in_specs=s...]
    unnamed x115 -> x148, local copies, waits for them, and re-layouts: 8.94 us -> 8.5 us
  transfers between devices with their start and end apart: 54 -> 54, of which waited for: 18 -> 20; matrix products, arithmetic and copies ran while one was open for 1% -> 1% of each run, Pallas kernels for 10% -> 8%
where the time goes in v3:
time: 185 us; the launch traced here: 184 us
  waiting for transfers between devices  66.6 us (36%)
  starting transfers between devices  61.8 us (33%)
  Pallas kernels  39.8 us (22%)
  local copies, waits for them, and re-layouts  9.99 us (5%)
  other arithmetic  4.32 us (2%)
    ppermute x50, waiting for transfers between devices, swap(): return lax.ppermute(value, axis, [(i, i ^ bits) for i in range(devices)])  66.6 us
    ppermute x50, starting transfers between devices, swap(): return lax.ppermute(value, axis, [(i, i ^ bits) for i in range(devices)])  43 us
    pallas_call x17, Pallas kernels, call(): pl.pallas_call(run, out_shape=shapes[0] if single else shapes, in_specs=s...  39.8 us
    all_to_all x3, starting transfers between devices, trade_exp(): return lax.all_to_all(value, 'exp', split_axis=0, concat_axis=0, tiled=True)  14.2 us
    unnamed x148, local copies, waits for them, and re-layouts  8.5 us
    all_to_all x1, starting transfers between devices, on_device(): lax.all_to_all(hold(sent, low), 'ctx', split_axis=0, concat_axis=0, tiled...  4.57 us
  transfers between devices with their start and end apart: 54, of which 20 were waited for; matrix products, arithmetic and copies ran while one was open for 1% of the time, Pallas kernels for 8%

profile of v3, /device:TPU:0, one launch (start us, length us, event | category | flops | bytes accessed | tf_op | source)
XLA Modules:
  0.0 184.0 jit_solution(13754008357667485904)
XLA Ops:
  2.7 2.7 %pack.1 = (bf16[4,112,448]{2,1,0:T(8,128)(2,1)}, bf16[208,768]{1,0:T(8,128)(2,1)}) custom-call(bf16[192,96]{1,0:T(8,128)(2,1)} %refs_0_.2, bf16[16,2,768]{2,1,0:T(2,128)(2,1)} %refs_1_.2, f32[16,8]{1,0:T(8,128)} %copy.31.refs_2_, bf16[64,2,768]{2,1,0:T(2,128)(2,1)} %refs_3_.2, bf16[96,192]{1,0:T(8,128)(2,1)} %refs_4_.1, bf16[96,192]{1,0:T(8,128)(2,1)} %refs_5_.2, ...), custom_call_target="tpu_custom_call" | custom-call | bytes 45000 | tf_op jit(solution)/shard_map/pack/pallas_call | solution.py:127
  5.4 2.9 %collective-permute-start.7 = (bf16[208,768]{1,0:T(8,128)(2,1)}, bf16[208,768]{1,0:T(8,128)(2,1)S(1)}, u32[]{:S(2)}, u32[]{:S(2)}) collective-permute-start(bf16[208,768]{1,0:T(8,128)(2,1)} %get-tuple-element.76.refs_0_.refs_4_), channel_id=1, source_target_pairs={{0,8},{4,12},{8,0},{12,4},{16,24},{20,28},{24,16},{28,20},{1,9},{5... | collective-permute-start | bytes 958472 | tf_op jit(solution)/shard_map/ppermute | solution.py:23
  8.4 4.9 %all-to-all-start = ((bf16[4,112,448]{2,1,0:T(8,128)(2,1)}), bf16[4,112,448]{2,1,0:T(8,128)(2,1)S(1)}, u32[]{:S(2)}, u32[]{:S(2)}) async-start(bf16[4,112,448]{2,1,0:T(8,128)(2,1)} %get-tuple-element.77), calls=%async_computation | async-start | bytes 917504 | tf_op jit(solution)/shard_map/all_to_all | solution.py:72
  13.3 1.5 collective-permute-start.8
  15.3 1.0 collective-permute-done.7
  16.2 12.8 %collective-permute-done.8 = bf16[208,768]{1,0:T(8,128)(2,1)S(1)} collective-permute-done((bf16[208,768]{1,0:T(8,128)(2,1)}, bf16[208,768]{1,0:T(8,128)(2,1)S(1)}, u32[]{:S(2)}, u32[]{:S(2)}) %collective-permute-start.8) | collective-permute-done | bytes 319520 | tf_op jit(solution)/shard_map/ppermute | solution.py:23
  31.8 1.5 collective-permute-start.1
  33.3 1.4 collective-permute-start.2
  35.5 4.1 %project.1 = (bf16[128,192]{1,0:T(8,128)(2,1)}, bf16[8,2,64,384]{3,2,1,0:T(8,128)(2,1)}, bf16[128,768]{1,0:T(8,128)(2,1)}, bf16[768,576]{1,0:T(8,128)(2,1)}) custom-call(f32[768]{0:T(1024)} %refs_1_.3, bf16[1,208,768]{2,1,0:T(8,128)(2,1)} %bitcast.64, bf16[1,208,768]{2,1,0:T(8,128)(2,1)} %bitcast.106, bf16[1,208,768]{2,1,0:T(8,128)(2,1)} %bitcast.108, ...), custom_call_target="tpu_custom_call" | custom-call | bytes 120000 | tf_op jit(solution)/shard_map/project/pallas_call | solution.py:127
  39.7 0.8 copy-done.47
  40.6 1.0 copy-done
  41.6 4.3 %collective-permute-done.1 = bf16[192,768]{1,0:T(8,128)(2,1)S(1)} collective-permute-done((bf16[192,768]{1,0:T(8,128)(2,1)S(1)}, bf16[192,768]{1,0:T(8,128)(2,1)S(1)}, u32[]{:S(2)}, u32[]{:S(2)}) %collective-permute-start.1) | collective-permute-done | bytes 294944 | tf_op jit(solution)/shard_map/ppermute | solution.py:23
  45.9 1.6 collective-permute-done.2
  48.3 4.7 %attend.1 = (f32[128,192]{1,0:T(8,128)}, bf16[192,128]{1,0:T(8,128)(2,1)}, f32[6,64,512]{2,1,0:T(8,128)}) custom-call(bf16[128,192]{1,0:T(8,128)(2,1)} %get-tuple-element.81.refs_0_.refs_2_.refs_7_, f32[12,32]{1,0:T(8,128)} %bitcast.114, s32[1,512]{1,0:T(1,128)} %bitcast.111, bf16[8,2,64,384]{3,2,1,0:T(8,128)(2,1)} %get-tuple-element.82.refs_3_.refs_8_, ...), custom_call_target="tpu_custom_call" | custom-call | bytes 144000 | tf_op jit(solution)/shard_map/attend/pallas_call | solution.py:127
  53.0 4.6 %all-to-all-start.1 = ((bf16[8,96,768]{2,1,0:T(8,128)(2,1)}), bf16[8,96,768]{2,1,0:T(8,128)(2,1)}, u32[]{:S(2)}, u32[]{:S(2)}) async-start(bf16[8,96,768]{2,1,0:T(8,128)(2,1)} %hold.1), calls=%async_computation.1 | async-start | bytes 2359296 | tf_op jit(solution)/shard_map/all_to_all | solution.py:851
  58.7 1.7 collective-permute-start.14
  60.5 2.4 %collective-permute-start.15 = (bf16[192,128]{1,0:T(8,128)(2,1)S(1)}, bf16[192,128]{1,0:T(8,128)(2,1)S(1)}, u32[]{:S(2)}, u32[]{:S(2)}) collective-permute-start(bf16[192,128]{1,0:T(8,128)(2,1)S(1)} %copy-done.48), channel_id=1, source_target_pairs={{0,2},{1,3},{2,0},{3,1},{4,6},{5,7},{6,4},{7,5},{8,10},{9,11},{10,... | collective-permute-start | bytes 147464 | tf_op jit(solution)/shard_map/ppermute | solution.py:23
  63.6 2.7 %collective-permute-done.15.refs_4_ = bf16[192,128]{1,0:T(8,128)(2,1)S(1)} collective-permute-done((bf16[192,128]{1,0:T(8,128)(2,1)S(1)}, bf16[192,128]{1,0:T(8,128)(2,1)S(1)}, u32[]{:S(2)}, u32[]{:S(2)}) %collective-permute-start.15) | collective-permute-done | bytes 49184 | tf_op jit(solution)/shard_map/ppermute | solution.py:23
  66.3 2.5 %collective-permute-done.16.refs_5_ = bf16[192,128]{1,0:T(8,128)(2,1)S(1)} collective-permute-done((bf16[192,128]{1,0:T(8,128)(2,1)S(1)}, bf16[192,128]{1,0:T(8,128)(2,1)S(1)}, u32[]{:S(2)}, u32[]{:S(2)}) %collective-permute-start.16) | collective-permute-done | bytes 49184 | tf_op jit(solution)/shard_map/ppermute | solution.py:23
  68.8 1.7 route.1
  70.5 0.8 copy-done.23
  71.3 1.7 collective-permute-start.17
  72.9 1.5 collective-permute-start.18
  74.7 3.8 %collective-permute-done.17 = bf16[96,896]{1,0:T(8,128)(2,1)S(1)} collective-permute-done((bf16[96,896]{1,0:T(8,128)(2,1)S(1)}, bf16[96,896]{1,0:T(8,128)(2,1)S(1)}, u32[]{:S(2)}, u32[]{:S(2)}) %collective-permute-start.17) | collective-permute-done | bytes 172064 | tf_op jit(solution)/shard_map/ppermute | solution.py:23
  78.6 3.2 %collective-permute-done.18 = bf16[96,896]{1,0:T(8,128)(2,1)S(1)} collective-permute-done((bf16[96,896]{1,0:T(8,128)(2,1)S(1)}, bf16[96,896]{1,0:T(8,128)(2,1)S(1)}, u32[]{:S(2)}, u32[]{:S(2)}) %collective-permute-start.18) | collective-permute-done | bytes 172064 | tf_op jit(solution)/shard_map/ppermute | solution.py:23
  82.3 0.9 collective-permute-done.22.refs_6_
  84.1 8.2 %expert_back.1 = (bf16[384,1536]{1,0:T(8,128)(2,1)}, bf16[384,1536]{1,0:T(8,128)(2,1)}, bf16[768,384]{1,0:T(8,128)(2,1)}, bf16[768,384]{1,0:T(8,128)(2,1)}, bf16[768,384]{1,0:T(8,128)(2,1)}, /*index=5*/f32[768,8]{1,0:T(8,128)}) custom-call(bf16[1,96,896]{2,1,0:T(8,128)(2,1)} %bitcast.85, bf16[1,96,896]{2,1,0:T(8,128)(2,1)} %bitcast.89, ...), custom_call_target="tpu_custom_call" | custom-call | bytes 240000 | tf_op jit(solution)/shard_map/expert_back/pallas_call | solution.py:127
  92.6 2.8 %collective-permute-done.24 = bf16[4,96,1536]{2,1,0:T(8,128)(2,1)S(1)} collective-permute-done((bf16[4,96,1536]{2,1,0:T(8,128)(2,1)}, bf16[4,96,1536]{2,1,0:T(8,128)(2,1)S(1)}, u32[]{:S(2)}, u32[]{:S(2)}) %collective-permute-start.24) | collective-permute-done | bytes 1179680 | tf_op jit(solution)/shard_map/ppermute | solution.py:23
  95.4 1.5 fusion
  97.4 1.1 collective-permute-start.26
  98.5 2.0 %collective-permute-start.27 = (bf16[96,1536]{1,0:T(8,128)(2,1)S(1)}, bf16[96,1536]{1,0:T(8,128)(2,1)S(1)}, u32[]{:S(2)}, u32[]{:S(2)}) collective-permute-start(bf16[96,1536]{1,0:T(8,128)(2,1)S(1)} %get-tuple-element.139), channel_id=1, source_target_pairs={{0,24},{4,28},{8,16},{12,20},{16,8},{20,12},{24,0},{28,4},{1,25},{... | collective-permute-start | bytes 884744 | tf_op jit(solution)/shard_map/ppermute | solution.py:23
  100.5 6.3 %collective-permute-done.25.refs_1_ = bf16[96,1536]{1,0:T(8,128)(2,1)S(1)} collective-permute-done((bf16[96,1536]{1,0:T(8,128)(2,1)S(1)}, bf16[96,1536]{1,0:T(8,128)(2,1)S(1)}, u32[]{:S(2)}, u32[]{:S(2)}) %collective-permute-start.25) | collective-permute-done | bytes 294944 | tf_op jit(solution)/shard_map/ppermute | solution.py:23
  106.8 6.2 %collective-permute-done.27.refs_3_ = bf16[96,1536]{1,0:T(8,128)(2,1)S(1)} collective-permute-done((bf16[96,1536]{1,0:T(8,128)(2,1)S(1)}, bf16[96,1536]{1,0:T(8,128)(2,1)S(1)}, u32[]{:S(2)}, u32[]{:S(2)}) %collective-permute-start.27) | collective-permute-done | bytes 294944 | tf_op jit(solution)/shard_map/ppermute | solution.py:23
  113.1 1.1 sum_back.1
  114.2 4.1 %all-to-all-start.2 = ((bf16[4,120,768]{2,1,0:T(8,128)(2,1)}), bf16[4,120,768]{2,1,0:T(8,128)(2,1)S(1)}, u32[]{:S(2)}, u32[]{:S(2)}) async-start(bf16[4,120,768]{2,1,0:T(8,128)(2,1)} %get-tuple-element.89), calls=%async_computation.2 | async-start | bytes 1474560 | tf_op jit(solution)/shard_map/all_to_all | solution.py:72
  118.4 1.1 copy-done.43
  119.5 1.7 expert_weights.1
  121.3 1.5 collective-permute-start.29
  123.2 1.2 collective-permute-start.31
  124.9 1.5 collective-permute-start.33
  126.4 1.6 collective-permute-done.29.refs_2_
  128.4 1.1 copy-done.46
  129.5 2.8 %expert_rest.1 = (f32[384,768]{1,0:T(8,128)}, f32[8,768]{1,0:T(8,128)S(1)}) custom-call(bf16[1,96,896]{2,1,0:T(8,128)(2,1)S(1)} %bitcast.87, bf16[1,96,896]{2,1,0:T(8,128)(2,1)S(1)} %bitcast.91, bf16[1,96,896]{2,1,0:T(8,128)(2,1)S(1)} %bitcast.95, bf16[1,96,896]{2,1,0:T(8,128)(2,1)S(1)} %bitcast.99, bf16[1,96,896]{2,1,0:T(8,128)(2,1)S(1)} %copy-done.34, ...), custom_call_target="tpu_custom_call" | custom-call | bytes 90000 | tf_op jit(solution)/shard_map/expert_rest/pallas_call | solution.py:127
  132.3 5.9 %collective-permute-done.32.refs_5_ = bf16[96,768]{1,0:T(8,128)(2,1)S(1)} collective-permute-done((bf16[96,768]{1,0:T(8,128)(2,1)S(1)}, bf16[96,768]{1,0:T(8,128)(2,1)S(1)}, u32[]{:S(2)}, u32[]{:S(2)}) %collective-permute-start.32) | collective-permute-done | bytes 147488 | tf_op jit(solution)/shard_map/ppermute | solution.py:23
  138.2 1.6 widen.1
  140.6 6.0 %attend_back.1 = (f32[32,768]{1,0:T(8,128)}, bf16[128,192]{1,0:T(8,128)(2,1)}, bf16[4,128,384]{2,1,0:T(8,128)(2,1)}, bf16[4,128,384]{2,1,0:T(8,128)(2,1)}, bf16[...) custom-call(bf16[4,120,768]{2,1,0:T(8,128)(2,1)} %copy-done.1, f32[128,768]{1,0:T(8,128)} %copy-done.23, ...), custom_call_target="tpu_custom_call" | custom-call | bytes 240000 | tf_op jit(solution)/shard_map/attend_back/pallas_call | solution.py:127
  147.2 1.6 collective-permute-done.35
  148.7 1.2 fusion.11
  150.0 1.6 collective-permute-start.36
  152.1 1.4 collective-permute-start.38
  153.8 1.3 table.1
  155.1 1.1 mix.1
  156.2 2.2 %collective-permute-done.37.refs_11_ = bf16[128,384]{1,0:T(8,128)(2,1)S(1)} collective-permute-done((bf16[128,384]{1,0:T(8,128)(2,1)S(1)}, bf16[128,384]{1,0:T(8,128)(2,1)S(1)}, u32[]{:S(2)}, u32[]{:S(2)}) %collective-permute-start.37) | collective-permute-done | bytes 98336 | tf_op jit(solution)/shard_map/ppermute | solution.py:23
  158.5 1.2 back_project.1
  159.7 3.8 %collective-permute-start.45 = (f32[8,768]{1,0:T(8,128)S(1)}, f32[8,768]{1,0:T(8,128)S(1)}, u32[]{:S(2)}, u32[]{:S(2)}) collective-permute-start(f32[8,768]{1,0:T(8,128)S(1)} %get-tuple-element.126), channel_id=1, source_target_pairs={{0,3},{1,2},{2,1},{3,0},{4,7},{5,6},{6,5},{7,4},{8,11},{9,10},{10,... | collective-permute-start | bytes 73736 | tf_op jit(solution)/shard_map/ppermute | solution.py:23
  164.1 5.2 %all-to-all-start.3 = ((bf16[4,32,768]{2,1,0:T(8,128)(2,1)}), bf16[4,32,768]{2,1,0:T(8,128)(2,1)S(1)}, u32[]{:S(2)}, u32[]{:S(2)}) async-start(bf16[4,32,768]{2,1,0:T(8,128)(2,1)} %get-tuple-element.123), calls=%async_computation.3 | async-start | bytes 393216 | tf_op jit(solution)/shard_map/all_to_all | solution.py:72
  170.1 1.2 collective-permute-start.41
  171.2 1.8 collective-permute-start.42
  173.1 1.2 collective-permute-done.46
  174.8 1.2 collective-permute-start.48
  176.0 2.3 %collective-permute-done.47.refs_9_ = f32[8,768]{1,0:T(8,128)S(1)} collective-permute-done((f32[8,768]{1,0:T(8,128)S(1)}, f32[8,768]{1,0:T(8,128)S(1)}, u32[]{:S(2)}, u32[]{:S(2)}) %collective-permute-start.47) | collective-permute-done | bytes 24608 | tf_op jit(solution)/shard_map/ppermute | solution.py:23
  178.3 1.2 collective-permute-start.49
  179.6 3.5 %collective-permute-done.49.refs_11_ = f32[8,768]{1,0:T(8,128)S(1)} collective-permute-done((f32[8,768]{1,0:T(8,128)S(1)}, f32[8,768]{1,0:T(8,128)S(1)}, u32[]{:S(2)}, u32[]{:S(2)}) %collective-permute-start.49) | collective-permute-done | bytes 24608 | tf_op jit(solution)/shard_map/ppermute | solution.py:23
  183.1 0.9 last.1
  (220 shorter events, 16.7 us)
Async XLA Ops:
  0.6 34.1 %copy-start.73 = (s32[512]{0:T(512)S(1)}, s32[512]{0:T(512)}, u32[]{:S(2)}) copy-start(s32[512]{0:T(512)} %param.24) | copy-start | bytes 6148
  5.4 10.8 %collective-permute-start.7 = (bf16[208,768]{1,0:T(8,128)(2,1)}, bf16[208,768]{1,0:T(8,128)(2,1)S(1)}, u32[]{:S(2)}, u32[]{:S(2)}) collective-permute-start(bf16[208,768]{1,0:T(8,128)(2,1)} %get-tuple-element.76.refs_0_.refs_4_), channel_id=1, source_target_pairs={{0,8},{4,12},{8,0},{12,4},{16,24},{20,28},{24,16},{28,20},{1,9},{5... | collective-permute-start | bytes 958472 | tf_op jit(solution)/shard_map/ppermute | solution.py:23
  8.4 21.2 %all-to-all-start = ((bf16[4,112,448]{2,1,0:T(8,128)(2,1)}), bf16[4,112,448]{2,1,0:T(8,128)(2,1)S(1)}, u32[]{:S(2)}, u32[]{:S(2)}) async-start(bf16[4,112,448]{2,1,0:T(8,128)(2,1)} %get-tuple-element.77), calls=%async_computation | async-start | bytes 917504 | tf_op jit(solution)/shard_map/all_to_all | solution.py:72
  13.3 15.8 %collective-permute-start.8 = (bf16[208,768]{1,0:T(8,128)(2,1)}, bf16[208,768]{1,0:T(8,128)(2,1)S(1)}, u32[]{:S(2)}, u32[]{:S(2)}) collective-permute-start(bf16[208,768]{1,0:T(8,128)(2,1)} %get-tuple-element.76.refs_0_.refs_4_), channel_id=1, source_target_pairs={{0,16},{4,20},{8,24},{12,28},{16,0},{20,4},{24,8},{28,12},{1,17},{... | collective-permute-start | bytes 958472 | tf_op jit(solution)/shard_map/ppermute | solution.py:23
  14.8 14.3 %collective-permute-start.9 = (bf16[208,768]{1,0:T(8,128)(2,1)}, bf16[208,768]{1,0:T(8,128)(2,1)S(1)}, u32[]{:S(2)}, u32[]{:S(2)}) collective-permute-start(bf16[208,768]{1,0:T(8,128)(2,1)} %get-tuple-element.76.refs_0_.refs_4_), channel_id=1, source_target_pairs={{0,24},{4,28},{8,16},{12,20},{16,8},{20,12},{24,0},{28,4},{1,25},{... | collective-permute-start | bytes 958472 | tf_op jit(solution)/shard_map/ppermute | solution.py:23
  15.3 16.6 %collective-permute-start.10 = (bf16[1,208,768]{2,1,0:T(8,128)(2,1)}, bf16[1,208,768]{2,1,0:T(8,128)(2,1)S(1)}, u32[]{:S(2)}, u32[]{:S(2)}) collective-permute-start(bf16[1,208,768]{2,1,0:T(8,128)(2,1)} %bitcast.63), channel_id=1, source_target_pairs={{0,4},{4,0},{8,12},{12,8},{16,20},{20,16},{24,28},{28,24},{1,5},{5... | collective-permute-start | bytes 958472 | tf_op jit(solution)/shard_map/ppermute | solution.py:23
  16.2 19.2 %copy-start.67 = (bf16[208,768]{1,0:T(8,128)(2,1)}, bf16[208,768]{1,0:T(8,128)(2,1)S(1)}, u32[]{:S(2)}) copy-start(bf16[208,768]{1,0:T(8,128)(2,1)S(1)} %collective-permute-done.7) | copy-start | bytes 958468
  16.2 17.1 %collective-permute-start.11 = (bf16[1,208,768]{2,1,0:T(8,128)(2,1)S(1)}, bf16[1,208,768]{2,1,0:T(8,128)(2,1)S(1)}, u32[]{:S(2)}, u32[]{:S(2)}) collective-permute-start(bf16[1,208,768]{2,1,0:T(8,128)(2,1)S(1)} %bitcast.105), channel_id=1, source_target_pairs={{0,4},{4,0},{8,12},{12,8},{16,20},{20,16},{24,28},{28,24},{1,5},{5... | collective-permute-start | bytes 958472 | tf_op jit(solution)/shard_map/ppermute | solution.py:23
  29.0 6.4 %collective-permute-start.12 = (bf16[1,208,768]{2,1,0:T(8,128)(2,1)S(1)}, bf16[1,208,768]{2,1,0:T(8,128)(2,1)}, u32[]{:S(2)}, u32[]{:S(2)}) collective-permute-start(bf16[1,208,768]{2,1,0:T(8,128)(2,1)S(1)} %bitcast.107), channel_id=1, source_target_pairs={{0,4},{4,0},{8,12},{12,8},{16,20},{20,16},{24,28},{28,24},{1,5},{5... | collective-permute-start | bytes 958472 | tf_op jit(solution)/shard_map/ppermute | solution.py:23
  29.1 6.4 %collective-permute-start.13 = (bf16[1,208,768]{2,1,0:T(8,128)(2,1)S(1)}, bf16[1,208,768]{2,1,0:T(8,128)(2,1)}, u32[]{:S(2)}, u32[]{:S(2)}) collective-permute-start(bf16[1,208,768]{2,1,0:T(8,128)(2,1)S(1)} %bitcast.109), channel_id=1, source_target_pairs={{0,4},{4,0},{8,12},{12,8},{16,20},{20,16},{24,28},{28,24},{1,5},{5... | collective-permute-start | bytes 958472 | tf_op jit(solution)/shard_map/ppermute | solution.py:23
  31.3 32.1 %copy-start.13 = (bf16[192,768]{1,0:T(8,128)(2,1)}, bf16[192,768]{1,0:T(8,128)(2,1)S(1)}, u32[]{:S(2)}) copy-start(bf16[192,768]{1,0:T(8,128)(2,1)S(1)} %get-tuple-element.78) | copy-start | bytes 884740
  31.3 10.3 %collective-permute-start = (bf16[192,768]{1,0:T(8,128)(2,1)S(1)}, bf16[192,768]{1,0:T(8,128)(2,1)S(1)}, u32[]{:S(2)}, u32[]{:S(2)}) collective-permute-start(bf16[192,768]{1,0:T(8,128)(2,1)S(1)} %get-tuple-element.78), channel_id=1, source_target_pairs={{0,8},{4,12},{8,0},{12,4},{16,24},{20,28},{24,16},{28,20},{1,9},{5... | collective-permute-start | bytes 884744 | tf_op jit(solution)/shard_map/ppermute | solution.py:23
  31.8 14.1 %collective-permute-start.1 = (bf16[192,768]{1,0:T(8,128)(2,1)S(1)}, bf16[192,768]{1,0:T(8,128)(2,1)S(1)}, u32[]{:S(2)}, u32[]{:S(2)}) collective-permute-start(bf16[192,768]{1,0:T(8,128)(2,1)S(1)} %get-tuple-element.78), channel_id=1, source_target_pairs={{0,16},{4,20},{8,24},{12,28},{16,0},{20,4},{24,8},{28,12},{1,17},{... | collective-permute-start | bytes 884744 | tf_op jit(solution)/shard_map/ppermute | solution.py:23
  33.3 14.2 %collective-permute-start.2 = (bf16[192,768]{1,0:T(8,128)(2,1)S(1)}, bf16[192,768]{1,0:T(8,128)(2,1)S(1)}, u32[]{:S(2)}, u32[]{:S(2)}) collective-permute-start(bf16[192,768]{1,0:T(8,128)(2,1)S(1)} %get-tuple-element.78), channel_id=1, source_target_pairs={{0,24},{4,28},{8,16},{12,20},{16,8},{20,12},{24,0},{28,4},{1,25},{... | collective-permute-start | bytes 884744 | tf_op jit(solution)/shard_map/ppermute | solution.py:23
  53.0 30.4 %all-to-all-start.1 = ((bf16[8,96,768]{2,1,0:T(8,128)(2,1)}), bf16[8,96,768]{2,1,0:T(8,128)(2,1)}, u32[]{:S(2)}, u32[]{:S(2)}) async-start(bf16[8,96,768]{2,1,0:T(8,128)(2,1)} %hold.1), calls=%async_computation.1 | async-start | bytes 2359296 | tf_op jit(solution)/shard_map/all_to_all | solution.py:851
  57.6 11.2 %copy-start.3 = (bf16[208,768]{1,0:T(8,128)(2,1)S(1)}, bf16[208,768]{1,0:T(8,128)(2,1)}, u32[]{:S(2)}) copy-start(bf16[208,768]{1,0:T(8,128)(2,1)} %get-tuple-element.76.refs_0_.refs_4_) | copy-start | bytes 958468
  57.6 11.2 %copy-start.60 = (f32[8,128]{1,0:T(8,128)S(1)}, f32[8,128]{1,0:T(8,128)}, u32[]{:S(2)}) copy-start(f32[8,128]{1,0:T(8,128)} %copy-done.59) | copy-start | bytes 12292
  57.6 11.2 %copy-start.62 = (f32[768,4]{0,1:T(4,128)S(1)}, f32[768,4]{0,1:T(4,128)}, u32[]{:S(2)}) copy-start(f32[768,4]{0,1:T(4,128)} %param.26) | copy-start | bytes 36868
  57.6 2.8 %collective-permute-start.3 = (bf16[1,192,768]{2,1,0:T(8,128)(2,1)S(1)}, bf16[1,192,768]{2,1,0:T(8,128)(2,1)S(1)}, u32[]{:S(2)}, u32[]{:S(2)}) collective-permute-start(bf16[1,192,768]{2,1,0:T(8,128)(2,1)S(1)} %bitcast.80), channel_id=1, source_target_pairs={{0,4},{4,0},{8,12},{12,8},{16,20},{20,16},{24,28},{28,24},{1,5},{5... | collective-permute-start | bytes 884744 | tf_op jit(solution)/shard_map/ppermute | solution.py:23
  57.9 5.0 %collective-permute-start.4 = (bf16[1,192,768]{2,1,0:T(8,128)(2,1)S(1)}, bf16[1,192,768]{2,1,0:T(8,128)(2,1)S(1)}, u32[]{:S(2)}, u32[]{:S(2)}) collective-permute-start(bf16[1,192,768]{2,1,0:T(8,128)(2,1)S(1)} %bitcast.67), channel_id=1, source_target_pairs={{0,4},{4,0},{8,12},{12,8},{16,20},{20,16},{24,28},{28,24},{1,5},{5... | collective-permute-start | bytes 884744 | tf_op jit(solution)/shard_map/ppermute | solution.py:23
  58.2 5.2 %collective-permute-start.5 = (bf16[1,192,768]{2,1,0:T(8,128)(2,1)S(1)}, bf16[1,192,768]{2,1,0:T(8,128)(2,1)S(1)}, u32[]{:S(2)}, u32[]{:S(2)}) collective-permute-start(bf16[1,192,768]{2,1,0:T(8,128)(2,1)S(1)} %bitcast.72), channel_id=1, source_target_pairs={{0,4},{4,0},{8,12},{12,8},{16,20},{20,16},{24,28},{28,24},{1,5},{5... | collective-permute-start | bytes 884744 | tf_op jit(solution)/shard_map/ppermute | solution.py:23
  58.4 5.0 %collective-permute-start.6 = (bf16[1,192,768]{2,1,0:T(8,128)(2,1)S(1)}, bf16[1,192,768]{2,1,0:T(8,128)(2,1)S(1)}, u32[]{:S(2)}, u32[]{:S(2)}) collective-permute-start(bf16[1,192,768]{2,1,0:T(8,128)(2,1)S(1)} %bitcast.77), channel_id=1, source_target_pairs={{0,4},{4,0},{8,12},{12,8},{16,20},{20,16},{24,28},{28,24},{1,5},{5... | collective-permute-start | bytes 884744 | tf_op jit(solution)/shard_map/ppermute | solution.py:23
  58.7 4.8 %collective-permute-start.14 = (bf16[192,128]{1,0:T(8,128)(2,1)S(1)}, bf16[192,128]{1,0:T(8,128)(2,1)S(1)}, u32[]{:S(2)}, u32[]{:S(2)}) collective-permute-start(bf16[192,128]{1,0:T(8,128)(2,1)S(1)} %copy-done.48), channel_id=1, source_target_pairs={{0,1},{1,0},{2,3},{3,2},{4,5},{5,4},{6,7},{7,6},{8,9},{9,8},{10,11... | collective-permute-start | bytes 147464 | tf_op jit(solution)/shard_map/ppermute | solution.py:23
  60.5 5.8 %collective-permute-start.15 = (bf16[192,128]{1,0:T(8,128)(2,1)S(1)}, bf16[192,128]{1,0:T(8,128)(2,1)S(1)}, u32[]{:S(2)}, u32[]{:S(2)}) collective-permute-start(bf16[192,128]{1,0:T(8,128)(2,1)S(1)} %copy-done.48), channel_id=1, source_target_pairs={{0,2},{1,3},{2,0},{3,1},{4,6},{5,7},{6,4},{7,5},{8,10},{9,11},{10,... | collective-permute-start | bytes 147464 | tf_op jit(solution)/shard_map/ppermute | solution.py:23
  62.8 5.9 %collective-permute-start.16 = (bf16[192,128]{1,0:T(8,128)(2,1)S(1)}, bf16[192,128]{1,0:T(8,128)(2,1)S(1)}, u32[]{:S(2)}, u32[]{:S(2)}) collective-permute-start(bf16[192,128]{1,0:T(8,128)(2,1)S(1)} %copy-done.48), channel_id=1, source_target_pairs={{0,3},{1,2},{2,1},{3,0},{4,7},{5,6},{6,5},{7,4},{8,11},{9,10},{10,... | collective-permute-start | bytes 147464 | tf_op jit(solution)/shard_map/ppermute | solution.py:23
  63.5 19.6 %copy-start.50 = (bf16[768,192]{1,0:T(8,128)(2,1)}, bf16[768,192]{1,0:T(8,128)(2,1)S(1)}, u32[]{:S(2)}) copy-start(bf16[768,192]{1,0:T(8,128)(2,1)S(1)} %get-tuple-element.92.refs_6_) | copy-start | bytes 884740
  71.2 12.1 %copy-start.25 = (bf16[96,896]{1,0:T(8,128)(2,1)}, bf16[96,896]{1,0:T(8,128)(2,1)S(1)}, u32[]{:S(2)}) copy-start(bf16[96,896]{1,0:T(8,128)(2,1)S(1)} %get-tuple-element.86) | copy-start | bytes 516100
  71.3 7.3 %collective-permute-start.17 = (bf16[96,896]{1,0:T(8,128)(2,1)S(1)}, bf16[96,896]{1,0:T(8,128)(2,1)S(1)}, u32[]{:S(2)}, u32[]{:S(2)}) collective-permute-start(bf16[96,896]{1,0:T(8,128)(2,1)S(1)} %get-tuple-element.86), channel_id=1, source_target_pairs={{0,8},{4,12},{8,0},{12,4},{16,24},{20,28},{24,16},{28,20},{1,9},{5... | collective-permute-start | bytes 516104 | tf_op jit(solution)/shard_map/ppermute | solution.py:23
  72.9 8.8 %collective-permute-start.18 = (bf16[96,896]{1,0:T(8,128)(2,1)S(1)}, bf16[96,896]{1,0:T(8,128)(2,1)S(1)}, u32[]{:S(2)}, u32[]{:S(2)}) collective-permute-start(bf16[96,896]{1,0:T(8,128)(2,1)S(1)} %get-tuple-element.86), channel_id=1, source_target_pairs={{0,16},{4,20},{8,24},{12,28},{16,0},{20,4},{24,8},{28,12},{1,17},{... | collective-permute-start | bytes 516104 | tf_op jit(solution)/shard_map/ppermute | solution.py:23
  74.4 7.3 %collective-permute-start.19 = (bf16[96,896]{1,0:T(8,128)(2,1)S(1)}, bf16[96,896]{1,0:T(8,128)(2,1)S(1)}, u32[]{:S(2)}, u32[]{:S(2)}) collective-permute-start(bf16[96,896]{1,0:T(8,128)(2,1)S(1)} %get-tuple-element.86), channel_id=1, source_target_pairs={{0,24},{4,28},{8,16},{12,20},{16,8},{20,12},{24,0},{28,4},{1,25},{... | collective-permute-start | bytes 516104 | tf_op jit(solution)/shard_map/ppermute | solution.py:23
  74.7 7.5 %collective-permute-start.20 = (bf16[1,96,896]{2,1,0:T(8,128)(2,1)S(1)}, bf16[1,96,896]{2,1,0:T(8,128)(2,1)S(1)}, u32[]{:S(2)}, u32[]{:S(2)}) collective-permute-start(bf16[1,96,896]{2,1,0:T(8,128)(2,1)S(1)} %bitcast.84), channel_id=1, source_target_pairs={{0,4},{4,0},{8,12},{12,8},{16,20},{20,16},{24,28},{28,24},{1,5},{5... | collective-permute-start | bytes 516104 | tf_op jit(solution)/shard_map/ppermute | solution.py:23
  78.6 3.7 %collective-permute-start.21 = (bf16[1,96,896]{2,1,0:T(8,128)(2,1)S(1)}, bf16[1,96,896]{2,1,0:T(8,128)(2,1)S(1)}, u32[]{:S(2)}, u32[]{:S(2)}) collective-permute-start(bf16[1,96,896]{2,1,0:T(8,128)(2,1)S(1)} %bitcast.88), channel_id=1, source_target_pairs={{0,4},{4,0},{8,12},{12,8},{16,20},{20,16},{24,28},{28,24},{1,5},{5... | collective-permute-start | bytes 516104 | tf_op jit(solution)/shard_map/ppermute | solution.py:23
  81.7 1.4 collective-permute-start.22
  81.7 1.6 collective-permute-start.23
  92.3 3.1 %collective-permute-start.24 = (bf16[4,96,1536]{2,1,0:T(8,128)(2,1)}, bf16[4,96,1536]{2,1,0:T(8,128)(2,1)S(1)}, u32[]{:S(2)}, u32[]{:S(2)}) collective-permute-start(bf16[4,96,1536]{2,1,0:T(8,128)(2,1)} %bitcast.118), channel_id=1, source_target_pairs={{0,4},{4,0},{8,12},{12,8},{16,20},{20,16},{24,28},{28,24},{1,5},{5... | collective-permute-start | bytes 3538952 | tf_op jit(solution)/shard_map/ppermute | solution.py:23
  96.9 9.9 %collective-permute-start.25 = (bf16[96,1536]{1,0:T(8,128)(2,1)S(1)}, bf16[96,1536]{1,0:T(8,128)(2,1)S(1)}, u32[]{:S(2)}, u32[]{:S(2)}) collective-permute-start(bf16[96,1536]{1,0:T(8,128)(2,1)S(1)} %get-tuple-element.141), channel_id=1, source_target_pairs={{0,8},{4,12},{8,0},{12,4},{16,24},{20,28},{24,16},{28,20},{1,9},{5... | collective-permute-start | bytes 884744 | tf_op jit(solution)/shard_map/ppermute | solution.py:23
  97.4 9.4 %collective-permute-start.26 = (bf16[96,1536]{1,0:T(8,128)(2,1)S(1)}, bf16[96,1536]{1,0:T(8,128)(2,1)S(1)}, u32[]{:S(2)}, u32[]{:S(2)}) collective-permute-start(bf16[96,1536]{1,0:T(8,128)(2,1)S(1)} %get-tuple-element.140), channel_id=1, source_target_pairs={{0,16},{4,20},{8,24},{12,28},{16,0},{20,4},{24,8},{28,12},{1,17},{... | collective-permute-start | bytes 884744 | tf_op jit(solution)/shard_map/ppermute | solution.py:23
  98.5 14.6 %collective-permute-start.27 = (bf16[96,1536]{1,0:T(8,128)(2,1)S(1)}, bf16[96,1536]{1,0:T(8,128)(2,1)S(1)}, u32[]{:S(2)}, u32[]{:S(2)}) collective-permute-start(bf16[96,1536]{1,0:T(8,128)(2,1)S(1)} %get-tuple-element.139), channel_id=1, source_target_pairs={{0,24},{4,28},{8,16},{12,20},{16,8},{20,12},{24,0},{28,4},{1,25},{... | collective-permute-start | bytes 884744 | tf_op jit(solution)/shard_map/ppermute | solution.py:23
  114.2 14.2 %copy-start.51 = (f32[768,8]{1,0:T(8,128)S(1)}, f32[768,8]{1,0:T(8,128)}, u32[]{:S(2)}) copy-start(f32[768,8]{1,0:T(8,128)} %get-tuple-element.107.refs_17_) | copy-start | bytes 73732
  114.2 25.5 %all-to-all-start.2 = ((bf16[4,120,768]{2,1,0:T(8,128)(2,1)}), bf16[4,120,768]{2,1,0:T(8,128)(2,1)S(1)}, u32[]{:S(2)}, u32[]{:S(2)}) async-start(bf16[4,120,768]{2,1,0:T(8,128)(2,1)} %get-tuple-element.89), calls=%async_computation.2 | async-start | bytes 1474560 | tf_op jit(solution)/shard_map/all_to_all | solution.py:72
  121.2 3.6 %collective-permute-start.28 = (bf16[96,768]{1,0:T(8,128)(2,1)S(1)}, bf16[96,768]{1,0:T(8,128)(2,1)S(1)}, u32[]{:S(2)}, u32[]{:S(2)}) collective-permute-start(bf16[96,768]{1,0:T(8,128)(2,1)S(1)} %get-tuple-element.98), channel_id=1, source_target_pairs={{0,4},{4,0},{8,12},{12,8},{16,20},{20,16},{24,28},{28,24},{1,5},{5... | collective-permute-start | bytes 442376 | tf_op jit(solution)/shard_map/ppermute | solution.py:23
  121.3 6.7 %collective-permute-start.29 = (bf16[96,768]{1,0:T(8,128)(2,1)S(1)}, bf16[96,768]{1,0:T(8,128)(2,1)S(1)}, u32[]{:S(2)}, u32[]{:S(2)}) collective-permute-start(bf16[96,768]{1,0:T(8,128)(2,1)S(1)} %get-tuple-element.99), channel_id=1, source_target_pairs={{0,8},{4,12},{8,0},{12,4},{16,24},{20,28},{24,16},{28,20},{1,9},{5... | collective-permute-start | bytes 442376 | tf_op jit(solution)/shard_map/ppermute | solution.py:23
  122.9 9.4 %collective-permute-start.30 = (bf16[96,768]{1,0:T(8,128)(2,1)S(1)}, bf16[96,768]{1,0:T(8,128)(2,1)S(1)}, u32[]{:S(2)}, u32[]{:S(2)}) collective-permute-start(bf16[96,768]{1,0:T(8,128)(2,1)S(1)} %get-tuple-element.100), channel_id=1, source_target_pairs={{0,12},{4,8},{8,4},{12,0},{16,28},{20,24},{24,20},{28,16},{1,13},{... | collective-permute-start | bytes 442376 | tf_op jit(solution)/shard_map/ppermute | solution.py:23
  123.2 9.1 %collective-permute-start.31 = (bf16[96,768]{1,0:T(8,128)(2,1)S(1)}, bf16[96,768]{1,0:T(8,128)(2,1)S(1)}, u32[]{:S(2)}, u32[]{:S(2)}) collective-permute-start(bf16[96,768]{1,0:T(8,128)(2,1)S(1)} %get-tuple-element.101), channel_id=1, source_target_pairs={{0,16},{4,20},{8,24},{12,28},{16,0},{20,4},{24,8},{28,12},{1,17},{... | collective-permute-start | bytes 442376 | tf_op jit(solution)/shard_map/ppermute | solution.py:23
  124.4 13.8 %collective-permute-start.32 = (bf16[96,768]{1,0:T(8,128)(2,1)S(1)}, bf16[96,768]{1,0:T(8,128)(2,1)S(1)}, u32[]{:S(2)}, u32[]{:S(2)}) collective-permute-start(bf16[96,768]{1,0:T(8,128)(2,1)S(1)} %get-tuple-element.102), channel_id=1, source_target_pairs={{0,20},{4,16},{8,28},{12,24},{16,4},{20,0},{24,12},{28,8},{1,21},{... | collective-permute-start | bytes 442376 | tf_op jit(solution)/shard_map/ppermute | solution.py:23
  124.9 13.3 %collective-permute-start.33 = (bf16[96,768]{1,0:T(8,128)(2,1)S(1)}, bf16[96,768]{1,0:T(8,128)(2,1)S(1)}, u32[]{:S(2)}, u32[]{:S(2)}) collective-permute-start(bf16[96,768]{1,0:T(8,128)(2,1)S(1)} %get-tuple-element.103), channel_id=1, source_target_pairs={{0,24},{4,28},{8,16},{12,20},{16,8},{20,12},{24,0},{28,4},{1,25},{... | collective-permute-start | bytes 442376 | tf_op jit(solution)/shard_map/ppermute | solution.py:23
  128.0 10.2 %collective-permute-start.34 = (bf16[96,768]{1,0:T(8,128)(2,1)S(1)}, bf16[96,768]{1,0:T(8,128)(2,1)S(1)}, u32[]{:S(2)}, u32[]{:S(2)}) collective-permute-start(bf16[96,768]{1,0:T(8,128)(2,1)S(1)} %get-tuple-element.104), channel_id=1, source_target_pairs={{0,28},{4,24},{8,20},{12,16},{16,12},{20,8},{24,4},{28,0},{1,29},{... | collective-permute-start | bytes 442376 | tf_op jit(solution)/shard_map/ppermute | solution.py:23
  146.7 2.0 %collective-permute-start.35 = (bf16[4,128,384]{2,1,0:T(8,128)(2,1)}, bf16[4,128,384]{2,1,0:T(8,128)(2,1)S(1)}, u32[]{:S(2)}, u32[]{:S(2)}) collective-permute-start(bf16[4,128,384]{2,1,0:T(8,128)(2,1)} %get-tuple-element.111), channel_id=1, source_target_pairs={{0,4},{4,0},{8,12},{12,8},{16,20},{20,16},{24,28},{28,24},{1,5},{5... | collective-permute-start | bytes 1179656 | tf_op jit(solution)/shard_map/ppermute | solution.py:23
  150.0 6.2 %collective-permute-start.36 = (bf16[128,384]{1,0:T(8,128)(2,1)S(1)}, bf16[128,384]{1,0:T(8,128)(2,1)S(1)}, u32[]{:S(2)}, u32[]{:S(2)}) collective-permute-start(bf16[128,384]{1,0:T(8,128)(2,1)S(1)} %get-tuple-element.149), channel_id=1, source_target_pairs={{0,8},{4,12},{8,0},{12,4},{16,24},{20,28},{24,16},{28,20},{1,9},{5... | collective-permute-start | bytes 294920 | tf_op jit(solution)/shard_map/ppermute | solution.py:23
  151.5 6.9 %collective-permute-start.37 = (bf16[128,384]{1,0:T(8,128)(2,1)S(1)}, bf16[128,384]{1,0:T(8,128)(2,1)S(1)}, u32[]{:S(2)}, u32[]{:S(2)}) collective-permute-start(bf16[128,384]{1,0:T(8,128)(2,1)S(1)} %get-tuple-element.148), channel_id=1, source_target_pairs={{0,16},{4,20},{8,24},{12,28},{16,0},{20,4},{24,8},{28,12},{1,17},{... | collective-permute-start | bytes 294920 | tf_op jit(solution)/shard_map/ppermute | solution.py:23
  152.1 6.3 %collective-permute-start.38 = (bf16[128,384]{1,0:T(8,128)(2,1)S(1)}, bf16[128,384]{1,0:T(8,128)(2,1)S(1)}, u32[]{:S(2)}, u32[]{:S(2)}) collective-permute-start(bf16[128,384]{1,0:T(8,128)(2,1)S(1)} %get-tuple-element.147), channel_id=1, source_target_pairs={{0,24},{4,28},{8,16},{12,20},{16,8},{20,12},{24,0},{28,4},{1,25},{... | collective-permute-start | bytes 294920 | tf_op jit(solution)/shard_map/ppermute | solution.py:23
  159.7 9.6 %collective-permute-start.39 = (bf16[4,96,768]{2,1,0:T(8,128)(2,1)S(1)}, bf16[4,96,768]{2,1,0:T(8,128)(2,1)S(1)}, u32[]{:S(2)}, u32[]{:S(2)}) collective-permute-start(bf16[4,96,768]{2,1,0:T(8,128)(2,1)S(1)} %get-tuple-element.125), channel_id=1, source_target_pairs={{0,4},{4,0},{8,12},{12,8},{16,20},{20,16},{24,28},{28,24},{1,5},{5... | collective-permute-start | bytes 1769480 | tf_op jit(solution)/shard_map/ppermute | solution.py:23
  159.7 11.6 %collective-permute-start.45 = (f32[8,768]{1,0:T(8,128)S(1)}, f32[8,768]{1,0:T(8,128)S(1)}, u32[]{:S(2)}, u32[]{:S(2)}) collective-permute-start(f32[8,768]{1,0:T(8,128)S(1)} %get-tuple-element.126), channel_id=1, source_target_pairs={{0,3},{1,2},{2,1},{3,0},{4,7},{5,6},{6,5},{7,4},{8,11},{9,10},{10,... | collective-permute-start | bytes 73736 | tf_op jit(solution)/shard_map/ppermute | solution.py:23
  163.5 9.5 %collective-permute-start.44 = (f32[8,768]{1,0:T(8,128)S(1)}, f32[8,768]{1,0:T(8,128)S(1)}, u32[]{:S(2)}, u32[]{:S(2)}) collective-permute-start(f32[8,768]{1,0:T(8,128)S(1)} %get-tuple-element.126), channel_id=1, source_target_pairs={{0,2},{1,3},{2,0},{3,1},{4,6},{5,7},{6,4},{7,5},{8,10},{9,11},{10,... | collective-permute-start | bytes 73736 | tf_op jit(solution)/shard_map/ppermute | solution.py:23
  163.5 9.5 %collective-permute-start.43 = (f32[8,768]{1,0:T(8,128)S(1)}, f32[8,768]{1,0:T(8,128)S(1)}, u32[]{:S(2)}, u32[]{:S(2)}) collective-permute-start(f32[8,768]{1,0:T(8,128)S(1)} %get-tuple-element.126), channel_id=1, source_target_pairs={{0,1},{1,0},{2,3},{3,2},{4,5},{5,4},{6,7},{7,6},{8,9},{9,8},{10,11... | collective-permute-start | bytes 73736 | tf_op jit(solution)/shard_map/ppermute | solution.py:23
  164.1 19.0 %copy-start.57 = (f32[32,768]{1,0:T(8,128)S(1)}, f32[32,768]{1,0:T(8,128)}, u32[]{:S(2)}) copy-start(f32[32,768]{1,0:T(8,128)} %get-tuple-element.113.refs_2_) | copy-start | bytes 294916
  164.1 19.0 %all-to-all-start.3 = ((bf16[4,32,768]{2,1,0:T(8,128)(2,1)}), bf16[4,32,768]{2,1,0:T(8,128)(2,1)S(1)}, u32[]{:S(2)}, u32[]{:S(2)}) async-start(bf16[4,32,768]{2,1,0:T(8,128)(2,1)} %get-tuple-element.123), calls=%async_computation.3 | async-start | bytes 393216 | tf_op jit(solution)/shard_map/all_to_all | solution.py:72
  169.4 13.6 %collective-permute-start.40 = (bf16[96,768]{1,0:T(8,128)(2,1)S(1)}, bf16[96,768]{1,0:T(8,128)(2,1)S(1)}, u32[]{:S(2)}, u32[]{:S(2)}) collective-permute-start(bf16[96,768]{1,0:T(8,128)(2,1)S(1)} %get-tuple-element.145), channel_id=1, source_target_pairs={{0,8},{4,12},{8,0},{12,4},{16,24},{20,28},{24,16},{28,20},{1,9},{5... | collective-permute-start | bytes 442376 | tf_op jit(solution)/shard_map/ppermute | solution.py:23
  170.1 13.0 %collective-permute-start.41 = (bf16[96,768]{1,0:T(8,128)(2,1)S(1)}, bf16[96,768]{1,0:T(8,128)(2,1)S(1)}, u32[]{:S(2)}, u32[]{:S(2)}) collective-permute-start(bf16[96,768]{1,0:T(8,128)(2,1)S(1)} %get-tuple-element.144), channel_id=1, source_target_pairs={{0,16},{4,20},{8,24},{12,28},{16,0},{20,4},{24,8},{28,12},{1,17},{... | collective-permute-start | bytes 442376 | tf_op jit(solution)/shard_map/ppermute | solution.py:23
  171.2 11.8 %collective-permute-start.42 = (bf16[96,768]{1,0:T(8,128)(2,1)S(1)}, bf16[96,768]{1,0:T(8,128)(2,1)S(1)}, u32[]{:S(2)}, u32[]{:S(2)}) collective-permute-start(bf16[96,768]{1,0:T(8,128)(2,1)S(1)} %get-tuple-element.143), channel_id=1, source_target_pairs={{0,24},{4,28},{8,16},{12,20},{16,8},{20,12},{24,0},{28,4},{1,25},{... | collective-permute-start | bytes 442376 | tf_op jit(solution)/shard_map/ppermute | solution.py:23
  173.0 1.3 collective-permute-start.46
  174.3 4.0 %collective-permute-start.47 = (f32[8,768]{1,0:T(8,128)S(1)}, f32[8,768]{1,0:T(8,128)S(1)}, u32[]{:S(2)}, u32[]{:S(2)}) collective-permute-start(f32[8,768]{1,0:T(8,128)S(1)} %add.71.refs_8_), channel_id=1, source_target_pairs={{0,8},{4,12},{8,0},{12,4},{16,24},{20,28},{24,16},{28,20},{1,9},{5... | collective-permute-start | bytes 73736 | tf_op jit(solution)/shard_map/ppermute | solution.py:23
  174.8 4.7 %collective-permute-start.48 = (f32[8,768]{1,0:T(8,128)S(1)}, f32[8,768]{1,0:T(8,128)S(1)}, u32[]{:S(2)}, u32[]{:S(2)}) collective-permute-start(f32[8,768]{1,0:T(8,128)S(1)} %add.71.refs_8_), channel_id=1, source_target_pairs={{0,16},{4,20},{8,24},{12,28},{16,0},{20,4},{24,8},{28,12},{1,17},{... | collective-permute-start | bytes 73736 | tf_op jit(solution)/shard_map/ppermute | solution.py:23
  178.3 4.7 %collective-permute-start.49 = (f32[8,768]{1,0:T(8,128)S(1)}, f32[8,768]{1,0:T(8,128)S(1)}, u32[]{:S(2)}, u32[]{:S(2)}) collective-permute-start(f32[8,768]{1,0:T(8,128)S(1)} %add.71.refs_8_), channel_id=1, source_target_pairs={{0,24},{4,28},{8,16},{12,20},{16,8},{20,12},{24,0},{28,4},{1,25},{... | collective-permute-start | bytes 73736 | tf_op jit(solution)/shard_map/ppermute | solution.py:23
  (64 other events, 306.6 us)

commit v4 on v3

--- a/solution.py
+++ b/solution.py
@@ -193,7 +193,7 @@
     return iota((parts * cap, rows), 0) == place, named
 
 
-def pack_body(folded, wo, cot, info, x, *refs):
+def pack_body(folded, wo, cot, routes, prior, x, *refs):
     weights, (out, message) = refs[:-2], refs[-2:]
     quarter, shard = cot.shape[0], wo.shape[1]
     width = cot.shape[2]
@@ -221,13 +221,15 @@
             first[lead : lead + quarter, :third] = piece[:, c * third : (c + 1) * third]
     eye = (iota((shard, shard), 0) == iota((shard, shard), 1)).astype(F32).astype(BF16)
     first[:shard, third:] = nt(eye, wo[...]).astype(BF16)
-    values = info[...]
-    hi = values.astype(BF16).astype(F32)
-    mid = (values - hi).astype(BF16).astype(F32)
-    low = values - hi - mid
+    choice, weight = routes[...].astype(F32), prior[...]
     total = jnp.zeros((16, LANES), F32)
     for s in range(2):
-        terms = [term[:, 4 * s : 4 * s + 4] for term in (hi, mid, low)]
+        values = jnp.concatenate(
+            [choice[:, 2 * s : 2 * s + 2], weight[:, 2 * s : 2 * s + 2]], axis=1
+        )
+        hi = values.astype(BF16).astype(F32)
+        mid = (values - hi).astype(BF16).astype(F32)
+        terms = [hi, mid, values - hi - mid]
         stacked = jnp.concatenate(terms + [jnp.zeros((quarter, 4), F32)], axis=1).astype(BF16)
         spot = iota((quarter, LANES), 0) + s * quarter == iota((quarter, LANES), 1)
         total = total + tn(stacked, jnp.where(spot, 1.0, 0.0).astype(BF16))
@@ -784,7 +786,6 @@
     down = down_weight.reshape(hidden, width)
 
     folded = shard * 5 // 6 if shard % 96 == 0 else 0
-    info = jnp.concatenate([routes.astype(F32), route_prior], axis=2).reshape(quarter, 4 * seqs)
     cot_pack, x = call(
         functools.partial(pack_body, folded),
         "pack",
@@ -792,7 +793,8 @@
             ((parts, max(3 * seqs * quarter, shard) + 16, width // 3 + hl), BF16),
             ((rows + folded, width), BF16),
         ],
-        output_weight, output_cotangent, info, block_input,
+        output_weight, output_cotangent, routes.reshape(quarter, 2 * seqs),
+        route_prior.reshape(quarter, 2 * seqs), block_input,
         *([query_weight, key_weight, value_weight] if folded else []), us=1.5, wide=True,
     )
     x_blocks = gather_ctx(x)
@@ -871,20 +873,13 @@
             back_near.reshape(half, slots, 2 * width), back_far.reshape(half, slots, 2 * width)
         )
     )
-    back_sums, summed = call(
-        functools.partial(back_sum_body, cap),
-        "sum_back",
-        ((parts, slots + cap, width), BF16),
-        *back_terms, us=2.0, token=True,
-    )
-    returned = trade_exp(back_sums)
     by_permutes = ctx_size <= 8 and hidden % LANES == 0
     w_shape = (shard, 2 * hidden)
     *w_grads, weighed = call(
         functools.partial(expert_weights_body, cut),
         "expert_weights",
         [(w_shape, BF16)] * ctx_size if by_permutes else [((ctx_size, *w_shape), BF16)],
-        *x_blocks, dg, du, us=4.0, after=[summed], token=True,
+        *x_blocks, dg, du, us=4.0, after=[back_terms[0]], token=True,
         scratch=[pltpu.VMEM((ctx_size, *w_shape), BF16)],
     )
     down_grad, router = call(
@@ -893,6 +888,13 @@
         [((hidden, width), F32), ((8, width), F32)],
         *x_blocks, *c_blocks, hid, spread, us=3.0, after=[weighed],
     )
+    back_sums, summed = call(
+        functools.partial(back_sum_body, cap),
+        "sum_back",
+        ((parts, slots + cap, width), BF16),
+        *back_terms, us=2.0, token=True, after=[router],
+    )
+    returned = trade_exp(back_sums)
     if by_permutes:
         w_back = [w_grads[0]] + [swap(w_grads[d], "ctx", d) for d in range(1, ctx_size)]
     else:
@@ -921,7 +923,7 @@
             pltpu.VMEM((rows, width), F32),
             pltpu.VMEM((ctx_size, seqs, tok, 2 * hl), BF16),
         ],
-        after=[widened, router], wide=True,
+        after=[widened], wide=True,
     )
     dkv_both = add_pair(dkv_near, dkv_far)
     dkv_terms = send_direct(dkv_both)

time: 185 us -> 182 us (0.984)
  waiting for transfers between devices: 66.6 us -> 64 us
    ppermute x50, waiting for transfers between devices: 66.6 us -> 63.8 us  [swap(): return lax.ppermute(value, axis, [(i, i ^ bits) for i in range(devices)])]
    reshape x1 -> x2, local copies, waits for them, and re-layouts: 0.67 us -> 2.72 us  [the longest x1 1.36 us: on_device(): routes.reshape(quarter, 2 * seqs)]
  transfers between devices with their start and end apart: 54 -> 54, of which waited for: 20 -> 22; matrix products, arithmetic and copies ran while one was open for 1% -> 1% of each run, Pallas kernels for 8% -> 8%
where the time goes in v4:
time: 182 us
  waiting for transfers between devices  64 us (35%)
  starting transfers between devices  61.9 us (34%)
  Pallas kernels  39.9 us (22%)
  local copies, waits for them, and re-layouts  11.3 us (6%)
  other arithmetic  3.07 us (2%)
    ppermute x50, waiting for transfers between devices, swap(): return lax.ppermute(value, axis, [(i, i ^ bits) for i in range(devices)])  63.8 us
    ppermute x50, starting transfers between devices, swap(): return lax.ppermute(value, axis, [(i, i ^ bits) for i in range(devices)])  43.6 us
    pallas_call x17, Pallas kernels, call(): pl.pallas_call(run, out_shape=shapes[0] if single else shapes, in_specs=s...  39.9 us
    all_to_all x3, starting transfers between devices, trade_exp(): return lax.all_to_all(value, 'exp', split_axis=0, concat_axis=0, tiled=True)  13.8 us
    unnamed x148, local copies, waits for them, and re-layouts  7.82 us
    all_to_all x1, starting transfers between devices, on_device(): lax.all_to_all(hold(sent, low), 'ctx', split_axis=0, concat_axis=0, tiled...  4.59 us
  transfers between devices with their start and end apart: 54, of which 22 were waited for; matrix products, arithmetic and copies ran while one was open for 1% of the time, Pallas kernels for 8%

profile of v4, /device:TPU:0, one launch (start us, length us, event | category | flops | bytes accessed | tf_op | source)
XLA Modules:
  0.0 181.7 jit_solution(18096092690564455935)
XLA Ops:
  0.7 1.4 copy.32.refs_2_
  2.0 1.4 copy.33.refs_3_
  3.4 2.8 %pack.1 = (bf16[4,112,448]{2,1,0:T(8,128)(2,1)}, bf16[208,768]{1,0:T(8,128)(2,1)}) custom-call(bf16[192,96]{1,0:T(8,128)(2,1)} %refs_0_.2, bf16[16,2,768]{2,1,0:T(2,128)(2,1)} %refs_1_.2, s32[16,4]{1,0:T(8,128)} %copy.32.refs_2_, f32[16,4]{1,0:T(8,128)} %copy.33.refs_3_, bf16[64,2,768]{2,1,0:T(2,128)(2,1)} %refs_4_.1, bf16[96,192]{1,0:T(8,128)(2,1)} %refs_5_.2, ...), custom_call_target="tpu_custom_call" | custom-call | bytes 45000 | tf_op jit(solution)/shard_map/pack/pallas_call | solution.py:127
  6.2 2.9 %collective-permute-start.7 = (bf16[208,768]{1,0:T(8,128)(2,1)}, bf16[208,768]{1,0:T(8,128)(2,1)S(1)}, u32[]{:S(2)}, u32[]{:S(2)}) collective-permute-start(bf16[208,768]{1,0:T(8,128)(2,1)} %get-tuple-element.75.refs_0_.refs_4_), channel_id=1, source_target_pairs={{0,8},{4,12},{8,0},{12,4},{16,24},{20,28},{24,16},{28,20},{1,9},{5... | collective-permute-start | bytes 958472 | tf_op jit(solution)/shard_map/ppermute | solution.py:23
  9.1 4.9 %all-to-all-start = ((bf16[4,112,448]{2,1,0:T(8,128)(2,1)}), bf16[4,112,448]{2,1,0:T(8,128)(2,1)S(1)}, u32[]{:S(2)}, u32[]{:S(2)}) async-start(bf16[4,112,448]{2,1,0:T(8,128)(2,1)} %get-tuple-element.76), calls=%async_computation | async-start | bytes 917504 | tf_op jit(solution)/shard_map/all_to_all | solution.py:72
  14.0 1.5 collective-permute-start.8
  16.0 1.0 collective-permute-done.7
  17.0 12.8 %collective-permute-done.8 = bf16[208,768]{1,0:T(8,128)(2,1)S(1)} collective-permute-done((bf16[208,768]{1,0:T(8,128)(2,1)}, bf16[208,768]{1,0:T(8,128)(2,1)S(1)}, u32[]{:S(2)}, u32[]{:S(2)}) %collective-permute-start.8) | collective-permute-done | bytes 319520 | tf_op jit(solution)/shard_map/ppermute | solution.py:23
  32.6 1.5 collective-permute-start.1
  34.1 1.6 collective-permute-start.2
  37.9 4.1 %project.1 = (bf16[128,192]{1,0:T(8,128)(2,1)}, bf16[8,2,64,384]{3,2,1,0:T(8,128)(2,1)}, bf16[128,768]{1,0:T(8,128)(2,1)}, bf16[768,576]{1,0:T(8,128)(2,1)}) custom-call(f32[768]{0:T(1024)} %refs_1_.3, bf16[1,208,768]{2,1,0:T(8,128)(2,1)} %bitcast.65, bf16[1,208,768]{2,1,0:T(8,128)(2,1)} %bitcast.107, bf16[1,208,768]{2,1,0:T(8,128)(2,1)} %bitcast.109, ...), custom_call_target="tpu_custom_call" | custom-call | bytes 120000 | tf_op jit(solution)/shard_map/project/pallas_call | solution.py:127
  43.0 1.0 copy-done
  44.0 2.7 %collective-permute-done.1 = bf16[192,768]{1,0:T(8,128)(2,1)S(1)} collective-permute-done((bf16[192,768]{1,0:T(8,128)(2,1)S(1)}, bf16[192,768]{1,0:T(8,128)(2,1)S(1)}, u32[]{:S(2)}, u32[]{:S(2)}) %collective-permute-start.1) | collective-permute-done | bytes 294944 | tf_op jit(solution)/shard_map/ppermute | solution.py:23
  46.7 1.6 collective-permute-done.2
  49.0 4.7 %attend.1 = (f32[128,192]{1,0:T(8,128)}, bf16[192,128]{1,0:T(8,128)(2,1)}, f32[6,64,512]{2,1,0:T(8,128)}) custom-call(bf16[128,192]{1,0:T(8,128)(2,1)} %get-tuple-element.80.refs_0_.refs_2_.refs_7_, f32[12,32]{1,0:T(8,128)} %bitcast.114, s32[1,512]{1,0:T(1,128)} %bitcast.112, bf16[8,2,64,384]{3,2,1,0:T(8,128)(2,1)} %get-tuple-element.81.refs_3_.refs_8_, ...), custom_call_target="tpu_custom_call" | custom-call | bytes 144000 | tf_op jit(solution)/shard_map/attend/pallas_call | solution.py:127
  53.7 4.6 %all-to-all-start.1 = ((bf16[8,96,768]{2,1,0:T(8,128)(2,1)}), bf16[8,96,768]{2,1,0:T(8,128)(2,1)}, u32[]{:S(2)}, u32[]{:S(2)}) async-start(bf16[8,96,768]{2,1,0:T(8,128)(2,1)} %hold.1), calls=%async_computation.1 | async-start | bytes 2359296 | tf_op jit(solution)/shard_map/all_to_all | solution.py:853
  59.5 1.7 collective-permute-start.14
  61.2 2.4 %collective-permute-start.15 = (bf16[192,128]{1,0:T(8,128)(2,1)S(1)}, bf16[192,128]{1,0:T(8,128)(2,1)S(1)}, u32[]{:S(2)}, u32[]{:S(2)}) collective-permute-start(bf16[192,128]{1,0:T(8,128)(2,1)S(1)} %copy-done.48), channel_id=1, source_target_pairs={{0,2},{1,3},{2,0},{3,1},{4,6},{5,7},{6,4},{7,5},{8,10},{9,11},{10,... | collective-permute-start | bytes 147464 | tf_op jit(solution)/shard_map/ppermute | solution.py:23
  64.3 2.7 %collective-permute-done.15.refs_4_ = bf16[192,128]{1,0:T(8,128)(2,1)S(1)} collective-permute-done((bf16[192,128]{1,0:T(8,128)(2,1)S(1)}, bf16[192,128]{1,0:T(8,128)(2,1)S(1)}, u32[]{:S(2)}, u32[]{:S(2)}) %collective-permute-start.15) | collective-permute-done | bytes 49184 | tf_op jit(solution)/shard_map/ppermute | solution.py:23
  67.0 2.5 %collective-permute-done.16.refs_5_ = bf16[192,128]{1,0:T(8,128)(2,1)S(1)} collective-permute-done((bf16[192,128]{1,0:T(8,128)(2,1)S(1)}, bf16[192,128]{1,0:T(8,128)(2,1)S(1)}, u32[]{:S(2)}, u32[]{:S(2)}) %collective-permute-start.16) | collective-permute-done | bytes 49184 | tf_op jit(solution)/shard_map/ppermute | solution.py:23
  69.6 1.7 route.1
  72.0 1.7 collective-permute-start.17
  73.7 1.5 collective-permute-start.18
  75.5 3.8 %collective-permute-done.17 = bf16[96,896]{1,0:T(8,128)(2,1)S(1)} collective-permute-done((bf16[96,896]{1,0:T(8,128)(2,1)S(1)}, bf16[96,896]{1,0:T(8,128)(2,1)S(1)}, u32[]{:S(2)}, u32[]{:S(2)}) %collective-permute-start.17) | collective-permute-done | bytes 172064 | tf_op jit(solution)/shard_map/ppermute | solution.py:23
  79.3 3.1 %collective-permute-done.18 = bf16[96,896]{1,0:T(8,128)(2,1)S(1)} collective-permute-done((bf16[96,896]{1,0:T(8,128)(2,1)S(1)}, bf16[96,896]{1,0:T(8,128)(2,1)S(1)}, u32[]{:S(2)}, u32[]{:S(2)}) %collective-permute-start.18) | collective-permute-done | bytes 172064 | tf_op jit(solution)/shard_map/ppermute | solution.py:23
  83.0 0.9 collective-permute-done.22.refs_6_
  84.8 8.2 %expert_back.1 = (bf16[384,1536]{1,0:T(8,128)(2,1)}, bf16[384,1536]{1,0:T(8,128)(2,1)}, bf16[768,384]{1,0:T(8,128)(2,1)}, bf16[768,384]{1,0:T(8,128)(2,1)}, bf16[768,384]{1,0:T(8,128)(2,1)}, /*index=5*/f32[768,8]{1,0:T(8,128)}) custom-call(bf16[1,96,896]{2,1,0:T(8,128)(2,1)} %bitcast.86, bf16[1,96,896]{2,1,0:T(8,128)(2,1)} %bitcast.90, ...), custom_call_target="tpu_custom_call" | custom-call | bytes 240000 | tf_op jit(solution)/shard_map/expert_back/pallas_call | solution.py:127
  93.4 2.8 %collective-permute-done.24 = bf16[4,96,1536]{2,1,0:T(8,128)(2,1)S(1)} collective-permute-done((bf16[4,96,1536]{2,1,0:T(8,128)(2,1)}, bf16[4,96,1536]{2,1,0:T(8,128)(2,1)S(1)}, u32[]{:S(2)}, u32[]{:S(2)}) %collective-permute-start.24) | collective-permute-done | bytes 1179680 | tf_op jit(solution)/shard_map/ppermute | solution.py:23
  96.2 1.7 fusion
  98.4 1.1 collective-permute-start.26
  99.5 2.0 %collective-permute-start.27 = (bf16[96,1536]{1,0:T(8,128)(2,1)S(1)}, bf16[96,1536]{1,0:T(8,128)(2,1)S(1)}, u32[]{:S(2)}, u32[]{:S(2)}) collective-permute-start(bf16[96,1536]{1,0:T(8,128)(2,1)S(1)} %get-tuple-element.137), channel_id=1, source_target_pairs={{0,24},{4,28},{8,16},{12,20},{16,8},{20,12},{24,0},{28,4},{1,25},{... | collective-permute-start | bytes 884744 | tf_op jit(solution)/shard_map/ppermute | solution.py:23
  101.6 1.7 expert_weights.1
  103.5 2.8 %expert_rest.1 = (f32[384,768]{1,0:T(8,128)}, f32[8,768]{1,0:T(8,128)S(1)}) custom-call(bf16[1,96,896]{2,1,0:T(8,128)(2,1)S(1)} %bitcast.88, bf16[1,96,896]{2,1,0:T(8,128)(2,1)S(1)} %bitcast.92, bf16[1,96,896]{2,1,0:T(8,128)(2,1)S(1)} %bitcast.96, bf16[1,96,896]{2,1,0:T(8,128)(2,1)S(1)} %bitcast.100, bf16[1,96,896]{2,1,0:T(8,128)(2,1)S(1)} %copy-done.34, ...), custom_call_target="tpu_custom_call" | custom-call | bytes 90000 | tf_op jit(solution)/shard_map/expert_rest/pallas_call | solution.py:127
  106.3 1.6 collective-permute-done.25.refs_1_
  107.8 6.2 %collective-permute-done.27.refs_3_ = bf16[96,1536]{1,0:T(8,128)(2,1)S(1)} collective-permute-done((bf16[96,1536]{1,0:T(8,128)(2,1)S(1)}, bf16[96,1536]{1,0:T(8,128)(2,1)S(1)}, u32[]{:S(2)}, u32[]{:S(2)}) %collective-permute-start.27) | collective-permute-done | bytes 294944 | tf_op jit(solution)/shard_map/ppermute | solution.py:23
  114.1 1.0 sum_back.1
  115.1 4.0 %all-to-all-start.2 = ((bf16[4,120,768]{2,1,0:T(8,128)(2,1)}), bf16[4,120,768]{2,1,0:T(8,128)(2,1)S(1)}, u32[]{:S(2)}, u32[]{:S(2)}) async-start(bf16[4,120,768]{2,1,0:T(8,128)(2,1)} %get-tuple-element.94), calls=%async_computation.2 | async-start | bytes 1474560 | tf_op jit(solution)/shard_map/all_to_all | solution.py:72
  119.1 1.5 collective-permute-start.29
  120.9 1.2 collective-permute-start.31
  122.6 1.7 collective-permute-start.33
  124.2 1.5 collective-permute-done.29.refs_2_
  126.2 1.9 %collective-permute-done.30.refs_3_ = bf16[96,768]{1,0:T(8,128)(2,1)S(1)} collective-permute-done((bf16[96,768]{1,0:T(8,128)(2,1)S(1)}, bf16[96,768]{1,0:T(8,128)(2,1)S(1)}, u32[]{:S(2)}, u32[]{:S(2)}) %collective-permute-start.30) | collective-permute-done | bytes 147488 | tf_op jit(solution)/shard_map/ppermute | solution.py:23
  128.1 7.7 %collective-permute-done.32.refs_5_ = bf16[96,768]{1,0:T(8,128)(2,1)S(1)} collective-permute-done((bf16[96,768]{1,0:T(8,128)(2,1)S(1)}, bf16[96,768]{1,0:T(8,128)(2,1)S(1)}, u32[]{:S(2)}, u32[]{:S(2)}) %collective-permute-start.32) | collective-permute-done | bytes 147488 | tf_op jit(solution)/shard_map/ppermute | solution.py:23
  135.8 1.6 widen.1
  138.4 6.1 %attend_back.1 = (f32[32,768]{1,0:T(8,128)}, bf16[128,192]{1,0:T(8,128)(2,1)}, bf16[4,128,384]{2,1,0:T(8,128)(2,1)}, bf16[4,128,384]{2,1,0:T(8,128)(2,1)}, bf16[...) custom-call(bf16[4,120,768]{2,1,0:T(8,128)(2,1)} %copy-done.1, f32[128,768]{1,0:T(8,128)} %copy-done.23, ...), custom_call_target="tpu_custom_call" | custom-call | bytes 240000 | tf_op jit(solution)/shard_map/attend_back/pallas_call | solution.py:127
  145.2 1.6 collective-permute-done.35
  146.7 1.2 fusion.11
  148.0 1.6 collective-permute-start.36
  150.3 1.3 collective-permute-start.38
  151.8 1.3 table.1
  153.1 1.1 mix.1
  154.2 2.2 %collective-permute-done.37.refs_11_ = bf16[128,384]{1,0:T(8,128)(2,1)S(1)} collective-permute-done((bf16[128,384]{1,0:T(8,128)(2,1)S(1)}, bf16[128,384]{1,0:T(8,128)(2,1)S(1)}, u32[]{:S(2)}, u32[]{:S(2)}) %collective-permute-start.37) | collective-permute-done | bytes 98336 | tf_op jit(solution)/shard_map/ppermute | solution.py:23
  156.4 1.2 back_project.1
  157.6 3.5 %collective-permute-start.45 = (f32[8,768]{1,0:T(8,128)S(1)}, f32[8,768]{1,0:T(8,128)S(1)}, u32[]{:S(2)}, u32[]{:S(2)}) collective-permute-start(f32[8,768]{1,0:T(8,128)S(1)} %get-tuple-element.124), channel_id=1, source_target_pairs={{0,3},{1,2},{2,1},{3,0},{4,7},{5,6},{6,5},{7,4},{8,11},{9,10},{10,... | collective-permute-start | bytes 73736 | tf_op jit(solution)/shard_map/ppermute | solution.py:23
  161.2 0.9 collective-permute-start.43
  162.0 4.9 %all-to-all-start.3 = ((bf16[4,32,768]{2,1,0:T(8,128)(2,1)}), bf16[4,32,768]{2,1,0:T(8,128)(2,1)S(1)}, u32[]{:S(2)}, u32[]{:S(2)}) async-start(bf16[4,32,768]{2,1,0:T(8,128)(2,1)} %get-tuple-element.121), calls=%async_computation.3 | async-start | bytes 393216 | tf_op jit(solution)/shard_map/all_to_all | solution.py:72
  167.7 1.2 collective-permute-start.41
  168.9 1.8 collective-permute-start.42
  170.8 1.2 collective-permute-done.46
  172.5 1.2 collective-permute-start.48
  173.7 2.3 %collective-permute-done.47.refs_9_ = f32[8,768]{1,0:T(8,128)S(1)} collective-permute-done((f32[8,768]{1,0:T(8,128)S(1)}, f32[8,768]{1,0:T(8,128)S(1)}, u32[]{:S(2)}, u32[]{:S(2)}) %collective-permute-start.47) | collective-permute-done | bytes 24608 | tf_op jit(solution)/shard_map/ppermute | solution.py:23
  176.0 1.2 collective-permute-start.49
  177.2 3.5 %collective-permute-done.49.refs_11_ = f32[8,768]{1,0:T(8,128)S(1)} collective-permute-done((f32[8,768]{1,0:T(8,128)S(1)}, f32[8,768]{1,0:T(8,128)S(1)}, u32[]{:S(2)}, u32[]{:S(2)}) %collective-permute-start.49) | collective-permute-done | bytes 24608 | tf_op jit(solution)/shard_map/ppermute | solution.py:23
  180.8 0.9 last.1
  (219 shorter events, 17.7 us)
Async XLA Ops:
  0.6 35.1 %copy-start.73 = (s32[512]{0:T(512)S(1)}, s32[512]{0:T(512)}, u32[]{:S(2)}) copy-start(s32[512]{0:T(512)} %param.24) | copy-start | bytes 6148
  6.2 10.8 %collective-permute-start.7 = (bf16[208,768]{1,0:T(8,128)(2,1)}, bf16[208,768]{1,0:T(8,128)(2,1)S(1)}, u32[]{:S(2)}, u32[]{:S(2)}) collective-permute-start(bf16[208,768]{1,0:T(8,128)(2,1)} %get-tuple-element.75.refs_0_.refs_4_), channel_id=1, source_target_pairs={{0,8},{4,12},{8,0},{12,4},{16,24},{20,28},{24,16},{28,20},{1,9},{5... | collective-permute-start | bytes 958472 | tf_op jit(solution)/shard_map/ppermute | solution.py:23
  9.1 21.2 %all-to-all-start = ((bf16[4,112,448]{2,1,0:T(8,128)(2,1)}), bf16[4,112,448]{2,1,0:T(8,128)(2,1)S(1)}, u32[]{:S(2)}, u32[]{:S(2)}) async-start(bf16[4,112,448]{2,1,0:T(8,128)(2,1)} %get-tuple-element.76), calls=%async_computation | async-start | bytes 917504 | tf_op jit(solution)/shard_map/all_to_all | solution.py:72
  14.0 15.8 %collective-permute-start.8 = (bf16[208,768]{1,0:T(8,128)(2,1)}, bf16[208,768]{1,0:T(8,128)(2,1)S(1)}, u32[]{:S(2)}, u32[]{:S(2)}) collective-permute-start(bf16[208,768]{1,0:T(8,128)(2,1)} %get-tuple-element.75.refs_0_.refs_4_), channel_id=1, source_target_pairs={{0,16},{4,20},{8,24},{12,28},{16,0},{20,4},{24,8},{28,12},{1,17},{... | collective-permute-start | bytes 958472 | tf_op jit(solution)/shard_map/ppermute | solution.py:23
  15.5 14.3 %collective-permute-start.9 = (bf16[208,768]{1,0:T(8,128)(2,1)}, bf16[208,768]{1,0:T(8,128)(2,1)S(1)}, u32[]{:S(2)}, u32[]{:S(2)}) collective-permute-start(bf16[208,768]{1,0:T(8,128)(2,1)} %get-tuple-element.75.refs_0_.refs_4_), channel_id=1, source_target_pairs={{0,24},{4,28},{8,16},{12,20},{16,8},{20,12},{24,0},{28,4},{1,25},{... | collective-permute-start | bytes 958472 | tf_op jit(solution)/shard_map/ppermute | solution.py:23
  16.0 16.6 %collective-permute-start.10 = (bf16[1,208,768]{2,1,0:T(8,128)(2,1)}, bf16[1,208,768]{2,1,0:T(8,128)(2,1)S(1)}, u32[]{:S(2)}, u32[]{:S(2)}) collective-permute-start(bf16[1,208,768]{2,1,0:T(8,128)(2,1)} %bitcast.64), channel_id=1, source_target_pairs={{0,4},{4,0},{8,12},{12,8},{16,20},{20,16},{24,28},{28,24},{1,5},{5... | collective-permute-start | bytes 958472 | tf_op jit(solution)/shard_map/ppermute | solution.py:23
  17.0 20.9 %copy-start.65 = (bf16[208,768]{1,0:T(8,128)(2,1)}, bf16[208,768]{1,0:T(8,128)(2,1)S(1)}, u32[]{:S(2)}) copy-start(bf16[208,768]{1,0:T(8,128)(2,1)S(1)} %collective-permute-done.7) | copy-start | bytes 958468
  17.0 17.1 %collective-permute-start.11 = (bf16[1,208,768]{2,1,0:T(8,128)(2,1)S(1)}, bf16[1,208,768]{2,1,0:T(8,128)(2,1)S(1)}, u32[]{:S(2)}, u32[]{:S(2)}) collective-permute-start(bf16[1,208,768]{2,1,0:T(8,128)(2,1)S(1)} %bitcast.106), channel_id=1, source_target_pairs={{0,4},{4,0},{8,12},{12,8},{16,20},{20,16},{24,28},{28,24},{1,5},{5... | collective-permute-start | bytes 958472 | tf_op jit(solution)/shard_map/ppermute | solution.py:23
  29.8 6.6 %collective-permute-start.12 = (bf16[1,208,768]{2,1,0:T(8,128)(2,1)S(1)}, bf16[1,208,768]{2,1,0:T(8,128)(2,1)S(1)}, u32[]{:S(2)}, u32[]{:S(2)}) collective-permute-start(bf16[1,208,768]{2,1,0:T(8,128)(2,1)S(1)} %bitcast.108), channel_id=1, source_target_pairs={{0,4},{4,0},{8,12},{12,8},{16,20},{20,16},{24,28},{28,24},{1,5},{5... | collective-permute-start | bytes 958472 | tf_op jit(solution)/shard_map/ppermute | solution.py:23
  29.8 6.6 %collective-permute-start.13 = (bf16[1,208,768]{2,1,0:T(8,128)(2,1)S(1)}, bf16[1,208,768]{2,1,0:T(8,128)(2,1)S(1)}, u32[]{:S(2)}, u32[]{:S(2)}) collective-permute-start(bf16[1,208,768]{2,1,0:T(8,128)(2,1)S(1)} %bitcast.110), channel_id=1, source_target_pairs={{0,4},{4,0},{8,12},{12,8},{16,20},{20,16},{24,28},{28,24},{1,5},{5... | collective-permute-start | bytes 958472 | tf_op jit(solution)/shard_map/ppermute | solution.py:23
  32.0 32.1 %copy-start.13 = (bf16[192,768]{1,0:T(8,128)(2,1)}, bf16[192,768]{1,0:T(8,128)(2,1)S(1)}, u32[]{:S(2)}) copy-start(bf16[192,768]{1,0:T(8,128)(2,1)S(1)} %get-tuple-element.77) | copy-start | bytes 884740
  32.0 12.0 %collective-permute-start = (bf16[192,768]{1,0:T(8,128)(2,1)S(1)}, bf16[192,768]{1,0:T(8,128)(2,1)S(1)}, u32[]{:S(2)}, u32[]{:S(2)}) collective-permute-start(bf16[192,768]{1,0:T(8,128)(2,1)S(1)} %get-tuple-element.77), channel_id=1, source_target_pairs={{0,8},{4,12},{8,0},{12,4},{16,24},{20,28},{24,16},{28,20},{1,9},{5... | collective-permute-start | bytes 884744 | tf_op jit(solution)/shard_map/ppermute | solution.py:23
  32.6 14.1 %collective-permute-start.1 = (bf16[192,768]{1,0:T(8,128)(2,1)S(1)}, bf16[192,768]{1,0:T(8,128)(2,1)S(1)}, u32[]{:S(2)}, u32[]{:S(2)}) collective-permute-start(bf16[192,768]{1,0:T(8,128)(2,1)S(1)} %get-tuple-element.77), channel_id=1, source_target_pairs={{0,16},{4,20},{8,24},{12,28},{16,0},{20,4},{24,8},{28,12},{1,17},{... | collective-permute-start | bytes 884744 | tf_op jit(solution)/shard_map/ppermute | solution.py:23
  34.1 14.2 %collective-permute-start.2 = (bf16[192,768]{1,0:T(8,128)(2,1)S(1)}, bf16[192,768]{1,0:T(8,128)(2,1)S(1)}, u32[]{:S(2)}, u32[]{:S(2)}) collective-permute-start(bf16[192,768]{1,0:T(8,128)(2,1)S(1)} %get-tuple-element.77), channel_id=1, source_target_pairs={{0,24},{4,28},{8,16},{12,20},{16,8},{20,12},{24,0},{28,4},{1,25},{... | collective-permute-start | bytes 884744 | tf_op jit(solution)/shard_map/ppermute | solution.py:23
  53.7 30.4 %all-to-all-start.1 = ((bf16[8,96,768]{2,1,0:T(8,128)(2,1)}), bf16[8,96,768]{2,1,0:T(8,128)(2,1)}, u32[]{:S(2)}, u32[]{:S(2)}) async-start(bf16[8,96,768]{2,1,0:T(8,128)(2,1)} %hold.1), calls=%async_computation.1 | async-start | bytes 2359296 | tf_op jit(solution)/shard_map/all_to_all | solution.py:853
  58.3 11.2 %copy-start.3 = (bf16[208,768]{1,0:T(8,128)(2,1)S(1)}, bf16[208,768]{1,0:T(8,128)(2,1)}, u32[]{:S(2)}) copy-start(bf16[208,768]{1,0:T(8,128)(2,1)} %get-tuple-element.75.refs_0_.refs_4_) | copy-start | bytes 958468
  58.4 11.2 %copy-start.57 = (f32[8,128]{1,0:T(8,128)S(1)}, f32[8,128]{1,0:T(8,128)}, u32[]{:S(2)}) copy-start(f32[8,128]{1,0:T(8,128)} %copy-done.56) | copy-start | bytes 12292
  58.4 11.2 %copy-start.60 = (f32[768,4]{0,1:T(4,128)S(1)}, f32[768,4]{0,1:T(4,128)}, u32[]{:S(2)}) copy-start(f32[768,4]{0,1:T(4,128)} %param.26) | copy-start | bytes 36868
  58.4 11.2 %copy-start.63 = (f32[768]{0:T(1024)S(1)}, f32[768]{0:T(1024)}, u32[]{:S(2)}) copy-start(f32[768]{0:T(1024)} %refs_3_.1) | copy-start | bytes 9220
  58.4 2.8 %collective-permute-start.3 = (bf16[1,192,768]{2,1,0:T(8,128)(2,1)S(1)}, bf16[1,192,768]{2,1,0:T(8,128)(2,1)S(1)}, u32[]{:S(2)}, u32[]{:S(2)}) collective-permute-start(bf16[1,192,768]{2,1,0:T(8,128)(2,1)S(1)} %bitcast.81), channel_id=1, source_target_pairs={{0,4},{4,0},{8,12},{12,8},{16,20},{20,16},{24,28},{28,24},{1,5},{5... | collective-permute-start | bytes 884744 | tf_op jit(solution)/shard_map/ppermute | solution.py:23
  58.6 5.0 %collective-permute-start.4 = (bf16[1,192,768]{2,1,0:T(8,128)(2,1)S(1)}, bf16[1,192,768]{2,1,0:T(8,128)(2,1)S(1)}, u32[]{:S(2)}, u32[]{:S(2)}) collective-permute-start(bf16[1,192,768]{2,1,0:T(8,128)(2,1)S(1)} %bitcast.68), channel_id=1, source_target_pairs={{0,4},{4,0},{8,12},{12,8},{16,20},{20,16},{24,28},{28,24},{1,5},{5... | collective-permute-start | bytes 884744 | tf_op jit(solution)/shard_map/ppermute | solution.py:23
  59.0 5.2 %collective-permute-start.5 = (bf16[1,192,768]{2,1,0:T(8,128)(2,1)S(1)}, bf16[1,192,768]{2,1,0:T(8,128)(2,1)S(1)}, u32[]{:S(2)}, u32[]{:S(2)}) collective-permute-start(bf16[1,192,768]{2,1,0:T(8,128)(2,1)S(1)} %bitcast.73), channel_id=1, source_target_pairs={{0,4},{4,0},{8,12},{12,8},{16,20},{20,16},{24,28},{28,24},{1,5},{5... | collective-permute-start | bytes 884744 | tf_op jit(solution)/shard_map/ppermute | solution.py:23
  59.1 5.0 %collective-permute-start.6 = (bf16[1,192,768]{2,1,0:T(8,128)(2,1)S(1)}, bf16[1,192,768]{2,1,0:T(8,128)(2,1)S(1)}, u32[]{:S(2)}, u32[]{:S(2)}) collective-permute-start(bf16[1,192,768]{2,1,0:T(8,128)(2,1)S(1)} %bitcast.78), channel_id=1, source_target_pairs={{0,4},{4,0},{8,12},{12,8},{16,20},{20,16},{24,28},{28,24},{1,5},{5... | collective-permute-start | bytes 884744 | tf_op jit(solution)/shard_map/ppermute | solution.py:23
  59.5 4.8 %collective-permute-start.14 = (bf16[192,128]{1,0:T(8,128)(2,1)S(1)}, bf16[192,128]{1,0:T(8,128)(2,1)S(1)}, u32[]{:S(2)}, u32[]{:S(2)}) collective-permute-start(bf16[192,128]{1,0:T(8,128)(2,1)S(1)} %copy-done.48), channel_id=1, source_target_pairs={{0,1},{1,0},{2,3},{3,2},{4,5},{5,4},{6,7},{7,6},{8,9},{9,8},{10,11... | collective-permute-start | bytes 147464 | tf_op jit(solution)/shard_map/ppermute | solution.py:23
  61.2 5.8 %collective-permute-start.15 = (bf16[192,128]{1,0:T(8,128)(2,1)S(1)}, bf16[192,128]{1,0:T(8,128)(2,1)S(1)}, u32[]{:S(2)}, u32[]{:S(2)}) collective-permute-start(bf16[192,128]{1,0:T(8,128)(2,1)S(1)} %copy-done.48), channel_id=1, source_target_pairs={{0,2},{1,3},{2,0},{3,1},{4,6},{5,7},{6,4},{7,5},{8,10},{9,11},{10,... | collective-permute-start | bytes 147464 | tf_op jit(solution)/shard_map/ppermute | solution.py:23
  63.6 5.9 %collective-permute-start.16 = (bf16[192,128]{1,0:T(8,128)(2,1)S(1)}, bf16[192,128]{1,0:T(8,128)(2,1)S(1)}, u32[]{:S(2)}, u32[]{:S(2)}) collective-permute-start(bf16[192,128]{1,0:T(8,128)(2,1)S(1)} %copy-done.48), channel_id=1, source_target_pairs={{0,3},{1,2},{2,1},{3,0},{4,7},{5,6},{6,5},{7,4},{8,11},{9,10},{10,... | collective-permute-start | bytes 147464 | tf_op jit(solution)/shard_map/ppermute | solution.py:23
  64.3 19.6 %copy-start.50 = (bf16[768,192]{1,0:T(8,128)(2,1)}, bf16[768,192]{1,0:T(8,128)(2,1)S(1)}, u32[]{:S(2)}) copy-start(bf16[768,192]{1,0:T(8,128)(2,1)S(1)} %get-tuple-element.97.refs_6_) | copy-start | bytes 884740
  72.0 12.1 %copy-start.25 = (bf16[96,896]{1,0:T(8,128)(2,1)}, bf16[96,896]{1,0:T(8,128)(2,1)S(1)}, u32[]{:S(2)}) copy-start(bf16[96,896]{1,0:T(8,128)(2,1)S(1)} %get-tuple-element.85) | copy-start | bytes 516100
  72.0 7.3 %collective-permute-start.17 = (bf16[96,896]{1,0:T(8,128)(2,1)S(1)}, bf16[96,896]{1,0:T(8,128)(2,1)S(1)}, u32[]{:S(2)}, u32[]{:S(2)}) collective-permute-start(bf16[96,896]{1,0:T(8,128)(2,1)S(1)} %get-tuple-element.85), channel_id=1, source_target_pairs={{0,8},{4,12},{8,0},{12,4},{16,24},{20,28},{24,16},{28,20},{1,9},{5... | collective-permute-start | bytes 516104 | tf_op jit(solution)/shard_map/ppermute | solution.py:23
  73.7 8.8 %collective-permute-start.18 = (bf16[96,896]{1,0:T(8,128)(2,1)S(1)}, bf16[96,896]{1,0:T(8,128)(2,1)S(1)}, u32[]{:S(2)}, u32[]{:S(2)}) collective-permute-start(bf16[96,896]{1,0:T(8,128)(2,1)S(1)} %get-tuple-element.85), channel_id=1, source_target_pairs={{0,16},{4,20},{8,24},{12,28},{16,0},{20,4},{24,8},{28,12},{1,17},{... | collective-permute-start | bytes 516104 | tf_op jit(solution)/shard_map/ppermute | solution.py:23
  75.2 7.3 %collective-permute-start.19 = (bf16[96,896]{1,0:T(8,128)(2,1)S(1)}, bf16[96,896]{1,0:T(8,128)(2,1)S(1)}, u32[]{:S(2)}, u32[]{:S(2)}) collective-permute-start(bf16[96,896]{1,0:T(8,128)(2,1)S(1)} %get-tuple-element.85), channel_id=1, source_target_pairs={{0,24},{4,28},{8,16},{12,20},{16,8},{20,12},{24,0},{28,4},{1,25},{... | collective-permute-start | bytes 516104 | tf_op jit(solution)/shard_map/ppermute | solution.py:23
  75.5 7.5 %collective-permute-start.20 = (bf16[1,96,896]{2,1,0:T(8,128)(2,1)S(1)}, bf16[1,96,896]{2,1,0:T(8,128)(2,1)S(1)}, u32[]{:S(2)}, u32[]{:S(2)}) collective-permute-start(bf16[1,96,896]{2,1,0:T(8,128)(2,1)S(1)} %bitcast.85), channel_id=1, source_target_pairs={{0,4},{4,0},{8,12},{12,8},{16,20},{20,16},{24,28},{28,24},{1,5},{5... | collective-permute-start | bytes 516104 | tf_op jit(solution)/shard_map/ppermute | solution.py:23
  79.3 3.7 %collective-permute-start.21 = (bf16[1,96,896]{2,1,0:T(8,128)(2,1)S(1)}, bf16[1,96,896]{2,1,0:T(8,128)(2,1)S(1)}, u32[]{:S(2)}, u32[]{:S(2)}) collective-permute-start(bf16[1,96,896]{2,1,0:T(8,128)(2,1)S(1)} %bitcast.89), channel_id=1, source_target_pairs={{0,4},{4,0},{8,12},{12,8},{16,20},{20,16},{24,28},{28,24},{1,5},{5... | collective-permute-start | bytes 516104 | tf_op jit(solution)/shard_map/ppermute | solution.py:23
  82.5 1.4 collective-permute-start.22
  82.5 1.6 collective-permute-start.23
  93.0 3.1 %collective-permute-start.24 = (bf16[4,96,1536]{2,1,0:T(8,128)(2,1)}, bf16[4,96,1536]{2,1,0:T(8,128)(2,1)S(1)}, u32[]{:S(2)}, u32[]{:S(2)}) collective-permute-start(bf16[4,96,1536]{2,1,0:T(8,128)(2,1)} %bitcast.120), channel_id=1, source_target_pairs={{0,4},{4,0},{8,12},{12,8},{16,20},{20,16},{24,28},{28,24},{1,5},{5... | collective-permute-start | bytes 3538952 | tf_op jit(solution)/shard_map/ppermute | solution.py:23
  97.9 9.9 %collective-permute-start.25 = (bf16[96,1536]{1,0:T(8,128)(2,1)S(1)}, bf16[96,1536]{1,0:T(8,128)(2,1)S(1)}, u32[]{:S(2)}, u32[]{:S(2)}) collective-permute-start(bf16[96,1536]{1,0:T(8,128)(2,1)S(1)} %get-tuple-element.139), channel_id=1, source_target_pairs={{0,8},{4,12},{8,0},{12,4},{16,24},{20,28},{24,16},{28,20},{1,9},{5... | collective-permute-start | bytes 884744 | tf_op jit(solution)/shard_map/ppermute | solution.py:23
  98.4 9.4 %collective-permute-start.26 = (bf16[96,1536]{1,0:T(8,128)(2,1)S(1)}, bf16[96,1536]{1,0:T(8,128)(2,1)S(1)}, u32[]{:S(2)}, u32[]{:S(2)}) collective-permute-start(bf16[96,1536]{1,0:T(8,128)(2,1)S(1)} %get-tuple-element.138), channel_id=1, source_target_pairs={{0,16},{4,20},{8,24},{12,28},{16,0},{20,4},{24,8},{28,12},{1,17},{... | collective-permute-start | bytes 884744 | tf_op jit(solution)/shard_map/ppermute | solution.py:23
  99.5 14.6 %collective-permute-start.27 = (bf16[96,1536]{1,0:T(8,128)(2,1)S(1)}, bf16[96,1536]{1,0:T(8,128)(2,1)S(1)}, u32[]{:S(2)}, u32[]{:S(2)}) collective-permute-start(bf16[96,1536]{1,0:T(8,128)(2,1)S(1)} %get-tuple-element.137), channel_id=1, source_target_pairs={{0,24},{4,28},{8,16},{12,20},{16,8},{20,12},{24,0},{28,4},{1,25},{... | collective-permute-start | bytes 884744 | tf_op jit(solution)/shard_map/ppermute | solution.py:23
  115.1 22.4 %all-to-all-start.2 = ((bf16[4,120,768]{2,1,0:T(8,128)(2,1)}), bf16[4,120,768]{2,1,0:T(8,128)(2,1)S(1)}, u32[]{:S(2)}, u32[]{:S(2)}) async-start(bf16[4,120,768]{2,1,0:T(8,128)(2,1)} %get-tuple-element.94), calls=%async_computation.2 | async-start | bytes 1474560 | tf_op jit(solution)/shard_map/all_to_all | solution.py:72
  119.1 3.5 %collective-permute-start.28 = (bf16[96,768]{1,0:T(8,128)(2,1)S(1)}, bf16[96,768]{1,0:T(8,128)(2,1)S(1)}, u32[]{:S(2)}, u32[]{:S(2)}) collective-permute-start(bf16[96,768]{1,0:T(8,128)(2,1)S(1)} %get-tuple-element.100), channel_id=1, source_target_pairs={{0,4},{4,0},{8,12},{12,8},{16,20},{20,16},{24,28},{28,24},{1,5},{5... | collective-permute-start | bytes 442376 | tf_op jit(solution)/shard_map/ppermute | solution.py:23
  119.1 6.6 %collective-permute-start.29 = (bf16[96,768]{1,0:T(8,128)(2,1)S(1)}, bf16[96,768]{1,0:T(8,128)(2,1)S(1)}, u32[]{:S(2)}, u32[]{:S(2)}) collective-permute-start(bf16[96,768]{1,0:T(8,128)(2,1)S(1)} %get-tuple-element.101), channel_id=1, source_target_pairs={{0,8},{4,12},{8,0},{12,4},{16,24},{20,28},{24,16},{28,20},{1,9},{5... | collective-permute-start | bytes 442376 | tf_op jit(solution)/shard_map/ppermute | solution.py:23
  120.5 7.6 %collective-permute-start.30 = (bf16[96,768]{1,0:T(8,128)(2,1)S(1)}, bf16[96,768]{1,0:T(8,128)(2,1)S(1)}, u32[]{:S(2)}, u32[]{:S(2)}) collective-permute-start(bf16[96,768]{1,0:T(8,128)(2,1)S(1)} %get-tuple-element.102), channel_id=1, source_target_pairs={{0,12},{4,8},{8,4},{12,0},{16,28},{20,24},{24,20},{28,16},{1,13},{... | collective-permute-start | bytes 442376 | tf_op jit(solution)/shard_map/ppermute | solution.py:23
  120.9 7.2 %collective-permute-start.31 = (bf16[96,768]{1,0:T(8,128)(2,1)S(1)}, bf16[96,768]{1,0:T(8,128)(2,1)S(1)}, u32[]{:S(2)}, u32[]{:S(2)}) collective-permute-start(bf16[96,768]{1,0:T(8,128)(2,1)S(1)} %get-tuple-element.103), channel_id=1, source_target_pairs={{0,16},{4,20},{8,24},{12,28},{16,0},{20,4},{24,8},{28,12},{1,17},{... | collective-permute-start | bytes 442376 | tf_op jit(solution)/shard_map/ppermute | solution.py:23
  122.1 13.7 %collective-permute-start.32 = (bf16[96,768]{1,0:T(8,128)(2,1)S(1)}, bf16[96,768]{1,0:T(8,128)(2,1)S(1)}, u32[]{:S(2)}, u32[]{:S(2)}) collective-permute-start(bf16[96,768]{1,0:T(8,128)(2,1)S(1)} %get-tuple-element.104), channel_id=1, source_target_pairs={{0,20},{4,16},{8,28},{12,24},{16,4},{20,0},{24,12},{28,8},{1,21},{... | collective-permute-start | bytes 442376 | tf_op jit(solution)/shard_map/ppermute | solution.py:23
  122.6 13.2 %collective-permute-start.33 = (bf16[96,768]{1,0:T(8,128)(2,1)S(1)}, bf16[96,768]{1,0:T(8,128)(2,1)S(1)}, u32[]{:S(2)}, u32[]{:S(2)}) collective-permute-start(bf16[96,768]{1,0:T(8,128)(2,1)S(1)} %get-tuple-element.105), channel_id=1, source_target_pairs={{0,24},{4,28},{8,16},{12,20},{16,8},{20,12},{24,0},{28,4},{1,25},{... | collective-permute-start | bytes 442376 | tf_op jit(solution)/shard_map/ppermute | solution.py:23
  125.7 10.1 %collective-permute-start.34 = (bf16[96,768]{1,0:T(8,128)(2,1)S(1)}, bf16[96,768]{1,0:T(8,128)(2,1)S(1)}, u32[]{:S(2)}, u32[]{:S(2)}) collective-permute-start(bf16[96,768]{1,0:T(8,128)(2,1)S(1)} %get-tuple-element.106), channel_id=1, source_target_pairs={{0,28},{4,24},{8,20},{12,16},{16,12},{20,8},{24,4},{28,0},{1,29},{... | collective-permute-start | bytes 442376 | tf_op jit(solution)/shard_map/ppermute | solution.py:23
  144.5 2.2 %collective-permute-start.35 = (bf16[4,128,384]{2,1,0:T(8,128)(2,1)}, bf16[4,128,384]{2,1,0:T(8,128)(2,1)S(1)}, u32[]{:S(2)}, u32[]{:S(2)}) collective-permute-start(bf16[4,128,384]{2,1,0:T(8,128)(2,1)} %get-tuple-element.109), channel_id=1, source_target_pairs={{0,4},{4,0},{8,12},{12,8},{16,20},{20,16},{24,28},{28,24},{1,5},{5... | collective-permute-start | bytes 1179656 | tf_op jit(solution)/shard_map/ppermute | solution.py:23
  148.0 6.2 %collective-permute-start.36 = (bf16[128,384]{1,0:T(8,128)(2,1)S(1)}, bf16[128,384]{1,0:T(8,128)(2,1)S(1)}, u32[]{:S(2)}, u32[]{:S(2)}) collective-permute-start(bf16[128,384]{1,0:T(8,128)(2,1)S(1)} %get-tuple-element.147), channel_id=1, source_target_pairs={{0,8},{4,12},{8,0},{12,4},{16,24},{20,28},{24,16},{28,20},{1,9},{5... | collective-permute-start | bytes 294920 | tf_op jit(solution)/shard_map/ppermute | solution.py:23
  149.5 6.9 %collective-permute-start.37 = (bf16[128,384]{1,0:T(8,128)(2,1)S(1)}, bf16[128,384]{1,0:T(8,128)(2,1)S(1)}, u32[]{:S(2)}, u32[]{:S(2)}) collective-permute-start(bf16[128,384]{1,0:T(8,128)(2,1)S(1)} %get-tuple-element.146), channel_id=1, source_target_pairs={{0,16},{4,20},{8,24},{12,28},{16,0},{20,4},{24,8},{28,12},{1,17},{... | collective-permute-start | bytes 294920 | tf_op jit(solution)/shard_map/ppermute | solution.py:23
  150.3 6.1 %collective-permute-start.38 = (bf16[128,384]{1,0:T(8,128)(2,1)S(1)}, bf16[128,384]{1,0:T(8,128)(2,1)S(1)}, u32[]{:S(2)}, u32[]{:S(2)}) collective-permute-start(bf16[128,384]{1,0:T(8,128)(2,1)S(1)} %get-tuple-element.145), channel_id=1, source_target_pairs={{0,24},{4,28},{8,16},{12,20},{16,8},{20,12},{24,0},{28,4},{1,25},{... | collective-permute-start | bytes 294920 | tf_op jit(solution)/shard_map/ppermute | solution.py:23
  157.6 9.3 %collective-permute-start.39 = (bf16[4,96,768]{2,1,0:T(8,128)(2,1)S(1)}, bf16[4,96,768]{2,1,0:T(8,128)(2,1)S(1)}, u32[]{:S(2)}, u32[]{:S(2)}) collective-permute-start(bf16[4,96,768]{2,1,0:T(8,128)(2,1)S(1)} %get-tuple-element.123), channel_id=1, source_target_pairs={{0,4},{4,0},{8,12},{12,8},{16,20},{20,16},{24,28},{28,24},{1,5},{5... | collective-permute-start | bytes 1769480 | tf_op jit(solution)/shard_map/ppermute | solution.py:23
  157.6 11.3 %collective-permute-start.45 = (f32[8,768]{1,0:T(8,128)S(1)}, f32[8,768]{1,0:T(8,128)S(1)}, u32[]{:S(2)}, u32[]{:S(2)}) collective-permute-start(f32[8,768]{1,0:T(8,128)S(1)} %get-tuple-element.124), channel_id=1, source_target_pairs={{0,3},{1,2},{2,1},{3,0},{4,7},{5,6},{6,5},{7,4},{8,11},{9,10},{10,... | collective-permute-start | bytes 73736 | tf_op jit(solution)/shard_map/ppermute | solution.py:23
  161.2 9.5 %collective-permute-start.44 = (f32[8,768]{1,0:T(8,128)S(1)}, f32[8,768]{1,0:T(8,128)S(1)}, u32[]{:S(2)}, u32[]{:S(2)}) collective-permute-start(f32[8,768]{1,0:T(8,128)S(1)} %get-tuple-element.124), channel_id=1, source_target_pairs={{0,2},{1,3},{2,0},{3,1},{4,6},{5,7},{6,4},{7,5},{8,10},{9,11},{10,... | collective-permute-start | bytes 73736 | tf_op jit(solution)/shard_map/ppermute | solution.py:23
  161.2 9.5 %collective-permute-start.43 = (f32[8,768]{1,0:T(8,128)S(1)}, f32[8,768]{1,0:T(8,128)S(1)}, u32[]{:S(2)}, u32[]{:S(2)}) collective-permute-start(f32[8,768]{1,0:T(8,128)S(1)} %get-tuple-element.124), channel_id=1, source_target_pairs={{0,1},{1,0},{2,3},{3,2},{4,5},{5,4},{6,7},{7,6},{8,9},{9,8},{10,11... | collective-permute-start | bytes 73736 | tf_op jit(solution)/shard_map/ppermute | solution.py:23
  162.0 18.7 %copy-start.55 = (f32[32,768]{1,0:T(8,128)S(1)}, f32[32,768]{1,0:T(8,128)}, u32[]{:S(2)}) copy-start(f32[32,768]{1,0:T(8,128)} %get-tuple-element.111.refs_2_) | copy-start | bytes 294916
  162.0 18.7 %all-to-all-start.3 = ((bf16[4,32,768]{2,1,0:T(8,128)(2,1)}), bf16[4,32,768]{2,1,0:T(8,128)(2,1)S(1)}, u32[]{:S(2)}, u32[]{:S(2)}) async-start(bf16[4,32,768]{2,1,0:T(8,128)(2,1)} %get-tuple-element.121), calls=%async_computation.3 | async-start | bytes 393216 | tf_op jit(solution)/shard_map/all_to_all | solution.py:72
  167.1 13.6 %collective-permute-start.40 = (bf16[96,768]{1,0:T(8,128)(2,1)S(1)}, bf16[96,768]{1,0:T(8,128)(2,1)S(1)}, u32[]{:S(2)}, u32[]{:S(2)}) collective-permute-start(bf16[96,768]{1,0:T(8,128)(2,1)S(1)} %get-tuple-element.143), channel_id=1, source_target_pairs={{0,8},{4,12},{8,0},{12,4},{16,24},{20,28},{24,16},{28,20},{1,9},{5... | collective-permute-start | bytes 442376 | tf_op jit(solution)/shard_map/ppermute | solution.py:23
  167.7 13.0 %collective-permute-start.41 = (bf16[96,768]{1,0:T(8,128)(2,1)S(1)}, bf16[96,768]{1,0:T(8,128)(2,1)S(1)}, u32[]{:S(2)}, u32[]{:S(2)}) collective-permute-start(bf16[96,768]{1,0:T(8,128)(2,1)S(1)} %get-tuple-element.142), channel_id=1, source_target_pairs={{0,16},{4,20},{8,24},{12,28},{16,0},{20,4},{24,8},{28,12},{1,17},{... | collective-permute-start | bytes 442376 | tf_op jit(solution)/shard_map/ppermute | solution.py:23
  168.9 11.8 %collective-permute-start.42 = (bf16[96,768]{1,0:T(8,128)(2,1)S(1)}, bf16[96,768]{1,0:T(8,128)(2,1)S(1)}, u32[]{:S(2)}, u32[]{:S(2)}) collective-permute-start(bf16[96,768]{1,0:T(8,128)(2,1)S(1)} %get-tuple-element.141), channel_id=1, source_target_pairs={{0,24},{4,28},{8,16},{12,20},{16,8},{20,12},{24,0},{28,4},{1,25},{... | collective-permute-start | bytes 442376 | tf_op jit(solution)/shard_map/ppermute | solution.py:23
  170.7 1.3 collective-permute-start.46
  172.0 4.0 %collective-permute-start.47 = (f32[8,768]{1,0:T(8,128)S(1)}, f32[8,768]{1,0:T(8,128)S(1)}, u32[]{:S(2)}, u32[]{:S(2)}) collective-permute-start(f32[8,768]{1,0:T(8,128)S(1)} %add.71.refs_8_), channel_id=1, source_target_pairs={{0,8},{4,12},{8,0},{12,4},{16,24},{20,28},{24,16},{28,20},{1,9},{5... | collective-permute-start | bytes 73736 | tf_op jit(solution)/shard_map/ppermute | solution.py:23
  172.5 4.7 %collective-permute-start.48 = (f32[8,768]{1,0:T(8,128)S(1)}, f32[8,768]{1,0:T(8,128)S(1)}, u32[]{:S(2)}, u32[]{:S(2)}) collective-permute-start(f32[8,768]{1,0:T(8,128)S(1)} %add.71.refs_8_), channel_id=1, source_target_pairs={{0,16},{4,20},{8,24},{12,28},{16,0},{20,4},{24,8},{28,12},{1,17},{... | collective-permute-start | bytes 73736 | tf_op jit(solution)/shard_map/ppermute | solution.py:23
  176.0 4.7 %collective-permute-start.49 = (f32[8,768]{1,0:T(8,128)S(1)}, f32[8,768]{1,0:T(8,128)S(1)}, u32[]{:S(2)}, u32[]{:S(2)}) collective-permute-start(f32[8,768]{1,0:T(8,128)S(1)} %add.71.refs_8_), channel_id=1, source_target_pairs={{0,24},{4,28},{8,16},{12,20},{16,8},{20,12},{24,0},{28,4},{1,25},{... | collective-permute-start | bytes 73736 | tf_op jit(solution)/shard_map/ppermute | solution.py:23
  (64 other events, 240.9 us)
